TPU v7x, 32 devices: a whole 2x2x4 slice. The times are simulated.
32 devices in a mesh: dp: 4 (over y, x), fsdp: 8 (over z, core).
Axes of the slice: x: 2, y: 2, z: 4, core: 2. Of those that a mesh axis runs over, the one named last changes fastest.
Arguments:
- tokens: bfloat16 [16384, 1152], P(('dp', 'fsdp')), may hold values from -6 to 6
- condition: bfloat16 [128, 1152], P(('dp', 'fsdp')), may hold values from -6 to 6
- kept_index: int32 [16384], P(('dp', 'fsdp')), may hold values from 0 to 1023, as said below
- segment: int32 [16384], P(('dp', 'fsdp')), may hold values from 0 to 3, as said below
- grid_side: int32 [128], P(('dp', 'fsdp')), may hold values from 16 to 32, as said below
- ada_weight: bfloat16 [1152, 6912], P('fsdp', 'dp'), may hold values from -0.1875 to 0.1875
- ada_bias: bfloat16 [6912], P(('dp', 'fsdp')), may hold values from -3 to 3
- attn_weight: bfloat16 [1152, 3456], P('fsdp', 'dp'), may hold values from -0.1875 to 0.1875
- attn_bias: bfloat16 [2304], P(('dp', 'fsdp')), may hold values from -1 to 1
- proj_weight: bfloat16 [1152, 1152], P('fsdp', 'dp'), may hold values from -2 to 2
- out_bias: bfloat16 [2304], P(('dp', 'fsdp')), may hold values from -3 to 3
- up_weight: bfloat16 [1152, 4608], P('fsdp', 'dp'), may hold values from -0.1875 to 0.1875
- up_bias: bfloat16 [4608], P(('dp', 'fsdp')), may hold values from -3 to 3
- down_weight: bfloat16 [4608, 1152], P('fsdp', 'dp'), may hold values from -0.09375 to 0.09375
- grad_out: bfloat16 [16384, 1152], P(('dp', 'fsdp')), may hold values from -6 to 6
Outputs:
- mixed: bfloat16 [16384, 1152], P(('dp', 'fsdp'))
- tokens_grad: float32 [16384, 1152], P(('dp', 'fsdp'))
- condition_grad: float32 [128, 1152], P(('dp', 'fsdp'))
- ada_weight_grad: float32 [1152, 6912], P('fsdp', 'dp')
- ada_bias_grad: float32 [6912], P(('dp', 'fsdp'))
- attn_weight_grad: float32 [1152, 3456], P('fsdp', 'dp')
- attn_bias_grad: float32 [2304], P(('dp', 'fsdp'))
- proj_weight_grad: float32 [1152, 1152], P('fsdp', 'dp')
- out_bias_grad: float32 [2304], P(('dp', 'fsdp'))
- up_weight_grad: float32 [1152, 4608], P('fsdp', 'dp')
- up_bias_grad: float32 [4608], P(('dp', 'fsdp'))
- down_weight_grad: float32 [4608, 1152], P('fsdp', 'dp')
Inputs may be any that keep to these rules, and one draw needn't show every extreme that they name: `segment`: each device's 512 rows hold whole images in rising slot order: a 512px image is 512 rows of one slot, a 256px image 128 rows of one slot; 512px images come first on a device. Slots without rows may exist on a device. `grid_side`: A slot that holds a 512px image has 32, one that holds a 256px image has 16; a slot without rows has either. `kept_index`: within one image the kept patch numbers are distinct, rise, and lie below the square of its slot's grid_side; every 512px image keeps its last patch.
All inputs are finite; a program needn't handle non-finite values.
Results may differ from a plain program's by a relative error of at most 0.015.
The roundings to bfloat16 on the way count: a program that leaves them out, or rounds other values in their place, can miss the bound.
Values may be sent and summed in bfloat16 or wider, within the bound.
A program may use at most 384 MiB of HBM per device.

v0:
```python
from functools import partial
import math

import jax
import jax.numpy as jnp
from jax import lax
from jax.sharding import PartitionSpec as P

HEADS = 16


def position_code(kept_index, side_rows, model_width):
    quarter = model_width // 4
    exponent = jnp.arange(quarter, dtype=jnp.float32) / quarter
    frequency = 1.0 / 10000.0**exponent
    column = (kept_index % side_rows).astype(jnp.float32)[:, None] * frequency[None, :]
    line_pos = (kept_index // side_rows).astype(jnp.float32)[:, None] * frequency[None, :]
    return jnp.concatenate(
        [jnp.sin(column), jnp.cos(column), jnp.sin(line_pos), jnp.cos(line_pos)], axis=1
    )


def layer_norm(values):
    center = values - jnp.mean(values, axis=-1, keepdims=True)
    return center * lax.rsqrt(jnp.mean(center * center, axis=-1, keepdims=True) + 1e-06)


def norm_modulate(values, shift_rows, scale_rows):
    return layer_norm(values) * (1.0 + scale_rows) + shift_rows


def matmul_nt(first_matrix, second_matrix):
    return lax.dot_general(
        first_matrix, second_matrix, (((1,), (1,)), ((), ())), preferred_element_type=jnp.float32
    )


def matmul_tn(first_matrix, second_matrix):
    return lax.dot_general(
        first_matrix, second_matrix, (((0,), (0,)), ((), ())), preferred_element_type=jnp.float32
    )


def attend_forward(query_bf, key_bf, value_bf, segment, head_count):
    row_count, model_width = query_bf.shape
    head_size = model_width // head_count
    block_rows = min(row_count, 512)
    block_count = row_count // block_rows
    score_scale = 1.0 / math.sqrt(head_size)
    key_heads = key_bf.reshape(row_count, head_count, head_size)
    value_heads = value_bf.reshape(row_count, head_count, head_size)

    def forward_block(block_index):
        query_rows = query_bf.reshape(block_rows, head_count, head_size)
        same_image = segment[:, None] == segment[None, :]
        scores = (
            jnp.einsum("qhd,khd->hqk", query_rows, key_heads, preferred_element_type=jnp.float32)
            * score_scale
        )
        scores = jnp.where(same_image[None], scores, -1e30)
        highest = jnp.max(scores, axis=2, keepdims=True)
        powers = jnp.exp(scores - highest)
        totals = jnp.sum(powers, axis=2, keepdims=True)
        probs_bf = (powers / totals).astype(jnp.bfloat16)
        attended = jnp.einsum(
            "hqk,khd->qhd", probs_bf, value_heads, preferred_element_type=jnp.float32
        )
        return (attended.reshape(block_rows, model_width), (highest + jnp.log(totals))[:, :, 0])

    attended, log_totals = lax.map(forward_block, jnp.arange(block_count, dtype=jnp.int32))
    return (attended.reshape(row_count, model_width), log_totals)


def attend_backward(query_bf, key_bf, value_bf, attended_grad, segment, log_totals, head_count):
    row_count, model_width = query_bf.shape
    head_size = model_width // head_count
    block_rows = min(row_count, 512)
    block_count = row_count // block_rows
    score_scale = 1.0 / math.sqrt(head_size)
    key_heads = key_bf.reshape(row_count, head_count, head_size)
    value_heads = value_bf.reshape(row_count, head_count, head_size)

    def backward_block(running, pieces):
        key_sum, value_sum = running
        block_index, log_rows = pieces
        query_rows = query_bf.reshape(block_rows, head_count, head_size)
        grad_rows = attended_grad.reshape(block_rows, head_count, head_size)
        same_image = segment[:, None] == segment[None, :]
        scores = (
            jnp.einsum("qhd,khd->hqk", query_rows, key_heads, preferred_element_type=jnp.float32)
            * score_scale
        )
        scores = jnp.where(same_image[None], scores, -1e30)
        probs = jnp.exp(scores - log_rows[:, :, None])
        probs_bf = probs.astype(jnp.bfloat16)
        prob_grad = jnp.einsum(
            "qhd,khd->hqk", grad_rows, value_heads, preferred_element_type=jnp.float32
        )
        row_inner = jnp.sum(probs * prob_grad, axis=2, keepdims=True)
        score_grad = (probs * (prob_grad - row_inner)).astype(jnp.bfloat16)
        query_grad = (
            jnp.einsum("hqk,khd->qhd", score_grad, key_heads, preferred_element_type=jnp.float32)
            * score_scale
        )
        key_sum = (
            key_sum
            + jnp.einsum("hqk,qhd->khd", score_grad, query_rows, preferred_element_type=jnp.float32)
            * score_scale
        )
        value_sum = value_sum + jnp.einsum(
            "hqk,qhd->khd", probs_bf, grad_rows, preferred_element_type=jnp.float32
        )
        return ((key_sum, value_sum), query_grad.reshape(block_rows, model_width))

    empty_sum = jnp.zeros((row_count, head_count, head_size), jnp.float32)
    sums, query_grad = lax.scan(
        backward_block,
        (empty_sum, empty_sum),
        (jnp.arange(block_count, dtype=jnp.int32), log_totals),
    )
    return (
        query_grad.reshape(row_count, model_width),
        sums[0].reshape(row_count, model_width),
        sums[1].reshape(row_count, model_width),
    )


def per_device(
    tokens,
    condition,
    kept_index,
    segment,
    grid_side,
    ada_weight,
    ada_bias,
    attn_weight,
    attn_bias,
    proj_weight,
    out_bias,
    up_weight,
    up_bias,
    down_weight,
    grad_out,
):
    model_width = tokens.shape[1]
    slot_count = condition.shape[0]
    row_parts = lax.axis_size("dp")
    column_parts = lax.axis_size("fsdp")

    def gather_order(vector):
        return vector.reshape(column_parts, row_parts, -1).transpose(1, 0, 2).reshape(-1)

    gathered = (
        lax.all_gather(ada_weight, "dp", axis=1, tiled=True),
        lax.all_gather(attn_weight, "dp", axis=1, tiled=True),
        lax.all_gather(proj_weight, "dp", axis=1, tiled=True),
        lax.all_gather(up_weight, "dp", axis=1, tiled=True),
        lax.all_gather(down_weight, "dp", axis=1, tiled=True),
        lax.all_gather(ada_bias, "dp", axis=0, tiled=True),
        lax.all_gather(attn_bias, "dp", axis=0, tiled=True),
        lax.all_gather(out_bias, "dp", axis=0, tiled=True),
        lax.all_gather(up_bias, "dp", axis=0, tiled=True),
    )
    (
        ada_full,
        attn_full,
        proj_full,
        up_full,
        down_full,
        ada_bfull,
        attn_bfull,
        out_bfull,
        up_bfull,
    ) = (
        lax.all_gather(gathered[0], "fsdp", axis=0, tiled=True),
        lax.all_gather(gathered[1], "fsdp", axis=0, tiled=True),
        lax.all_gather(gathered[2], "fsdp", axis=0, tiled=True),
        lax.all_gather(gathered[3], "fsdp", axis=0, tiled=True),
        lax.all_gather(gathered[4], "fsdp", axis=0, tiled=True),
        lax.all_gather(gathered[5], "fsdp", axis=0, tiled=True),
        lax.all_gather(gathered[6], "fsdp", axis=0, tiled=True),
        lax.all_gather(gathered[7], "fsdp", axis=0, tiled=True),
        lax.all_gather(gathered[8], "fsdp", axis=0, tiled=True),
    )
    ada_bfull = gather_order(ada_bfull)
    attn_bfull = gather_order(attn_bfull)
    out_bfull = gather_order(out_bfull)
    up_bfull = gather_order(up_bfull)
    slot_ids = jnp.arange(slot_count, dtype=jnp.int32)
    same_slot = segment[:, None] == slot_ids[None, :]
    slot_table = same_slot.astype(jnp.float32)
    side_rows = jnp.sum(jnp.where(same_slot, grid_side[None, :], 0), axis=1)
    start = tokens.astype(jnp.float32) + position_code(kept_index, side_rows, model_width)
    condition_f = condition.astype(jnp.float32)
    silu_cond, silu_back = jax.vjp(jax.nn.silu, condition_f)
    silu_bf = silu_cond.astype(jnp.bfloat16)
    modulation = jnp.dot(silu_bf, ada_full, preferred_element_type=jnp.float32) + ada_bfull.astype(
        jnp.float32
    )
    mod_rows = jnp.dot(
        slot_table, modulation, precision=lax.Precision.HIGHEST, preferred_element_type=jnp.float32
    )
    shift_one, scale_one, gate_one, shift_two, scale_two, gate_two = jnp.split(mod_rows, 6, axis=1)
    normed1, norm1_back = jax.vjp(norm_modulate, start, shift_one, scale_one)
    normed1_bf = normed1.astype(jnp.bfloat16)
    projected = jnp.dot(normed1_bf, attn_full, preferred_element_type=jnp.float32)
    attn_bias_f = attn_bfull.astype(jnp.float32)
    query_bf = (projected[:, :model_width] + attn_bias_f[:model_width]).astype(jnp.bfloat16)
    key_bf = projected[:, model_width : 2 * model_width].astype(jnp.bfloat16)
    value_bf = (projected[:, 2 * model_width :] + attn_bias_f[model_width:]).astype(jnp.bfloat16)
    attended, log_totals = attend_forward(query_bf, key_bf, value_bf, segment, HEADS)
    attended_bf = attended.astype(jnp.bfloat16)
    out_bias_f = out_bfull.astype(jnp.float32)
    branch1 = (
        jnp.dot(attended_bf, proj_full, preferred_element_type=jnp.float32)
        + out_bias_f[:model_width]
    )
    middle = start + gate_one * branch1
    normed2, norm2_back = jax.vjp(norm_modulate, middle, shift_two, scale_two)
    normed2_bf = normed2.astype(jnp.bfloat16)
    hidden_pre = jnp.dot(normed2_bf, up_full, preferred_element_type=jnp.float32) + up_bfull.astype(
        jnp.float32
    )
    hidden_act, gelu_back = jax.vjp(partial(jax.nn.gelu, approximate=True), hidden_pre)
    hidden_bf = hidden_act.astype(jnp.bfloat16)
    branch2 = (
        jnp.dot(hidden_bf, down_full, preferred_element_type=jnp.float32) + out_bias_f[model_width:]
    )
    mixed = (middle + gate_two * branch2).astype(jnp.bfloat16)
    out_grad = grad_out.astype(jnp.float32)
    grad_gate_two = out_grad * branch2
    grad_branch2 = (out_grad * gate_two).astype(jnp.bfloat16)
    down_grad = matmul_tn(hidden_bf, grad_branch2)
    hidden_grad = matmul_nt(grad_branch2, down_full)
    pre_grad = gelu_back(hidden_grad)[0].astype(jnp.bfloat16)
    up_grad = matmul_tn(normed2_bf, pre_grad)
    up_bias_term = jnp.sum(pre_grad, axis=0, dtype=jnp.float32)
    part_up, part_down, part_bias = (
        lax.psum_scatter(
            up_grad.astype(jnp.bfloat16), "dp", scatter_dimension=1, tiled=True
        ).astype(jnp.float32),
        lax.psum_scatter(
            down_grad.astype(jnp.bfloat16), "dp", scatter_dimension=1, tiled=True
        ).astype(jnp.float32),
        lax.psum_scatter(
            up_bias_term.astype(jnp.bfloat16), "dp", scatter_dimension=0, tiled=True
        ).astype(jnp.float32),
    )
    up_weight_grad, down_weight_grad, up_bias_grad = (
        lax.psum_scatter(part_up, "fsdp", scatter_dimension=0, tiled=True),
        lax.psum_scatter(part_down, "fsdp", scatter_dimension=0, tiled=True),
        lax.psum_scatter(part_bias, "fsdp", scatter_dimension=0, tiled=True),
    )
    normed2_grad = matmul_nt(pre_grad, up_full)
    middle_part, grad_shift_two, grad_scale_two = norm2_back(normed2_grad)
    middle_grad = out_grad + middle_part
    grad_gate_one = middle_grad * branch1
    grad_branch1 = (middle_grad * gate_one).astype(jnp.bfloat16)
    proj_grad = matmul_tn(attended_bf, grad_branch1)
    attended_grad = matmul_nt(grad_branch1, proj_full).astype(jnp.bfloat16)
    query_grad, key_grad, value_grad = attend_backward(
        query_bf, key_bf, value_bf, attended_grad, segment, log_totals, HEADS
    )
    query_grad_bf = query_grad.astype(jnp.bfloat16)
    value_grad_bf = value_grad.astype(jnp.bfloat16)
    joined_grad = jnp.concatenate(
        [query_grad_bf, key_grad.astype(jnp.bfloat16), value_grad_bf], axis=1
    )
    attn_grad = matmul_tn(normed1_bf, joined_grad)
    attn_bias_term = jnp.concatenate(
        [
            jnp.sum(query_grad_bf, axis=0, dtype=jnp.float32),
            jnp.sum(value_grad_bf, axis=0, dtype=jnp.float32),
        ]
    )
    normed1_grad = matmul_nt(joined_grad, attn_full)
    start_part, grad_shift_one, grad_scale_one = norm1_back(normed1_grad)
    tokens_grad = middle_grad + start_part
    mod_rows_grad = jnp.concatenate(
        [
            grad_shift_one,
            grad_scale_one,
            grad_gate_one,
            grad_shift_two,
            grad_scale_two,
            grad_gate_two,
        ],
        axis=1,
    )
    modulation_grad = lax.dot_general(
        slot_table,
        mod_rows_grad,
        (((0,), (0,)), ((), ())),
        precision=lax.Precision.HIGHEST,
        preferred_element_type=jnp.float32,
    ).astype(jnp.bfloat16)
    ada_grad = matmul_tn(silu_bf, modulation_grad)
    ada_bias_term = jnp.sum(modulation_grad, axis=0, dtype=jnp.float32)
    condition_grad = silu_back(matmul_nt(modulation_grad, ada_full))[0]
    out_bias_term = jnp.concatenate(
        [
            jnp.sum(grad_branch1, axis=0, dtype=jnp.float32),
            jnp.sum(grad_branch2, axis=0, dtype=jnp.float32),
        ]
    )
    shares = (
        lax.psum_scatter(
            ada_grad.astype(jnp.bfloat16), "dp", scatter_dimension=1, tiled=True
        ).astype(jnp.float32),
        lax.psum_scatter(
            attn_grad.astype(jnp.bfloat16), "dp", scatter_dimension=1, tiled=True
        ).astype(jnp.float32),
        lax.psum_scatter(
            proj_grad.astype(jnp.bfloat16), "dp", scatter_dimension=1, tiled=True
        ).astype(jnp.float32),
        lax.psum_scatter(
            ada_bias_term.astype(jnp.bfloat16), "dp", scatter_dimension=0, tiled=True
        ).astype(jnp.float32),
        lax.psum_scatter(
            attn_bias_term.astype(jnp.bfloat16), "dp", scatter_dimension=0, tiled=True
        ).astype(jnp.float32),
        lax.psum_scatter(
            out_bias_term.astype(jnp.bfloat16), "dp", scatter_dimension=0, tiled=True
        ).astype(jnp.float32),
    )
    (
        ada_weight_grad,
        attn_weight_grad,
        proj_weight_grad,
        ada_bias_grad,
        attn_bias_grad,
        out_bias_grad,
    ) = (
        lax.psum_scatter(shares[0], "fsdp", scatter_dimension=0, tiled=True),
        lax.psum_scatter(shares[1], "fsdp", scatter_dimension=0, tiled=True),
        lax.psum_scatter(shares[2], "fsdp", scatter_dimension=0, tiled=True),
        lax.psum_scatter(shares[3], "fsdp", scatter_dimension=0, tiled=True),
        lax.psum_scatter(shares[4], "fsdp", scatter_dimension=0, tiled=True),
        lax.psum_scatter(shares[5], "fsdp", scatter_dimension=0, tiled=True),
    )
    return (
        mixed,
        tokens_grad,
        condition_grad,
        ada_weight_grad,
        ada_bias_grad,
        attn_weight_grad,
        attn_bias_grad,
        proj_weight_grad,
        out_bias_grad,
        up_weight_grad,
        up_bias_grad,
        down_weight_grad,
    )


def solution(mesh):
    return jax.shard_map(
        per_device,
        mesh=mesh,
        in_specs=(
            P(("dp", "fsdp"), None),
            P(("dp", "fsdp"), None),
            P(("dp", "fsdp")),
            P(("dp", "fsdp")),
            P(("dp", "fsdp")),
            P("fsdp", "dp"),
            P(("dp", "fsdp")),
            P("fsdp", "dp"),
            P(("dp", "fsdp")),
            P("fsdp", "dp"),
            P(("dp", "fsdp")),
            P("fsdp", "dp"),
            P(("dp", "fsdp")),
            P("fsdp", "dp"),
            P(("dp", "fsdp"), None),
        ),
        out_specs=(
            P(("dp", "fsdp"), None),
            P(("dp", "fsdp"), None),
            P(("dp", "fsdp"), None),
            P("fsdp", "dp"),
            P(("dp", "fsdp")),
            P("fsdp", "dp"),
            P(("dp", "fsdp")),
            P("fsdp", "dp"),
            P(("dp", "fsdp")),
            P("fsdp", "dp"),
            P(("dp", "fsdp")),
            P("fsdp", "dp"),
        ),
        check_vma=False,
    )
```

profile of v0, /device:TPU:0, one launch (start us, length us, event | category | flops | bytes accessed | tf_op | source)
XLA Modules:
  0.0 1398.0 jit_solution(7367727196981750000)
XLA Ops:
  9.4 38.2 %all-gather.26.cloned.1.call-done = bf16[4,1728,144]{1,2,0:T(8,128)(2,1)} async-done(((bf16[1,1728,144]{1,2,0:T(8,128)(2,1)}), bf16[4,1728,144]{1,2,0:T(8,128)(2,1)}) %all-gather.26.cloned.1.call-update) | async-done | bytes 1990672 | tf_op jit(solution)/shard_map/all_gather | solution.py:154
  53.2 15.6 %all-gather.1 = bf16[4,864,144]{1,2,0:T(8,128)(2,1)S(1)} all-gather(bf16[1,864,144]{1,2,0:T(8,128)(2,1)S(1)} %bitcast.110), channel_id=1, replica_groups=mesh['dp'=4,'fsdp'=8] {'dp'}, dimensions={0}, use_global_device_ids=true | all-gather | bytes 1244160 | tf_op jit(solution)/shard_map/all_gather | solution.py:155
  71.0 13.6 all-gather.2
  86.8 30.2 %all-gather.22.cloned.1.call-done = bf16[576,1152]{0,1:T(8,128)(2,1)} async-done(((bf16[576,288]{0,1:T(8,128)(2,1)}), bf16[576,1152]{0,1:T(8,128)(2,1)}) %all-gather.22.cloned.1.call-update) | async-done | bytes 1327120 | tf_op jit(solution)/shard_map/all_gather | solution.py:158
  125.2 9.0 all-reduce.19
  135.2 31.6 %all-reduce.17 = (bf16[6912]{0:T(1024)(128)(2,1)S(1)}, bf16[2304]{0:T(1024)(128)(2,1)S(1)}, bf16[2304]{0:T(1024)(128)(2,1)S(1)}, bf16[4608]{0:T(1024)(128)(2,1)S(1)}) all-reduce(bf16[6912]{0:T(1024)(128)(2,1)S(1)} %dynamic-update-slice.1, bf16[2304]{0:T(1024)(128)(2,1)S(1)} %dynamic-update-slice.3, ...), channel_id=1, replica_groups=mesh['dp'=4,'fsdp'=8] {'fsdp'}, use_global_device_ids=true, to_apply=%add.1 | all-reduce | flops 16128 | bytes 64512
  182.7 81.2 %all-gather.12.cloned.1.call-done = bf16[1152,6912]{1,0:T(8,128)(2,1)} async-done(((bf16[144,6912]{1,0:T(8,128)(2,1)}), bf16[1152,6912]{1,0:T(8,128)(2,1)}) %all-gather.12.cloned.1.call-update) | async-done | bytes 15925264 | tf_op jit(solution)/shard_map/all_gather | solution.py:175
  282.9 59.8 %all-gather.14.cloned.1.call-done = bf16[1152,3456]{1,0:T(8,128)(2,1)} async-done(((bf16[144,3456]{1,0:T(8,128)(2,1)}), bf16[1152,3456]{1,0:T(8,128)(2,1)}) %all-gather.14.cloned.1.call-update) | async-done | bytes 7962640 | tf_op jit(solution)/shard_map/all_gather | solution.py:176
  342.7 18.6 %fusion.61 = f32[512,3456]{1,0:T(8,128)S(1)} fusion(bf16[512,1152]{1,0:T(8,128)(2,1)S(1)} %fusion.18, bf16[1152,3456]{1,0:T(8,128)(2,1)} %all-gather.14.cloned.1.call-done), kind=kOutput, calls=%fused_computation.134 | convolution fusion | flops 4076863488 | bytes 16220160 | tf_op jit(solution)/shard_map/dot_general | solution.py:206
  411.0 67.7 %all-gather.20.cloned.1.call-done = bf16[1152,4608]{1,0:T(8,128)(2,1)} async-done(((bf16[144,4608]{1,0:T(8,128)(2,1)}), bf16[1152,4608]{1,0:T(8,128)(2,1)}) %all-gather.20.cloned.1.call-update) | async-done | bytes 10616848 | tf_op jit(solution)/shard_map/all_gather | solution.py:178
  501.8 77.4 %all-gather.24.cloned.1.call-done = bf16[4608,1152]{1,0:T(8,128)(2,1)} async-done(((bf16[576,1152]{1,0:T(8,128)(2,1)}), bf16[4608,1152]{1,0:T(8,128)(2,1)}) %all-gather.24.cloned.1.call-update) | async-done | bytes 10616848 | tf_op jit(solution)/shard_map/all_gather | solution.py:179
  579.2 16.7 %fusion.44 = (bf16[4608]{0:T(1024)(128)(2,1)}, bf16[512,4608]{1,0:T(8,128)(2,1)S(1)}) fusion(f32[512,4608]{1,0:T(8,128)} %copy-done.67, f32[4608]{0:T(1024)} %reshape.206, bf16[512,1152]{1,0:T(8,128)(2,1)} %copy-done.28, bf16[4608,1152]{1,0:T(8,128)(2,1)} %all-gather.24.cloned.1.call-done), kind=kOutput, calls=%fused_computation.119 | convolution fusion | flops 5487717888 | bytes 25979904 | tf_op jit(solution)/shard_map/dot_general | solution.py:33
  595.9 13.4 multiply_reduce_fusion.2
  609.3 17.3 %fusion.50 = (f32[512]{0:T(512)S(1)}, f32[512,1152]{1,0:T(8,128)S(1)}, bf16[512,1152]{1,0:T(8,128)(2,1)}, f32[512,1152]{1,0:T(8,128)}) fusion(f32[512]{0:T(512)S(1)} %multiply_multiply_fusion.3, f32[512,1152]{1,0:T(8,128)S(1)} %copy-done.4, f32[512]{0:T(512)S(1)} %broadcast_multiply_fusion, f32[512]{0:T(512)S(1)} %fusion.39, ...), kind=kOutput, calls=%fused_computation.123 | convolution fusion | flops 5466488320 | bytes 35420672 | tf_op jit(solution)/shard_map/dot_general | solution.py:227
  643.2 11.4 multiply_reduce_fusion
  654.7 12.5 multiply_convert_fusion
  672.0 9.7 fusion.59
  682.8 10.4 convolution_convert_fusion.3
  694.4 10.6 convolution_convert_fusion.2
  705.0 15.4 %copy.149 = bf16[1152,4608]{0,1:T(8,128)(2,1)} copy(bf16[1152,4608]{1,0:T(8,128)(2,1)} %convolution_convert_fusion.2) | data formatting | bytes 21233664
  722.1 11.8 constant_dynamic-update-slice_fusion.1
  772.7 41.8 %reduce-scatter.23.cloned.1.call-done = bf16[1152,864]{0,1:T(8,128)(2,1)} async-done(((bf16[1152,3456]{0,1:T(8,128)(2,1)}), bf16[1152,864]{0,1:T(8,128)(2,1)}) %reduce-scatter.23.cloned.1.call-update) | async-done | bytes 1990672 | tf_op jit(solution)/shard_map/reduce_scatter | solution.py:310
  818.9 103.6 %reduce-scatter.37.cloned.1.call-done = bf16[1152,1152]{1,0:T(8,128)(2,1)} async-done(((bf16[4608,1152]{1,0:T(8,128)(2,1)}), bf16[1152,1152]{1,0:T(8,128)(2,1)}) %reduce-scatter.37.cloned.1.call-update) | async-done | bytes 2654224
  929.2 143.9 %reduce-scatter.21.cloned.1.call-done = bf16[1152,1728]{0,1:T(8,128)(2,1)} async-done(((bf16[1152,6912]{0,1:T(8,128)(2,1)}), bf16[1152,1728]{0,1:T(8,128)(2,1)}) %reduce-scatter.21.cloned.1.call-update) | async-done | bytes 3981328 | tf_op jit(solution)/shard_map/reduce_scatter | solution.py:307
  1084.3 15.7 %all-reduce.18 = (bf16[6912]{0:T(1024)(128)(2,1)S(1)}, bf16[2304]{0:T(1024)(128)(2,1)S(1)}, bf16[2304]{0:T(1024)(128)(2,1)S(1)}, bf16[4608]{0:T(1024)(128)(2,1)S(1)}) all-reduce(bf16[6912]{0:T(1024)(128)(2,1)S(1)} %get-tuple-element.198, bf16[2304]{0:T(1024)(128)(2,1)S(1)} %pad_maximum_fusion.3, ...), channel_id=4, replica_groups=mesh['dp'=4,'fsdp'=8] {'dp'}, use_global_device_ids=true, to_apply=%region_15.16.clone | all-reduce | flops 16128 | bytes 64512
  1100.3 28.0 %all-reduce.16 = (f32[1728]{0:T(1024)S(1)}, f32[576]{0:T(1024)S(1)}, f32[576]{0:T(1024)S(1)}, f32[1152]{0:T(1024)S(1)}) all-reduce(f32[1728]{0:T(1024)S(1)} %dynamic-slice_convert_fusion.1, f32[576]{0:T(1024)S(1)} %dynamic-slice_convert_fusion.3, ...), channel_id=5, replica_groups=mesh['dp'=4,'fsdp'=8] {'fsdp'}, use_global_device_ids=true, to_apply=%region_16.17.clone | all-reduce | flops 4032 | bytes 32256
  1130.7 10.5 fusion.31
  1141.3 11.9 reduce-scatter.39.cloned.1.call-done
  1155.5 33.7 %reduce-scatter.35.cloned.1.call-done = f32[144,288]{1,0:T(8,128)} async-done(((f32[1152,288]{1,0:T(8,128)}), f32[144,288]{1,0:T(8,128)}) %reduce-scatter.35.cloned.1.call-update) | async-done | bytes 165904
  1189.2 50.3 %reduce-scatter.33.cloned.1.call-done = f32[144,864]{1,0:T(8,128)} async-done(((f32[1152,864]{1,0:T(8,128)}), f32[144,864]{1,0:T(8,128)}) %reduce-scatter.33.cloned.1.call-update) | async-done | bytes 497680
  1239.5 61.5 %reduce-scatter.27.cloned.1.call-done = f32[144,1152]{1,0:T(8,128)} async-done(((f32[1152,1152]{1,0:T(8,128)}), f32[144,1152]{1,0:T(8,128)}) %reduce-scatter.27.cloned.1.call-update) | async-done | bytes 663568 | tf_op jit(solution)/shard_map/reduce_scatter | solution.py:250
  1301.1 89.6 %reduce-scatter.31.cloned.1.call-done = f32[144,1728]{1,0:T(8,128)} async-done(((f32[1152,1728]{1,0:T(8,128)}), f32[144,1728]{1,0:T(8,128)}) %reduce-scatter.31.cloned.1.call-update) | async-done | bytes 995344
  (284 shorter events, 212.0 us)
Async XLA Ops:
  7.2 40.5 %all-gather.26.cloned.1.call-start = ((), (), s32[]{:S(2)}) async-start(), calls=%async_computation.22 | async-start | bytes 2580480 | tf_op jit(solution)/shard_map/all_gather | solution.py:154
  7.9 78.1 %all-gather.18.cloned.1.call-start = ((), (), s32[]{:S(2)}) async-start(), calls=%async_computation.13 | async-start | bytes 1658880 | tf_op jit(solution)/shard_map/all_gather | solution.py:157
  8.7 108.4 %all-gather.22.cloned.1.call-start = ((), (), s32[]{:S(2)}) async-start(), calls=%async_computation.15 | async-start | bytes 1843200 | tf_op jit(solution)/shard_map/all_gather | solution.py:158
  9.4 254.4 %all-gather.12.cloned.1.call-start = ((), (), s32[]{:S(2)}) async-start(), calls=%async_computation.10 | async-start | bytes 17915904 | tf_op jit(solution)/shard_map/all_gather | solution.py:175
  53.1 289.6 %all-gather.14.cloned.1.call-start = ((), (), s32[]{:S(2)}) async-start(), calls=%async_computation.11 | async-start | bytes 8957952 | tf_op jit(solution)/shard_map/all_gather | solution.py:176
  71.0 324.8 %all-gather.16.cloned.1.call-start = ((), (), s32[]{:S(2)}) async-start(), calls=%async_computation.12 | async-start | bytes 2985984 | tf_op jit(solution)/shard_map/all_gather | solution.py:177
  85.9 392.8 %all-gather.20.cloned.1.call-start = ((), (), s32[]{:S(2)}) async-start(), calls=%async_computation.14 | async-start | bytes 11943936 | tf_op jit(solution)/shard_map/all_gather | solution.py:178
  86.7 38.0 %copy-start.64 = (bf16[144]{0:T(256)(128)(2,1)S(1)}, bf16[144]{0:T(256)(128)(2,1)}, u32[]{:S(2)}) copy-start(bf16[144]{0:T(256)(128)(2,1)} %param.27) | copy-start | bytes 868
  86.7 38.3 %copy-start.65 = (bf16[216]{0:T(256)(128)(2,1)S(1)}, bf16[216]{0:T(256)(128)(2,1)}, u32[]{:S(2)}) copy-start(bf16[216]{0:T(256)(128)(2,1)} %param.21) | copy-start | bytes 1300
  86.7 83.4 %copy-start.33 = (s32[512]{0:T(512)S(1)}, s32[512]{0:T(512)}, u32[]{:S(2)}) copy-start(s32[512]{0:T(512)} %param.18) | copy-start | bytes 6148
  86.7 83.4 %copy-start.61 = (s32[4]{0:T(128)S(1)}, s32[4]{0:T(128)}, u32[]{:S(2)}) copy-start(s32[4]{0:T(128)} %param.19) | copy-start | bytes 52
  86.8 83.5 %copy-start.60 = (s32[512]{0:T(512)S(1)}, s32[512]{0:T(512)}, u32[]{:S(2)}) copy-start(s32[512]{0:T(512)} %param.17) | copy-start | bytes 6148
  86.8 492.5 %all-gather.24.cloned.1.call-start = ((), (), s32[]{:S(2)}) async-start(), calls=%async_computation.16 | async-start | bytes 11943936 | tf_op jit(solution)/shard_map/all_gather | solution.py:179
  119.7 644.5 %reduce-scatter.29.cloned.1.call-start = ((), (), s32[]{:S(2)}) async-start(), calls=%async_computation.21 | async-start | bytes 13271040 | tf_op jit(solution)/shard_map/reduce_scatter | solution.py:242
  181.2 214.6 %copy-start.1 = (f32[512,1152]{1,0:T(8,128)}, f32[512,1152]{1,0:T(8,128)S(1)}, u32[]{:S(2)}) copy-start(f32[512,1152]{1,0:T(8,128)S(1)} %get-tuple-element.164) | copy-start | bytes 7077892
  181.2 82.7 %copy-start.37 = (bf16[4,1152]{1,0:T(4,128)(2,1)S(1)}, bf16[4,1152]{1,0:T(4,128)(2,1)}, u32[]{:S(2)}) copy-start(bf16[4,1152]{1,0:T(4,128)(2,1)} %param.16) | copy-start | bytes 27652
  181.2 96.1 %copy-start.39 = (f32[512]{0:T(512)}, f32[512]{0:T(512)S(1)}, u32[]{:S(2)}) copy-start(f32[512]{0:T(512)S(1)} %broadcast_multiply_fusion.1) | copy-start | bytes 6148
  181.6 90.0 %copy-start.50 = (f32[512]{0:T(512)}, f32[512]{0:T(512)S(1)}, u32[]{:S(2)}) copy-start(f32[512]{0:T(512)S(1)} %multiply_reduce_fusion.4) | copy-start | bytes 6148
  181.6 95.7 %copy-start.46 = (f32[512]{0:T(512)}, f32[512]{0:T(512)S(1)}, u32[]{:S(2)}) copy-start(f32[512]{0:T(512)S(1)} %fusion.38) | copy-start | bytes 6148
  282.9 78.5 %copy-start.22 = (bf16[512,1152]{1,0:T(8,128)(2,1)}, bf16[512,1152]{1,0:T(8,128)(2,1)S(1)}, u32[]{:S(2)}) copy-start(bf16[512,1152]{1,0:T(8,128)(2,1)S(1)} %fusion.18) | copy-start | bytes 3538948
  407.6 80.2 %copy-start.28 = (bf16[512,1152]{1,0:T(8,128)(2,1)}, bf16[512,1152]{1,0:T(8,128)(2,1)S(1)}, u32[]{:S(2)}) copy-start(bf16[512,1152]{1,0:T(8,128)(2,1)S(1)} %get-tuple-element.156) | copy-start | bytes 3538948
  411.0 76.7 %copy-start.24 = (bf16[512,1152]{1,0:T(8,128)(2,1)}, bf16[512,1152]{1,0:T(8,128)(2,1)S(1)}, u32[]{:S(2)}) copy-start(bf16[512,1152]{1,0:T(8,128)(2,1)S(1)} %fusion.15) | copy-start | bytes 3538948
  500.5 269.5 %reduce-scatter.25.cloned.1.call-start = ((), (), s32[]{:S(2)}) async-start(), calls=%async_computation.19 | async-start | bytes 3317760 | tf_op jit(solution)/shard_map/reduce_scatter | solution.py:313
  501.8 94.1 %copy-start.4 = (f32[512,1152]{1,0:T(8,128)S(1)}, f32[512,1152]{1,0:T(8,128)}, u32[]{:S(2)}) copy-start(f32[512,1152]{1,0:T(8,128)} %copy-done.3) | copy-start | bytes 7077892
  642.0 172.5 %reduce-scatter.23.cloned.1.call-start = ((), (), s32[]{:S(2)}) async-start(), calls=%async_computation.18 | async-start | bytes 9953280 | tf_op jit(solution)/shard_map/reduce_scatter | solution.py:310
  693.2 229.2 %reduce-scatter.37.cloned.1.call-start = ((), (), s32[]{:S(2)}) async-start(), calls=%async_computation.26 | async-start | bytes 13271040
  720.4 352.7 %reduce-scatter.21.cloned.1.call-start = ((), (), s32[]{:S(2)}) async-start(), calls=%async_computation.17 | async-start | bytes 19906560 | tf_op jit(solution)/shard_map/reduce_scatter | solution.py:307
  764.1 389.1 %reduce-scatter.39.cloned.1.call-start = ((), (), s32[]{:S(2)}) async-start(), calls=%async_computation.27 | async-start | bytes 7962624
  769.9 419.3 %reduce-scatter.35.cloned.1.call-start = ((), (), s32[]{:S(2)}) async-start(), calls=%async_computation.25 | async-start | bytes 1990656
  772.6 466.9 %reduce-scatter.33.cloned.1.call-start = ((), (), s32[]{:S(2)}) async-start(), calls=%async_computation.24 | async-start | bytes 4644864
  818.8 482.3 %reduce-scatter.27.cloned.1.call-start = ((), (), s32[]{:S(2)}) async-start(), calls=%async_computation.20 | async-start | bytes 5971968 | tf_op jit(solution)/shard_map/reduce_scatter | solution.py:250
  929.2 461.5 %reduce-scatter.31.cloned.1.call-start = ((), (), s32[]{:S(2)}) async-start(), calls=%async_computation.23 | async-start | bytes 9289728
  (54 other events, 424.8 us)
Sparse Core Ops, SparseCore 0:
  9.9 37.7 all-gather.25
  49.5 35.3 all-gather.17
  86.7 30.3 all-gather.21
  118.5 145.2 all-gather.11
  265.9 76.7 all-gather.13
  344.8 32.7 all-gather.15
  379.2 99.4 all-gather.19
  480.3 98.8 all-gather.23
  582.3 102.9 reduce-scatter.28
  688.2 39.8 reduce-scatter.24
  731.2 83.2 reduce-scatter.22
  817.8 104.6 reduce-scatter.36
  925.8 147.2 reduce-scatter.20
  1075.3 77.8 reduce-scatter.38
  1155.9 33.2 reduce-scatter.34
  1192.0 47.5 reduce-scatter.32
  1242.4 58.6 reduce-scatter.26
  1303.9 86.7 reduce-scatter.30
where the time goes:
time: 1400 us
  waiting for transfers between devices  894 us (64%)
  matrix products  213 us (15%)
  blocking collectives  114 us (8%)
  local copies, waits for them, and re-layouts  96 us (7%)
  other arithmetic  57.1 us (4%)
  between operations  23.4 us (2%)
    unnamed x23, waiting for transfers between devices  292 us
    reduce_scatter x1, waiting for transfers between devices, per_device(): lax.psum_scatter(ada_grad.astype(jnp.bfloat16), 'dp', scatter_dimension=1...  144 us
    unnamed x4, blocking collectives  84.3 us
    all_gather x1, waiting for transfers between devices, per_device(): lax.all_gather(gathered[0], 'fsdp', axis=0, tiled=True)  81.2 us
    all_gather x1, waiting for transfers between devices, per_device(): lax.all_gather(gathered[4], 'fsdp', axis=0, tiled=True)  77.4 us
    unnamed x168, local copies, waits for them, and re-layouts  74.5 us
    all_gather x1, waiting for transfers between devices, per_device(): lax.all_gather(gathered[3], 'fsdp', axis=0, tiled=True)  67.7 us
    reduce_scatter x1, waiting for transfers between devices, per_device(): lax.psum_scatter(part_up, 'fsdp', scatter_dimension=0, tiled=True)  61.5 us
  transfers between devices with their start and end apart: 18, of which 14 were waited for; matrix products, arithmetic and copies ran while one was open for 25% of the time, Pallas kernels for 0%

commit v1 on v0

--- a/solution.py
+++ b/solution.py
@@ -4,9 +4,12 @@
 import jax
 import jax.numpy as jnp
 from jax import lax
+from jax.experimental import pallas as pl
+from jax.experimental.pallas import tpu as pltpu
 from jax.sharding import PartitionSpec as P
 
 HEADS = 16
+AXES = ("dp", "fsdp")
 
 
 def position_code(kept_index, side_rows, model_width):
@@ -123,6 +126,282 @@
         sums[0].reshape(row_count, model_width),
         sums[1].reshape(row_count, model_width),
     )
+
+
+def on_box():
+    return lax.axis_size("dp") == 4 and lax.axis_size("fsdp") == 8
+
+
+def neighbour(index, axis):
+    plane, line = index // 8, index % 8
+    if axis == "x":
+        plane ^= 1
+    elif axis == "y":
+        plane ^= 2
+    elif axis == "core":
+        line ^= 1
+    else:
+        line = (line - 2 * axis) % 8
+    return plane * 8 + line
+
+
+def swap(values, axis):
+    return lax.ppermute(values, AXES, [(index, neighbour(index, axis)) for index in range(32)])
+
+
+HALF_ORDERS = (("x", 1, "y", 2), ("y", 2, "x", 1))
+
+
+def place():
+    plane, line = lax.axis_index("dp"), lax.axis_index("fsdp")
+    return plane, line // 2, line % 2
+
+
+def flipped(plane, flip):
+    if flip % 2:
+        plane = plane + 1 - 2 * (plane % 2)
+    if flip // 2:
+        plane = plane + 2 - 4 * (plane // 2)
+    return plane
+
+
+def gather_line(shard):
+    return [shard] + [swap(shard, turn) for turn in (1, 2, 3)]
+
+
+def gather_plane(line):
+    depth = place()[1]
+    ring = jnp.stack(line + line)
+    begin = (4 - depth) % 4
+    own = []
+    for half, (first, first_flip, second, second_flip) in enumerate(HALF_ORDERS):
+        piece = lax.dynamic_slice_in_dim(ring, begin + 2 * half, 2, axis=0)
+        beside = swap(piece, first)
+        across = [swap(piece, second), swap(beside, second)]
+        found = [piece, None, None, across[1]]
+        found[first_flip] = beside
+        found[second_flip] = across[0]
+        own.append(found)
+    other = [[swap(piece, "core") for piece in found] for found in own]
+    return (own, other)
+
+
+def lay_out(plane_major, *refs):
+    pieces, out, sems = refs[:16], refs[16], refs[17]
+    plane, _, core = place()
+    copies = []
+    for flip_core in range(2):
+        for half in range(2):
+            for flip in range(4):
+                at = flipped(plane, flip)
+                side = core if flip_core == 0 else 1 - core
+                rows = pl.ds(2 * half, 2)
+                target = out.at[at, rows, side] if plane_major else out.at[rows, at, side]
+                count = len(copies)
+                copies.append(pltpu.make_async_copy(pieces[count], target, sems.at[count]))
+    for copy in copies:
+        copy.start()
+    for copy in copies:
+        copy.wait()
+
+
+def assemble(pieces, plane_major):
+    flat = [piece for side in pieces for found in side for piece in found]
+    rows, columns = flat[0].shape[1:]
+    whole = pl.pallas_call(
+        partial(lay_out, plane_major),
+        out_shape=jax.ShapeDtypeStruct((4, 4, 2, rows, columns), flat[0].dtype),
+        in_specs=[pl.BlockSpec(memory_space=pl.ANY)] * 16,
+        out_specs=pl.BlockSpec(memory_space=pl.ANY),
+        scratch_shapes=[pltpu.SemaphoreType.DMA((16,))],
+        cost_estimate=pl.CostEstimate(
+            flops=0, bytes_accessed=2 * 32 * rows * columns * 2, transcendentals=0
+        ),
+    )(*flat)
+    return whole.reshape(4, 8 * rows, columns)
+
+
+def scatter_terms(sibling, own):
+    depth = place()[1]
+    totals = []
+    for half, (first, first_flip, second, second_flip) in enumerate(HALF_ORDERS):
+        summed = [
+            own[half][flip].astype(jnp.float32)
+            + swap(sibling[half][flip].astype(jnp.bfloat16), "core").astype(jnp.float32)
+            for flip in range(4)
+        ]
+        across = summed[second_flip] + swap(summed[3].astype(jnp.bfloat16), first).astype(jnp.float32)
+        home = summed[0] + swap(summed[first_flip].astype(jnp.bfloat16), first).astype(jnp.float32)
+        totals.append(home + swap(across.astype(jnp.bfloat16), second).astype(jnp.float32))
+    total = jnp.concatenate(totals)
+    result = lax.dynamic_index_in_dim(total, depth, axis=0, keepdims=False)
+    for turn in (1, 2, 3):
+        term = lax.dynamic_index_in_dim(total, (depth - turn) % 4, axis=0, keepdims=False)
+        result = result + swap(term.astype(jnp.bfloat16), turn).astype(jnp.float32)
+    return result
+
+
+def halves(terms):
+    return [[term[:2] for term in terms], [term[2:] for term in terms]]
+
+
+def core_columns(values):
+    rows, columns = values.shape
+    core = place()[2]
+    cut = values.reshape(rows, 4, 2, columns // 8)
+    return [
+        lax.dynamic_index_in_dim(cut, side, axis=2, keepdims=False).reshape(rows, columns // 2)
+        for side in (core, 1 - core)
+    ]
+
+
+def pick(values, index):
+    return lax.dynamic_index_in_dim(values, index, axis=0, keepdims=False)
+
+
+def gather_blocks(attn_weight, proj_weight, up_weight, down_weight):
+    if not on_box():
+        parts = lax.axis_size("dp")
+        attn, proj, up, down = [
+            lax.all_gather(lax.all_gather(weight, "dp", axis=1, tiled=True), "fsdp", axis=0, tiled=True)
+            for weight in (attn_weight, proj_weight, up_weight, down_weight)
+        ]
+        width = attn.shape[0]
+
+        def by_block(weight):
+            return weight.reshape(weight.shape[0], parts, -1).transpose(1, 0, 2)
+
+        joined = jnp.concatenate([by_block(attn), by_block(proj)], axis=2)
+        return joined, by_block(up), by_block(down.T.reshape(width, -1))
+    core = place()[2]
+    rows, _ = up_weight.shape
+    joined_line = gather_line(jnp.concatenate([attn_weight, proj_weight], axis=1))
+    turned = down_weight.T.reshape(2, rows, down_weight.shape[0])
+    mine, theirs = pick(turned, core), pick(turned, 1 - core)
+    arrived = swap(theirs, "core")
+    down_shard = jnp.where(
+        core == 0,
+        jnp.concatenate([mine, arrived], axis=1),
+        jnp.concatenate([arrived, mine], axis=1),
+    )
+    up_shard, _ = lax.optimization_barrier((up_weight, joined_line[1:]))
+    up_line = gather_line(up_shard)
+    down_shard, _ = lax.optimization_barrier((down_shard, up_line[1:]))
+    down_line = gather_line(down_shard)
+    return (
+        assemble(gather_plane(joined_line), True),
+        assemble(gather_plane(up_line), True),
+        assemble(gather_plane(down_line), False),
+    )
+
+
+def scatter_down(hidden, grad_branch2):
+    if not on_box():
+        rows = hidden.shape[1]
+        flat = hidden.transpose(1, 0, 2).reshape(rows, -1)
+        return scatter_whole(matmul_tn(flat, grad_branch2))
+    plane, _, core = place()
+    width = grad_branch2.shape[1]
+    block = width // 8
+    columns = grad_branch2.reshape(-1, 4, 2, block)
+    order = jnp.stack([flipped(plane, flip) for flip in range(4)])
+    columns = jnp.take(columns, order, axis=1)
+    terms = []
+    for side in (1 - core, core):
+        lhs = lax.dynamic_index_in_dim(columns, side, axis=2, keepdims=False).reshape(-1, width // 2)
+        found = [matmul_tn(lhs, hidden[part]).reshape(4, block, -1) for part in range(4)]
+        if len(terms) == 0:
+            found = [value.astype(jnp.bfloat16) for value in found]
+        terms.append(
+            [
+                [jnp.stack([found[2 * half][flip], found[2 * half + 1][flip]]) for flip in range(4)]
+                for half in range(2)
+            ]
+        )
+    total = scatter_terms(terms[0], terms[1])
+    depth = total.shape[1] // 2
+    cut = total.reshape(block, 2, depth).transpose(1, 0, 2)
+    mine, theirs = pick(cut, core), pick(cut, 1 - core)
+    arrived = swap(theirs, "core")
+    whole = jnp.where(
+        core == 0, jnp.concatenate([mine, arrived]), jnp.concatenate([arrived, mine])
+    )
+    return whole.T
+
+
+def scatter_whole(gradient):
+    part = lax.psum_scatter(
+        gradient.astype(jnp.bfloat16), "dp", scatter_dimension=1, tiled=True
+    ).astype(jnp.float32)
+    return lax.psum_scatter(part, "fsdp", scatter_dimension=0, tiled=True)
+
+
+def scatter_rows(pairs):
+    if not on_box():
+        return [
+            scatter_whole(matmul_tn(left, right.transpose(1, 0, 2).reshape(left.shape[0], -1)))
+            for left, right in pairs
+        ]
+    plane = place()[0]
+    cut = [core_columns(left) for left, _ in pairs]
+    terms = []
+    for side in (1, 0):
+        found = []
+        for flip in range(4):
+            products = [
+                matmul_tn(left[side], pick(right, flipped(plane, flip)))
+                for left, (_, right) in zip(cut, pairs)
+            ]
+            joined = jnp.concatenate(products, axis=1)
+            if side:
+                joined = joined.astype(jnp.bfloat16)
+            found.append(joined.reshape(4, -1, joined.shape[1]))
+        terms.append(halves(found))
+    total = scatter_terms(terms[0], terms[1])
+    results, begin = [], 0
+    for _, right in pairs:
+        results.append(total[:, begin : begin + right.shape[2]])
+        begin += right.shape[2]
+    return results
+
+
+def modulate_slots(silu_bf, ada_weight, ada_bias):
+    planes, lines = lax.axis_size("dp"), lax.axis_size("fsdp")
+    slots = silu_bf.shape[0]
+    rows, columns = ada_weight.shape
+    everyone = lax.all_gather(silu_bf, AXES, axis=0, tiled=True)
+    silu_part = lax.dynamic_slice_in_dim(everyone, lax.axis_index("fsdp") * rows, rows, axis=1)
+    term = jnp.dot(silu_part, ada_weight, preferred_element_type=jnp.float32)
+    term = lax.psum_scatter(
+        term.reshape(planes, lines, slots, columns), "fsdp", scatter_dimension=1, tiled=True
+    )
+    term = lax.all_to_all(term.reshape(planes, slots, columns), "dp", 0, 0, tiled=True)
+    modulation = term.transpose(1, 0, 2).reshape(slots, planes * columns)
+    return modulation + ada_bias.astype(jnp.float32), silu_part
+
+
+def modulation_back(modulation_grad, silu_part, ada_weight):
+    planes, lines = lax.axis_size("dp"), lax.axis_size("fsdp")
+    slots = modulation_grad.shape[0]
+    rows, columns = ada_weight.shape
+    cut = modulation_grad.reshape(slots, planes, columns).transpose(1, 0, 2)
+    cut = lax.all_to_all(cut, "dp", 0, 0, tiled=True)
+    cut = lax.all_gather(cut, "fsdp", axis=1)
+    cut = cut.reshape(planes * lines * slots, columns)
+    ada_grad = matmul_tn(silu_part, cut)
+    sums = jnp.sum(cut, axis=0, dtype=jnp.float32)
+    bias_width = columns // lines
+    ada_bias_grad = lax.dynamic_slice_in_dim(sums, lax.axis_index("fsdp") * bias_width, bias_width)
+    silu_grad = matmul_nt(cut, ada_weight).reshape(planes, lines, slots, rows)
+    silu_grad = lax.psum_scatter(silu_grad, "dp", scatter_dimension=0, tiled=True)
+    silu_grad = lax.all_to_all(silu_grad.reshape(lines, slots, rows), "fsdp", 0, 0, tiled=True)
+    silu_grad = silu_grad.transpose(1, 0, 2).reshape(slots, lines * rows)
+    return ada_grad, ada_bias_grad, silu_grad
+
+
+def by_columns(values, parts):
+    rows, columns = values.shape
+    return values.reshape(rows, parts, columns // parts).transpose(1, 0, 2)
 
 
 def per_device(
@@ -144,48 +423,16 @@
 ):
     model_width = tokens.shape[1]
     slot_count = condition.shape[0]
-    row_parts = lax.axis_size("dp")
-    column_parts = lax.axis_size("fsdp")
-
-    def gather_order(vector):
-        return vector.reshape(column_parts, row_parts, -1).transpose(1, 0, 2).reshape(-1)
-
-    gathered = (
-        lax.all_gather(ada_weight, "dp", axis=1, tiled=True),
-        lax.all_gather(attn_weight, "dp", axis=1, tiled=True),
-        lax.all_gather(proj_weight, "dp", axis=1, tiled=True),
-        lax.all_gather(up_weight, "dp", axis=1, tiled=True),
-        lax.all_gather(down_weight, "dp", axis=1, tiled=True),
-        lax.all_gather(ada_bias, "dp", axis=0, tiled=True),
-        lax.all_gather(attn_bias, "dp", axis=0, tiled=True),
-        lax.all_gather(out_bias, "dp", axis=0, tiled=True),
-        lax.all_gather(up_bias, "dp", axis=0, tiled=True),
-    )
-    (
-        ada_full,
-        attn_full,
-        proj_full,
-        up_full,
-        down_full,
-        ada_bfull,
-        attn_bfull,
-        out_bfull,
-        up_bfull,
-    ) = (
-        lax.all_gather(gathered[0], "fsdp", axis=0, tiled=True),
-        lax.all_gather(gathered[1], "fsdp", axis=0, tiled=True),
-        lax.all_gather(gathered[2], "fsdp", axis=0, tiled=True),
-        lax.all_gather(gathered[3], "fsdp", axis=0, tiled=True),
-        lax.all_gather(gathered[4], "fsdp", axis=0, tiled=True),
-        lax.all_gather(gathered[5], "fsdp", axis=0, tiled=True),
-        lax.all_gather(gathered[6], "fsdp", axis=0, tiled=True),
-        lax.all_gather(gathered[7], "fsdp", axis=0, tiled=True),
-        lax.all_gather(gathered[8], "fsdp", axis=0, tiled=True),
-    )
-    ada_bfull = gather_order(ada_bfull)
-    attn_bfull = gather_order(attn_bfull)
-    out_bfull = gather_order(out_bfull)
-    up_bfull = gather_order(up_bfull)
+    planes = lax.axis_size("dp")
+    joined_w, up_w, down_w = gather_blocks(attn_weight, proj_weight, up_weight, down_weight)
+    attn_columns = attn_weight.shape[1]
+    small = (ada_bias, attn_bias, out_bias, up_bias)
+    everyone = lax.all_gather(jnp.concatenate(small), AXES, axis=0)
+    biases, begin = [], 0
+    for vector in small:
+        biases.append(everyone[:, begin : begin + vector.shape[0]].reshape(-1))
+        begin += vector.shape[0]
+    ada_bfull, attn_bfull, out_bfull, up_bfull = biases
     slot_ids = jnp.arange(slot_count, dtype=jnp.int32)
     same_slot = segment[:, None] == slot_ids[None, :]
     slot_table = same_slot.astype(jnp.float32)
@@ -194,16 +441,21 @@
     condition_f = condition.astype(jnp.float32)
     silu_cond, silu_back = jax.vjp(jax.nn.silu, condition_f)
     silu_bf = silu_cond.astype(jnp.bfloat16)
-    modulation = jnp.dot(silu_bf, ada_full, preferred_element_type=jnp.float32) + ada_bfull.astype(
-        jnp.float32
-    )
+    modulation, silu_part = modulate_slots(silu_bf, ada_weight, ada_bfull)
     mod_rows = jnp.dot(
         slot_table, modulation, precision=lax.Precision.HIGHEST, preferred_element_type=jnp.float32
     )
     shift_one, scale_one, gate_one, shift_two, scale_two, gate_two = jnp.split(mod_rows, 6, axis=1)
     normed1, norm1_back = jax.vjp(norm_modulate, start, shift_one, scale_one)
     normed1_bf = normed1.astype(jnp.bfloat16)
-    projected = jnp.dot(normed1_bf, attn_full, preferred_element_type=jnp.float32)
+    projected = jnp.concatenate(
+        [
+            jnp.dot(normed1_bf, joined_w[part, :, :attn_columns], preferred_element_type=jnp.float32)
+            for part in range(planes)
+        ],
+        axis=1,
+    )
+    proj_full = joined_w[:, :, attn_columns:].transpose(1, 0, 2).reshape(model_width, model_width)
     attn_bias_f = attn_bfull.astype(jnp.float32)
     query_bf = (projected[:, :model_width] + attn_bias_f[:model_width]).astype(jnp.bfloat16)
     key_bf = projected[:, model_width : 2 * model_width].astype(jnp.bfloat16)
@@ -218,45 +470,34 @@
     middle = start + gate_one * branch1
     normed2, norm2_back = jax.vjp(norm_modulate, middle, shift_two, scale_two)
     normed2_bf = normed2.astype(jnp.bfloat16)
-    hidden_pre = jnp.dot(normed2_bf, up_full, preferred_element_type=jnp.float32) + up_bfull.astype(
-        jnp.float32
-    )
-    hidden_act, gelu_back = jax.vjp(partial(jax.nn.gelu, approximate=True), hidden_pre)
-    hidden_bf = hidden_act.astype(jnp.bfloat16)
-    branch2 = (
-        jnp.dot(hidden_bf, down_full, preferred_element_type=jnp.float32) + out_bias_f[model_width:]
-    )
+    hidden_parts, gelu_parts = [], []
+    up_bias_f = up_bfull.astype(jnp.float32).reshape(planes, -1)
+    branch2 = out_bias_f[model_width:]
+    for part in range(planes):
+        hidden_pre = (
+            jnp.dot(normed2_bf, up_w[part], preferred_element_type=jnp.float32) + up_bias_f[part]
+        )
+        hidden_act, gelu_back = jax.vjp(partial(jax.nn.gelu, approximate=True), hidden_pre)
+        hidden_parts.append(hidden_act.astype(jnp.bfloat16))
+        gelu_parts.append(gelu_back)
+        branch2 = branch2 + matmul_nt(hidden_parts[part], down_w[part])
     mixed = (middle + gate_two * branch2).astype(jnp.bfloat16)
     out_grad = grad_out.astype(jnp.float32)
     grad_gate_two = out_grad * branch2
     grad_branch2 = (out_grad * gate_two).astype(jnp.bfloat16)
-    down_grad = matmul_tn(hidden_bf, grad_branch2)
-    hidden_grad = matmul_nt(grad_branch2, down_full)
-    pre_grad = gelu_back(hidden_grad)[0].astype(jnp.bfloat16)
-    up_grad = matmul_tn(normed2_bf, pre_grad)
-    up_bias_term = jnp.sum(pre_grad, axis=0, dtype=jnp.float32)
-    part_up, part_down, part_bias = (
-        lax.psum_scatter(
-            up_grad.astype(jnp.bfloat16), "dp", scatter_dimension=1, tiled=True
-        ).astype(jnp.float32),
-        lax.psum_scatter(
-            down_grad.astype(jnp.bfloat16), "dp", scatter_dimension=1, tiled=True
-        ).astype(jnp.float32),
-        lax.psum_scatter(
-            up_bias_term.astype(jnp.bfloat16), "dp", scatter_dimension=0, tiled=True
-        ).astype(jnp.float32),
-    )
-    up_weight_grad, down_weight_grad, up_bias_grad = (
-        lax.psum_scatter(part_up, "fsdp", scatter_dimension=0, tiled=True),
-        lax.psum_scatter(part_down, "fsdp", scatter_dimension=0, tiled=True),
-        lax.psum_scatter(part_bias, "fsdp", scatter_dimension=0, tiled=True),
-    )
-    normed2_grad = matmul_nt(pre_grad, up_full)
+    down_weight_grad = scatter_down(jnp.stack(hidden_parts), grad_branch2)
+    pre_parts = []
+    for part in range(planes):
+        hidden_grad = jnp.dot(grad_branch2, down_w[part], preferred_element_type=jnp.float32)
+        pre_parts.append(gelu_parts[part](hidden_grad)[0].astype(jnp.bfloat16))
+    pre_grad = jnp.stack(pre_parts)
+    (up_weight_grad,) = scatter_rows([(normed2_bf, pre_grad)])
+    up_bias_term = jnp.sum(pre_grad, axis=1, dtype=jnp.float32).reshape(-1)
+    normed2_grad = sum(matmul_nt(pre_parts[part], up_w[part]) for part in range(planes))
     middle_part, grad_shift_two, grad_scale_two = norm2_back(normed2_grad)
     middle_grad = out_grad + middle_part
     grad_gate_one = middle_grad * branch1
     grad_branch1 = (middle_grad * gate_one).astype(jnp.bfloat16)
-    proj_grad = matmul_tn(attended_bf, grad_branch1)
     attended_grad = matmul_nt(grad_branch1, proj_full).astype(jnp.bfloat16)
     query_grad, key_grad, value_grad = attend_backward(
         query_bf, key_bf, value_bf, attended_grad, segment, log_totals, HEADS
@@ -266,14 +507,19 @@
     joined_grad = jnp.concatenate(
         [query_grad_bf, key_grad.astype(jnp.bfloat16), value_grad_bf], axis=1
     )
-    attn_grad = matmul_tn(normed1_bf, joined_grad)
+    joined_parts = by_columns(joined_grad, planes)
+    attn_weight_grad, proj_weight_grad = scatter_rows(
+        [(normed1_bf, joined_parts), (attended_bf, by_columns(grad_branch1, planes))]
+    )
     attn_bias_term = jnp.concatenate(
         [
             jnp.sum(query_grad_bf, axis=0, dtype=jnp.float32),
             jnp.sum(value_grad_bf, axis=0, dtype=jnp.float32),
         ]
     )
-    normed1_grad = matmul_nt(joined_grad, attn_full)
+    normed1_grad = sum(
+        matmul_nt(joined_parts[part], joined_w[part, :, :attn_columns]) for part in range(planes)
+    )
     start_part, grad_shift_one, grad_scale_one = norm1_back(normed1_grad)
     tokens_grad = middle_grad + start_part
     mod_rows_grad = jnp.concatenate(
@@ -294,49 +540,20 @@
         precision=lax.Precision.HIGHEST,
         preferred_element_type=jnp.float32,
     ).astype(jnp.bfloat16)
-    ada_grad = matmul_tn(silu_bf, modulation_grad)
-    ada_bias_term = jnp.sum(modulation_grad, axis=0, dtype=jnp.float32)
-    condition_grad = silu_back(matmul_nt(modulation_grad, ada_full))[0]
+    ada_weight_grad, ada_bias_grad, silu_grad = modulation_back(modulation_grad, silu_part, ada_weight)
+    condition_grad = silu_back(silu_grad)[0]
     out_bias_term = jnp.concatenate(
         [
             jnp.sum(grad_branch1, axis=0, dtype=jnp.float32),
             jnp.sum(grad_branch2, axis=0, dtype=jnp.float32),
         ]
     )
-    shares = (
-        lax.psum_scatter(
-            ada_grad.astype(jnp.bfloat16), "dp", scatter_dimension=1, tiled=True
-        ).astype(jnp.float32),
-        lax.psum_scatter(
-            attn_grad.astype(jnp.bfloat16), "dp", scatter_dimension=1, tiled=True
-        ).astype(jnp.float32),
-        lax.psum_scatter(
-            proj_grad.astype(jnp.bfloat16), "dp", scatter_dimension=1, tiled=True
-        ).astype(jnp.float32),
-        lax.psum_scatter(
-            ada_bias_term.astype(jnp.bfloat16), "dp", scatter_dimension=0, tiled=True
-        ).astype(jnp.float32),
-        lax.psum_scatter(
-            attn_bias_term.astype(jnp.bfloat16), "dp", scatter_dimension=0, tiled=True
-        ).astype(jnp.float32),
-        lax.psum_scatter(
-            out_bias_term.astype(jnp.bfloat16), "dp", scatter_dimension=0, tiled=True
-        ).astype(jnp.float32),
-    )
-    (
-        ada_weight_grad,
-        attn_weight_grad,
-        proj_weight_grad,
-        ada_bias_grad,
-        attn_bias_grad,
-        out_bias_grad,
-    ) = (
-        lax.psum_scatter(shares[0], "fsdp", scatter_dimension=0, tiled=True),
-        lax.psum_scatter(shares[1], "fsdp", scatter_dimension=0, tiled=True),
-        lax.psum_scatter(shares[2], "fsdp", scatter_dimension=0, tiled=True),
-        lax.psum_scatter(shares[3], "fsdp", scatter_dimension=0, tiled=True),
-        lax.psum_scatter(shares[4], "fsdp", scatter_dimension=0, tiled=True),
-        lax.psum_scatter(shares[5], "fsdp", scatter_dimension=0, tiled=True),
+    devices = planes * lax.axis_size("fsdp")
+    terms = (attn_bias_term, out_bias_term, up_bias_term)
+    shared = jnp.concatenate([term.reshape(devices, -1) for term in terms], axis=1)
+    shared = lax.psum_scatter(shared, AXES, scatter_dimension=0, tiled=True)[0]
+    attn_bias_grad, out_bias_grad, up_bias_grad = jnp.split(
+        shared, [attn_bias.shape[0], attn_bias.shape[0] + out_bias.shape[0]]
     )
     return (
         mixed,

time: 1400 us -> 1970 us (1.41)
  Pallas kernels: 0 us -> 969 us
  waiting for transfers between devices: 894 us -> 295 us
  starting transfers between devices: 0.73 us -> 90.5 us
  local copies, waits for them, and re-layouts: 96 us -> 149 us
  other arithmetic: 57.1 us -> 103 us
  blocking collectives: 114 us -> 148 us
    pallas_call x0 -> x3, Pallas kernels: none -> 969 us  [assemble(): pl.pallas_call(partial(lay_out, plane_major), out_shape=jax.ShapeDtypeStr...]
    all_gather x8 -> x0, waiting for transfers between devices: 355 us -> none  [the longest x1 81.2 us: per_device(): lax.all_gather(gathered[0], 'fsdp', axis=0, tiled=True)]
    unnamed x23 -> x4, waiting for transfers between devices: 292 us -> 21.9 us
    ppermute x0 -> x104, waiting for transfers between devices: none -> 260 us  [swap(): lax.ppermute(values, AXES, [(index, neighbour(index, axis)) for index in...]
    reduce_scatter x5 -> x0, waiting for transfers between devices: 247 us -> none  [the longest x1 144 us: per_device(): lax.psum_scatter(ada_grad.astype(jnp.bfloat16), 'dp', scatter_dimension=1...]
    ppermute x0 -> x104, starting transfers between devices: none -> 78.1 us  [swap(): lax.ppermute(values, AXES, [(index, neighbour(index, axis)) for index in...]
    all_gather x2, blocking collectives: 29.3 us -> 71 us  [the longest x1 55.6 us: modulate_slots(): everyone = lax.all_gather(silu_bf, AXES, axis=0, tiled=True)]
    slice x5 -> x28, local copies, waits for them, and re-layouts: 3.99 us -> 40 us  [the longest x8 13 us: halves(): return [[term[:2] for term in terms], [term[2:] for term in terms]]]
  transfers between devices with their start and end apart: 18 -> 109, of which waited for: 14 -> 35; matrix products, arithmetic and copies ran while one was open for 25% -> 21% of each run, Pallas kernels for 0% -> 49%
where the time goes in v1:
time: 1970 us
  Pallas kernels  969 us (49%)
  waiting for transfers between devices  295 us (15%)
  matrix products  196 us (10%)
  local copies, waits for them, and re-layouts  149 us (8%)
  blocking collectives  148 us (8%)
  other arithmetic  103 us (5%)
  starting transfers between devices  90.5 us (5%)
    pallas_call x3, Pallas kernels, assemble(): pl.pallas_call(partial(lay_out, plane_major), out_shape=jax.ShapeDtypeStr...  969 us
    ppermute x104, waiting for transfers between devices, swap(): lax.ppermute(values, AXES, [(index, neighbour(index, axis)) for index in...  260 us
    ppermute x104, starting transfers between devices, swap(): lax.ppermute(values, AXES, [(index, neighbour(index, axis)) for index in...  78.1 us
    unnamed x2, blocking collectives  76.5 us
    dot_general x33, matrix products, matmul_tn(): lax.dot_general(first_matrix, second_matrix, (((0,), (0,)), ((), ())), pr...  58.5 us
    all_gather x1, blocking collectives, modulate_slots(): everyone = lax.all_gather(silu_bf, AXES, axis=0, tiled=True)  55.6 us
    dot_general x14, matrix products, matmul_nt(): lax.dot_general(first_matrix, second_matrix, (((1,), (1,)), ((), ())), pr...  53.2 us
    unnamed x427, local copies, waits for them, and re-layouts  52 us
  transfers between devices with their start and end apart: 109, of which 35 were waited for; matrix products, arithmetic and copies ran while one was open for 21% of the time, Pallas kernels for 49%

profile of v1, /device:TPU:0, one launch (start us, length us, event | category | flops | bytes accessed | tf_op | source)
XLA Modules:
  0.0 1966.5 jit_solution(10812277109089027803)
XLA Ops:
  18.7 55.6 %all-gather.2 = bf16[32,4,1152]{2,1,0:T(4,128)(2,1)S(1)} all-gather(bf16[1,4,1152]{2,1,0:T(4,128)(2,1)S(1)} %fusion.238), channel_id=1, replica_groups=mesh['dp'=4,'fsdp'=8] {'dp','fsdp'}, dimensions={0}, use_global_device_ids=true | all-gather | bytes 304128 | tf_op jit(solution)/shard_map/all_gather | solution.py:372
  76.5 37.9 %all-reduce = bf16[16128]{0:T(1024)(128)(2,1)S(1)} all-reduce(bf16[16128]{0:T(1024)(128)(2,1)S(1)} %dynamic-update-slice), channel_id=2, replica_groups=mesh['dp'=4,'fsdp'=8] {'dp','fsdp'}, use_global_device_ids=true, to_apply=%add | all-reduce | flops 16128 | bytes 64512
  168.3 10.0 all-to-all-done
  210.1 16.8 collective-permute-done.36
  227.3 10.9 collective-permute-done.37
  241.9 14.2 collective-permute-done.3.refs_1_
  258.2 9.5 collective-permute-done.8.refs_7_
  275.2 322.9 %shard_map.238 = bf16[4,4,2,144,1152]{4,3,2,1,0:T(8,128)(2,1)} custom-call(bf16[2,144,1152]{2,1,0:T(8,128)(2,1)} %get-tuple-element.142.refs_0_, bf16[2,144,1152]{2,1,0:T(8,128)(2,1)} %copy-done.113, bf16[2,144,1152]{2,1,0:T(8,128)(2,1)} %copy-done.116, bf16[2,144,1152]{2,1,0:T(8,128)(2,1)} %copy-done.122, bf16[2,144,1152]{2,1,0:T(8,128)(2,1)} %get-tuple-element.141.refs_4_, ...), custom_call_target="tpu_custom_call" | custom-call | bytes 21233664 | tf_op jit(solution)/shard_map/pallas_call | solution.py:211
  630.6 8.2 fusion
  673.7 12.1 collective-permute-done.22.refs_3_
  699.6 322.9 %shard_map.239 = bf16[4,4,2,144,1152]{4,3,2,1,0:T(8,128)(2,1)} custom-call(bf16[2,144,1152]{2,1,0:T(8,128)(2,1)} %get-tuple-element.138.refs_0_, bf16[2,144,1152]{2,1,0:T(8,128)(2,1)} %collective-permute-done.20.refs_1_, bf16[2,144,1152]{2,1,0:T(8,128)(2,1)} %collective-permute-done.21.refs_2_, bf16[2,144,1152]{2,1,0:T(8,128)(2,1)} %collective-permute-done.22.refs_3_, ...), custom_call_target="tpu_custom_call" | custom-call | bytes 21233664 | tf_op jit(solution)/shard_map/pallas_call | solution.py:211
  1061.8 11.7 collective-permute-done.39.refs_2_
  1074.8 12.2 collective-permute-done.40.refs_3_
  1092.5 322.9 %shard_map.240 = bf16[4,4,2,144,1152]{4,3,2,1,0:T(8,128)(2,1)} custom-call(bf16[2,144,1152]{2,1,0:T(8,128)(2,1)} %get-tuple-element.140.refs_0_, bf16[2,144,1152]{2,1,0:T(8,128)(2,1)} %collective-permute-done.38.refs_1_, bf16[2,144,1152]{2,1,0:T(8,128)(2,1)} %copy-done.115, bf16[2,144,1152]{2,1,0:T(8,128)(2,1)} %copy-done.121, ...), custom_call_target="tpu_custom_call" | custom-call | bytes 21233664 | tf_op jit(solution)/shard_map/pallas_call | solution.py:211
  1457.5 10.7 fusion.256
  1512.1 9.1 convert_reduce_fusion.3
  1521.2 11.1 multiply_reduce_fusion
  1532.3 11.7 multiply_convert_fusion
  1587.7 38.6 %all-reduce.3 = f32[32,288]{1,0:T(8,128)S(1)} all-reduce(f32[32,288]{1,0:T(8,128)S(1)} %pad_maximum_fusion.22), channel_id=6, replica_groups=mesh['dp'=4,'fsdp'=8] {'dp','fsdp'}, use_global_device_ids=true, to_apply=%region_20.21.clone | all-reduce | flops 9216 | bytes 73728
  1676.4 15.4 all-gather.1
  1696.4 21.9 %reduce-scatter.5.cloned.1.call-done = f32[1,8,4,144]{3,1,2,0:T(8,128)} async-done(((f32[4,8,4,144]{3,1,2,0:T(8,128)}), f32[1,8,4,144]{3,1,2,0:T(8,128)}) %reduce-scatter.5.cloned.1.call-update) | async-done | bytes 18448
  1746.8 14.5 collective-permute-done.98
  1765.4 12.3 collective-permute-done.74
  1784.6 8.5 collective-permute-done.57
  1800.2 13.4 collective-permute-done.95
  1830.5 11.4 collective-permute-done.61
  1842.0 8.3 collective-permute-done.65
  1862.4 19.9 %collective-permute-done.101 = bf16[144,1152]{1,0:T(8,128)(2,1)S(1)} collective-permute-done((bf16[144,1152]{1,0:T(8,128)(2,1)S(1)}, bf16[144,1152]{1,0:T(8,128)(2,1)S(1)}, u32[]{:S(2)}, u32[]{:S(2)}) %collective-permute-start.101) | collective-permute-done | bytes 331808 | tf_op jit(solution)/shard_map/ppermute | solution.py:149
  1891.2 9.3 collective-permute-done.71
  1904.9 8.4 collective-permute-done.82
  1923.2 19.4 collective-permute-done.67
  1945.4 12.9 collective-permute-done.84
  (859 shorter events, 525.2 us)
Async XLA Ops:
  7.2 153.9 %all-reduce.6.cloned.1.call-start = ((), (), s32[]{:S(2)}) async-start(), calls=%async_computation.4 | async-start | bytes 1835008
  9.2 129.7 %collective-permute-start.2 = (bf16[144,1152]{1,0:T(8,128)(2,1)}, bf16[144,1152]{1,0:T(8,128)(2,1)}, u32[]{:S(2)}, u32[]{:S(2)}) collective-permute-start(bf16[144,1152]{1,0:T(8,128)(2,1)} %get-tuple-element.80), channel_id=1, source_target_pairs={{0,2},{1,3},{2,4},{3,5},{4,6},{5,7},{6,0},{7,1},{8,10},{9,11},{10,... | collective-permute-start | bytes 995336 | tf_op jit(solution)/shard_map/ppermute | solution.py:149
  12.3 126.6 %collective-permute-start.1 = (bf16[144,1152]{1,0:T(8,128)(2,1)}, bf16[144,1152]{1,0:T(8,128)(2,1)}, u32[]{:S(2)}, u32[]{:S(2)}) collective-permute-start(bf16[144,1152]{1,0:T(8,128)(2,1)} %get-tuple-element.80), channel_id=1, source_target_pairs={{0,4},{1,5},{2,6},{3,7},{4,0},{5,1},{6,2},{7,3},{8,12},{9,13},{10,... | collective-permute-start | bytes 995336 | tf_op jit(solution)/shard_map/ppermute | solution.py:149
  14.9 124.1 %collective-permute-start = (bf16[144,1152]{1,0:T(8,128)(2,1)}, bf16[144,1152]{1,0:T(8,128)(2,1)}, u32[]{:S(2)}, u32[]{:S(2)}) collective-permute-start(bf16[144,1152]{1,0:T(8,128)(2,1)} %get-tuple-element.80), channel_id=1, source_target_pairs={{0,6},{1,7},{2,0},{3,1},{4,2},{5,3},{6,4},{7,5},{8,14},{9,15},{10,... | collective-permute-start | bytes 995336 | tf_op jit(solution)/shard_map/ppermute | solution.py:149
  18.0 118.8 %collective-permute-start.34 = (bf16[144,576]{1,0:T(8,128)(2,1)}, bf16[144,576]{1,0:T(8,128)(2,1)S(1)}, u32[]{:S(2)}, u32[]{:S(2)}) collective-permute-start(bf16[144,576]{1,0:T(8,128)(2,1)} %get-tuple-element.186), channel_id=1, source_target_pairs={{0,1},{1,0},{2,3},{3,2},{4,5},{5,4},{6,7},{7,6},{8,9},{9,8},{10,11... | collective-permute-start | bytes 497672 | tf_op jit(solution)/shard_map/ppermute | solution.py:149
  138.9 58.6 %collective-permute-start.19 = (bf16[144,1152]{1,0:T(8,128)(2,1)S(1)}, bf16[144,1152]{1,0:T(8,128)(2,1)}, u32[]{:S(2)}, u32[]{:S(2)}) collective-permute-start(bf16[144,1152]{1,0:T(8,128)(2,1)S(1)} %copy-done.98), channel_id=1, source_target_pairs={{0,2},{1,3},{2,4},{3,5},{4,6},{5,7},{6,0},{7,1},{8,10},{9,11},{10,... | collective-permute-start | bytes 995336 | tf_op jit(solution)/shard_map/ppermute | solution.py:149
  141.3 58.0 %collective-permute-start.18 = (bf16[144,1152]{1,0:T(8,128)(2,1)S(1)}, bf16[144,1152]{1,0:T(8,128)(2,1)}, u32[]{:S(2)}, u32[]{:S(2)}) collective-permute-start(bf16[144,1152]{1,0:T(8,128)(2,1)S(1)} %copy-done.98), channel_id=1, source_target_pairs={{0,4},{1,5},{2,6},{3,7},{4,0},{5,1},{6,2},{7,3},{8,12},{9,13},{10,... | collective-permute-start | bytes 995336 | tf_op jit(solution)/shard_map/ppermute | solution.py:149
  141.4 57.9 %collective-permute-start.17 = (bf16[144,1152]{1,0:T(8,128)(2,1)S(1)}, bf16[144,1152]{1,0:T(8,128)(2,1)}, u32[]{:S(2)}, u32[]{:S(2)}) collective-permute-start(bf16[144,1152]{1,0:T(8,128)(2,1)S(1)} %copy-done.98), channel_id=1, source_target_pairs={{0,6},{1,7},{2,0},{3,1},{4,2},{5,3},{6,4},{7,5},{8,14},{9,15},{10,... | collective-permute-start | bytes 995336 | tf_op jit(solution)/shard_map/ppermute | solution.py:149
  158.8 79.7 %collective-permute-start.13 = (bf16[2,144,1152]{2,1,0:T(8,128)(2,1)}, bf16[2,144,1152]{2,1,0:T(8,128)(2,1)}, u32[]{:S(2)}, u32[]{:S(2)}) collective-permute-start(bf16[2,144,1152]{2,1,0:T(8,128)(2,1)} %get-tuple-element.141.refs_4_), channel_id=1, source_target_pairs={{0,1},{1,0},{2,3},{3,2},{4,5},{5,4},{6,7},{7,6},{8,9},{9,8},{10,11... | collective-permute-start | bytes 1990664 | tf_op jit(solution)/shard_map/ppermute | solution.py:149
  158.8 81.6 %collective-permute-start.7 = (bf16[2,144,1152]{2,1,0:T(8,128)(2,1)}, bf16[2,144,1152]{2,1,0:T(8,128)(2,1)}, u32[]{:S(2)}, u32[]{:S(2)}) collective-permute-start(bf16[2,144,1152]{2,1,0:T(8,128)(2,1)} %get-tuple-element.141.refs_4_), channel_id=1, source_target_pairs={{0,16},{1,17},{2,18},{3,19},{4,20},{5,21},{6,22},{7,23},{8,24},{9,... | collective-permute-start | bytes 1990664 | tf_op jit(solution)/shard_map/ppermute | solution.py:149
  199.3 58.3 %collective-permute-start.9 = (bf16[2,144,1152]{2,1,0:T(8,128)(2,1)S(1)}, bf16[2,144,1152]{2,1,0:T(8,128)(2,1)S(1)}, u32[]{:S(2)}, u32[]{:S(2)}) collective-permute-start(bf16[2,144,1152]{2,1,0:T(8,128)(2,1)S(1)} %copy-done.66), channel_id=1, source_target_pairs={{0,1},{1,0},{2,3},{3,2},{4,5},{5,4},{6,7},{7,6},{8,9},{9,8},{10,11... | collective-permute-start | bytes 1990664 | tf_op jit(solution)/shard_map/ppermute | solution.py:149
  269.6 385.3 %collective-permute-start.30 = (bf16[2,144,1152]{2,1,0:T(8,128)(2,1)}, bf16[2,144,1152]{2,1,0:T(8,128)(2,1)}, u32[]{:S(2)}, u32[]{:S(2)}) collective-permute-start(bf16[2,144,1152]{2,1,0:T(8,128)(2,1)} %get-tuple-element.137.refs_4_), channel_id=1, source_target_pairs={{0,1},{1,0},{2,3},{3,2},{4,5},{5,4},{6,7},{7,6},{8,9},{9,8},{10,11... | collective-permute-start | bytes 1990664 | tf_op jit(solution)/shard_map/ppermute | solution.py:149
  269.8 385.4 %collective-permute-start.24 = (bf16[2,144,1152]{2,1,0:T(8,128)(2,1)}, bf16[2,144,1152]{2,1,0:T(8,128)(2,1)}, u32[]{:S(2)}, u32[]{:S(2)}) collective-permute-start(bf16[2,144,1152]{2,1,0:T(8,128)(2,1)} %get-tuple-element.137.refs_4_), channel_id=1, source_target_pairs={{0,16},{1,17},{2,18},{3,19},{4,20},{5,21},{6,22},{7,23},{8,24},{9,... | collective-permute-start | bytes 1990664 | tf_op jit(solution)/shard_map/ppermute | solution.py:149
  271.5 383.7 %collective-permute-start.23 = (bf16[2,144,1152]{2,1,0:T(8,128)(2,1)}, bf16[2,144,1152]{2,1,0:T(8,128)(2,1)}, u32[]{:S(2)}, u32[]{:S(2)}) collective-permute-start(bf16[2,144,1152]{2,1,0:T(8,128)(2,1)} %get-tuple-element.137.refs_4_), channel_id=1, source_target_pairs={{0,8},{1,9},{2,10},{3,11},{4,12},{5,13},{6,14},{7,15},{8,0},{9,1},... | collective-permute-start | bytes 1990664 | tf_op jit(solution)/shard_map/ppermute | solution.py:149
  273.0 393.9 %collective-permute-start.26 = (bf16[2,144,1152]{2,1,0:T(8,128)(2,1)}, bf16[2,144,1152]{2,1,0:T(8,128)(2,1)}, u32[]{:S(2)}, u32[]{:S(2)}) collective-permute-start(bf16[2,144,1152]{2,1,0:T(8,128)(2,1)} %get-tuple-element.138.refs_0_), channel_id=1, source_target_pairs={{0,1},{1,0},{2,3},{3,2},{4,5},{5,4},{6,7},{7,6},{8,9},{9,8},{10,11... | collective-permute-start | bytes 1990664 | tf_op jit(solution)/shard_map/ppermute | solution.py:149
  274.6 382.3 %collective-permute-start.20 = (bf16[2,144,1152]{2,1,0:T(8,128)(2,1)}, bf16[2,144,1152]{2,1,0:T(8,128)(2,1)}, u32[]{:S(2)}, u32[]{:S(2)}) collective-permute-start(bf16[2,144,1152]{2,1,0:T(8,128)(2,1)} %get-tuple-element.138.refs_0_), channel_id=1, source_target_pairs={{0,8},{1,9},{2,10},{3,11},{4,12},{5,13},{6,14},{7,15},{8,0},{9,1},... | collective-permute-start | bytes 1990664 | tf_op jit(solution)/shard_map/ppermute | solution.py:149
  696.6 358.9 %collective-permute-start.48 = (bf16[2,144,1152]{2,1,0:T(8,128)(2,1)}, bf16[2,144,1152]{2,1,0:T(8,128)(2,1)}, u32[]{:S(2)}, u32[]{:S(2)}) collective-permute-start(bf16[2,144,1152]{2,1,0:T(8,128)(2,1)} %get-tuple-element.139.refs_4_), channel_id=1, source_target_pairs={{0,1},{1,0},{2,3},{3,2},{4,5},{5,4},{6,7},{7,6},{8,9},{9,8},{10,11... | collective-permute-start | bytes 1990664 | tf_op jit(solution)/shard_map/ppermute | solution.py:149
  697.2 360.0 %collective-permute-start.42 = (bf16[2,144,1152]{2,1,0:T(8,128)(2,1)}, bf16[2,144,1152]{2,1,0:T(8,128)(2,1)}, u32[]{:S(2)}, u32[]{:S(2)}) collective-permute-start(bf16[2,144,1152]{2,1,0:T(8,128)(2,1)} %get-tuple-element.139.refs_4_), channel_id=1, source_target_pairs={{0,16},{1,17},{2,18},{3,19},{4,20},{5,21},{6,22},{7,23},{8,24},{9,... | collective-permute-start | bytes 1990664 | tf_op jit(solution)/shard_map/ppermute | solution.py:149
  697.5 359.7 %collective-permute-start.41 = (bf16[2,144,1152]{2,1,0:T(8,128)(2,1)}, bf16[2,144,1152]{2,1,0:T(8,128)(2,1)}, u32[]{:S(2)}, u32[]{:S(2)}) collective-permute-start(bf16[2,144,1152]{2,1,0:T(8,128)(2,1)} %get-tuple-element.139.refs_4_), channel_id=1, source_target_pairs={{0,8},{1,9},{2,10},{3,11},{4,12},{5,13},{6,14},{7,15},{8,0},{9,1},... | collective-permute-start | bytes 1990664 | tf_op jit(solution)/shard_map/ppermute | solution.py:149
  699.2 362.6 %collective-permute-start.44 = (bf16[2,144,1152]{2,1,0:T(8,128)(2,1)}, bf16[2,144,1152]{2,1,0:T(8,128)(2,1)}, u32[]{:S(2)}, u32[]{:S(2)}) collective-permute-start(bf16[2,144,1152]{2,1,0:T(8,128)(2,1)} %get-tuple-element.140.refs_0_), channel_id=1, source_target_pairs={{0,1},{1,0},{2,3},{3,2},{4,5},{5,4},{6,7},{7,6},{8,9},{9,8},{10,11... | collective-permute-start | bytes 1990664 | tf_op jit(solution)/shard_map/ppermute | solution.py:149
  699.2 359.6 %collective-permute-start.38 = (bf16[2,144,1152]{2,1,0:T(8,128)(2,1)}, bf16[2,144,1152]{2,1,0:T(8,128)(2,1)}, u32[]{:S(2)}, u32[]{:S(2)}) collective-permute-start(bf16[2,144,1152]{2,1,0:T(8,128)(2,1)} %get-tuple-element.140.refs_0_), channel_id=1, source_target_pairs={{0,8},{1,9},{2,10},{3,11},{4,12},{5,13},{6,14},{7,15},{8,0},{9,1},... | collective-permute-start | bytes 1990664 | tf_op jit(solution)/shard_map/ppermute | solution.py:149
  1089.5 641.3 %collective-permute-start.94 = (bf16[2,144,1152]{2,1,0:T(8,128)(2,1)}, bf16[2,144,1152]{2,1,0:T(8,128)(2,1)}, u32[]{:S(2)}, u32[]{:S(2)}) collective-permute-start(bf16[2,144,1152]{2,1,0:T(8,128)(2,1)} %pad_maximum_fusion.18), channel_id=1, source_target_pairs={{0,1},{1,0},{2,3},{3,2},{4,5},{5,4},{6,7},{7,6},{8,9},{9,8},{10,11... | collective-permute-start | bytes 1990664 | tf_op jit(solution)/shard_map/ppermute | solution.py:149
  1090.1 656.5 %collective-permute-start.96 = (bf16[2,144,1152]{2,1,0:T(8,128)(2,1)}, bf16[2,144,1152]{2,1,0:T(8,128)(2,1)}, u32[]{:S(2)}, u32[]{:S(2)}) collective-permute-start(bf16[2,144,1152]{2,1,0:T(8,128)(2,1)} %pad_maximum_fusion.19), channel_id=1, source_target_pairs={{0,1},{1,0},{2,3},{3,2},{4,5},{5,4},{6,7},{7,6},{8,9},{9,8},{10,11... | collective-permute-start | bytes 1990664 | tf_op jit(solution)/shard_map/ppermute | solution.py:149
  1090.2 642.4 %collective-permute-start.97 = (bf16[2,144,1152]{2,1,0:T(8,128)(2,1)}, bf16[2,144,1152]{2,1,0:T(8,128)(2,1)}, u32[]{:S(2)}, u32[]{:S(2)}) collective-permute-start(bf16[2,144,1152]{2,1,0:T(8,128)(2,1)} %pad_maximum_fusion.20), channel_id=1, source_target_pairs={{0,1},{1,0},{2,3},{3,2},{4,5},{5,4},{6,7},{7,6},{8,9},{9,8},{10,11... | collective-permute-start | bytes 1990664 | tf_op jit(solution)/shard_map/ppermute | solution.py:149
  1090.6 704.2 %collective-permute-start.93 = (bf16[2,144,1152]{2,1,0:T(8,128)(2,1)}, bf16[2,144,1152]{2,1,0:T(8,128)(2,1)}, u32[]{:S(2)}, u32[]{:S(2)}) collective-permute-start(bf16[2,144,1152]{2,1,0:T(8,128)(2,1)} %pad_maximum_fusion.17), channel_id=1, source_target_pairs={{0,1},{1,0},{2,3},{3,2},{4,5},{5,4},{6,7},{7,6},{8,9},{9,8},{10,11... | collective-permute-start | bytes 1990664 | tf_op jit(solution)/shard_map/ppermute | solution.py:149
  1092.3 642.3 %collective-permute-start.87 = (bf16[2,144,1152]{2,1,0:T(8,128)(2,1)}, bf16[2,144,1152]{2,1,0:T(8,128)(2,1)}, u32[]{:S(2)}, u32[]{:S(2)}) collective-permute-start(bf16[2,144,1152]{2,1,0:T(8,128)(2,1)} %pad_maximum_fusion.14), channel_id=1, source_target_pairs={{0,1},{1,0},{2,3},{3,2},{4,5},{5,4},{6,7},{7,6},{8,9},{9,8},{10,11... | collective-permute-start | bytes 1990664 | tf_op jit(solution)/shard_map/ppermute | solution.py:149
  1659.4 58.9 %reduce-scatter.5.cloned.1.call-start = ((), (), s32[]{:S(2)}) async-start(), calls=%async_computation.5 | async-start | bytes 163840
  1842.0 46.2 %collective-permute-start.69 = (bf16[2,144,1152]{2,1,0:T(8,128)(2,1)}, bf16[2,144,1152]{2,1,0:T(8,128)(2,1)}, u32[]{:S(2)}, u32[]{:S(2)}) collective-permute-start(bf16[2,144,1152]{2,1,0:T(8,128)(2,1)} %bitcast.109), channel_id=1, source_target_pairs={{0,1},{1,0},{2,3},{3,2},{4,5},{5,4},{6,7},{7,6},{8,9},{9,8},{10,11... | collective-permute-start | bytes 1990664 | tf_op jit(solution)/shard_map/ppermute | solution.py:149
  1850.3 51.9 %collective-permute-start.76 = (bf16[2,144,1152]{2,1,0:T(8,128)(2,1)}, bf16[2,144,1152]{2,1,0:T(8,128)(2,1)}, u32[]{:S(2)}, u32[]{:S(2)}) collective-permute-start(bf16[2,144,1152]{2,1,0:T(8,128)(2,1)} %bitcast.120), channel_id=1, source_target_pairs={{0,1},{1,0},{2,3},{3,2},{4,5},{5,4},{6,7},{7,6},{8,9},{9,8},{10,11... | collective-permute-start | bytes 1990664 | tf_op jit(solution)/shard_map/ppermute | solution.py:149
  1860.9 43.7 %collective-permute-start.78 = (bf16[2,144,1152]{2,1,0:T(8,128)(2,1)}, bf16[2,144,1152]{2,1,0:T(8,128)(2,1)}, u32[]{:S(2)}, u32[]{:S(2)}) collective-permute-start(bf16[2,144,1152]{2,1,0:T(8,128)(2,1)} %add_convert_fusion.3), channel_id=1, source_target_pairs={{0,16},{1,17},{2,18},{3,19},{4,20},{5,21},{6,22},{7,23},{8,24},{9,... | collective-permute-start | bytes 1990664 | tf_op jit(solution)/shard_map/ppermute | solution.py:149
  1900.4 44.0 %collective-permute-start.103 = (f32[144,576]{1,0:T(8,128)S(1)}, f32[144,576]{1,0:T(8,128)S(1)}, u32[]{:S(2)}, u32[]{:S(2)}) collective-permute-start(f32[144,576]{1,0:T(8,128)S(1)} %bitcast.578), channel_id=1, source_target_pairs={{0,1},{1,0},{2,3},{3,2},{4,5},{5,4},{6,7},{7,6},{8,9},{9,8},{10,11... | collective-permute-start | bytes 995336 | tf_op jit(solution)/shard_map/ppermute | solution.py:149
  1915.3 43.0 %collective-permute-start.84 = (bf16[144,1152]{1,0:T(8,128)(2,1)S(1)}, bf16[144,1152]{1,0:T(8,128)(2,1)S(1)}, u32[]{:S(2)}, u32[]{:S(2)}) collective-permute-start(bf16[144,1152]{1,0:T(8,128)(2,1)S(1)} %get-tuple-element.124), channel_id=1, source_target_pairs={{0,4},{1,5},{2,6},{3,7},{4,0},{5,1},{6,2},{7,3},{8,12},{9,13},{10,... | collective-permute-start | bytes 995336 | tf_op jit(solution)/shard_map/ppermute | solution.py:149
  (276 other events, 3338.1 us)
Sparse Core Ops, SparseCore 0:
  76.2 55.5 all-reduce.5
  1694.1 24.1 reduce-scatter.4

commit v2 on v1

--- a/solution.py
+++ b/solution.py
@@ -187,21 +187,41 @@
 
 
 def lay_out(plane_major, *refs):
-    pieces, out, sems = refs[:16], refs[16], refs[17]
+    pieces, out, room, arrive, leave = refs[:16], refs[16], refs[17], refs[18], refs[19]
     plane, _, core = place()
-    copies = []
-    for flip_core in range(2):
-        for half in range(2):
-            for flip in range(4):
-                at = flipped(plane, flip)
-                side = core if flip_core == 0 else 1 - core
-                rows = pl.ds(2 * half, 2)
-                target = out.at[at, rows, side] if plane_major else out.at[rows, at, side]
-                count = len(copies)
-                copies.append(pltpu.make_async_copy(pieces[count], target, sems.at[count]))
-    for copy in copies:
-        copy.start()
-    for copy in copies:
+    sides = (core, 1 - core)
+
+    def fill(block):
+        slot = block % 2
+        copies = []
+        for flip_core in range(2):
+            for step in range(2 if plane_major else 4):
+                if plane_major:
+                    source = pieces[flip_core * 8 + step * 4 + block]
+                    target = room.at[slot, pl.ds(2 * step, 2), sides[flip_core]]
+                else:
+                    source = pieces[flip_core * 8 + block // 2 * 4 + step].at[block % 2]
+                    target = room.at[slot, flipped(plane, step), sides[flip_core]]
+                copies.append(
+                    pltpu.make_async_copy(source, target, arrive.at[slot, len(copies)])
+                )
+        for copy in copies:
+            copy.start()
+        return copies
+
+    filling, draining = [fill(0), None], [None, None]
+    for block in range(4):
+        slot = block % 2
+        if block < 3:
+            if draining[1 - slot] is not None:
+                draining[1 - slot].wait()
+            filling[1 - slot] = fill(block + 1)
+        for copy in filling[slot]:
+            copy.wait()
+        at = flipped(plane, block) if plane_major else block
+        draining[slot] = pltpu.make_async_copy(room.at[slot], out.at[at], leave.at[slot])
+        draining[slot].start()
+    for copy in draining:
         copy.wait()
 
 
@@ -213,7 +233,12 @@
         out_shape=jax.ShapeDtypeStruct((4, 4, 2, rows, columns), flat[0].dtype),
         in_specs=[pl.BlockSpec(memory_space=pl.ANY)] * 16,
         out_specs=pl.BlockSpec(memory_space=pl.ANY),
-        scratch_shapes=[pltpu.SemaphoreType.DMA((16,))],
+        scratch_shapes=[
+            pltpu.VMEM((2, 4, 2, rows, columns), flat[0].dtype),
+            pltpu.SemaphoreType.DMA((2, 8)),
+            pltpu.SemaphoreType.DMA((2,)),
+        ],
+        compiler_params=pltpu.CompilerParams(vmem_limit_bytes=16 * 2**20),
         cost_estimate=pl.CostEstimate(
             flops=0, bytes_accessed=2 * 32 * rows * columns * 2, transcendentals=0
         ),
@@ -365,38 +390,135 @@
     return results
 
 
-def modulate_slots(silu_bf, ada_weight, ada_bias):
+def trade(one_for_all, values, out, send_sems, recv_sems):
     planes, lines = lax.axis_size("dp"), lax.axis_size("fsdp")
-    slots = silu_bf.shape[0]
+    count = planes * lines
+    me = lax.axis_index("dp") * lines + lax.axis_index("fsdp")
+
+    def device(index):
+        return (index // lines, index % lines)
+
+    def chunk(index):
+        return values if one_for_all else values.at[index]
+
+    barrier = pltpu.get_barrier_semaphore()
+
+    @pl.loop(1, count)
+    def _(step):
+        pl.semaphore_signal(
+            barrier,
+            inc=1,
+            device_id=device((me + step) % count),
+            device_id_type=pl.DeviceIdType.MESH,
+        )
+
+    pl.semaphore_wait(barrier, count - 1)
+
+    @pl.loop(1, count)
+    def _(step):
+        peer = (me + step) % count
+        pltpu.make_async_remote_copy(
+            src_ref=chunk(peer),
+            dst_ref=out.at[me],
+            send_sem=send_sems.at[step],
+            recv_sem=recv_sems.at[step],
+            device_id=device(peer),
+            device_id_type=pl.DeviceIdType.MESH,
+        ).start()
+
+    if one_for_all:
+        out[me] = values[...]
+    else:
+        out[me] = values[me]
+
+    @pl.loop(1, count)
+    def _(step):
+        peer = (me + step) % count
+        copy = pltpu.make_async_remote_copy(
+            src_ref=chunk(peer),
+            dst_ref=out.at[(me + count - step) % count],
+            send_sem=send_sems.at[step],
+            recv_sem=recv_sems.at[step],
+            device_id=device(peer),
+            device_id_type=pl.DeviceIdType.MESH,
+        )
+        copy.wait()
+
+
+def exchange(values, collective_id, one_for_all=False):
+    count = lax.axis_size("dp") * lax.axis_size("fsdp")
+    chunk = values.shape[-2:]
+    size = count * chunk[0] * chunk[1] * values.dtype.itemsize
+    return pl.pallas_call(
+        partial(trade, one_for_all),
+        out_shape=jax.ShapeDtypeStruct((count,) + chunk, values.dtype),
+        in_specs=[pl.BlockSpec(memory_space=pltpu.VMEM)],
+        out_specs=pl.BlockSpec(memory_space=pltpu.VMEM),
+        scratch_shapes=[pltpu.SemaphoreType.DMA((count,)), pltpu.SemaphoreType.DMA((count,))],
+        compiler_params=pltpu.CompilerParams(
+            collective_id=collective_id,
+            has_side_effects=True,
+            vmem_limit_bytes=3 * size + 4 * 2**20,
+        ),
+        cost_estimate=pl.CostEstimate(flops=0, bytes_accessed=8 * size, transcendentals=0),
+    )(values)
+
+
+def gather_small(silu_bf, vectors):
+    flat = jnp.concatenate([silu_bf.reshape(-1), *vectors])
+    width = -(-flat.shape[0] // 2048) * 128
+    flat = jnp.pad(flat, (0, 16 * width - flat.shape[0])).reshape(16, width)
+    everyone = exchange(flat, 0, one_for_all=True)
+    everyone = everyone.reshape(everyone.shape[0], -1)
+    begin = silu_bf.size
+    silu_all = everyone[:, :begin].reshape(-1, silu_bf.shape[1])
+    found = []
+    for vector in vectors:
+        found.append(everyone[:, begin : begin + vector.shape[0]].reshape(-1))
+        begin += vector.shape[0]
+    return silu_all, found
+
+
+def modulate_slots(silu_all, ada_weight, ada_bias):
+    planes, lines = lax.axis_size("dp"), lax.axis_size("fsdp")
     rows, columns = ada_weight.shape
-    everyone = lax.all_gather(silu_bf, AXES, axis=0, tiled=True)
-    silu_part = lax.dynamic_slice_in_dim(everyone, lax.axis_index("fsdp") * rows, rows, axis=1)
+    devices = planes * lines
+    slots = silu_all.shape[0] // devices
+    silu_part = lax.dynamic_slice_in_dim(silu_all, lax.axis_index("fsdp") * rows, rows, axis=1)
     term = jnp.dot(silu_part, ada_weight, preferred_element_type=jnp.float32)
-    term = lax.psum_scatter(
-        term.reshape(planes, lines, slots, columns), "fsdp", scatter_dimension=1, tiled=True
-    )
-    term = lax.all_to_all(term.reshape(planes, slots, columns), "dp", 0, 0, tiled=True)
+    term = exchange(term.reshape(devices, slots, columns), 1)
+    term = jnp.sum(term.reshape(planes, lines, slots, columns), axis=1)
     modulation = term.transpose(1, 0, 2).reshape(slots, planes * columns)
     return modulation + ada_bias.astype(jnp.float32), silu_part
 
 
-def modulation_back(modulation_grad, silu_part, ada_weight):
+def modulation_back(modulation_grad, silu_part, ada_weight, terms):
     planes, lines = lax.axis_size("dp"), lax.axis_size("fsdp")
+    devices = planes * lines
     slots = modulation_grad.shape[0]
     rows, columns = ada_weight.shape
     cut = modulation_grad.reshape(slots, planes, columns).transpose(1, 0, 2)
-    cut = lax.all_to_all(cut, "dp", 0, 0, tiled=True)
-    cut = lax.all_gather(cut, "fsdp", axis=1)
-    cut = cut.reshape(planes * lines * slots, columns)
+    cut = cut.reshape(planes, 1, 16, slots * columns // 16)
+    cut = jnp.broadcast_to(cut, (planes, lines) + cut.shape[2:])
+    cut = exchange(cut.reshape((devices,) + cut.shape[2:]), 2)
+    cut = cut.reshape(devices * slots, columns)
     ada_grad = matmul_tn(silu_part, cut)
     sums = jnp.sum(cut, axis=0, dtype=jnp.float32)
     bias_width = columns // lines
     ada_bias_grad = lax.dynamic_slice_in_dim(sums, lax.axis_index("fsdp") * bias_width, bias_width)
-    silu_grad = matmul_nt(cut, ada_weight).reshape(planes, lines, slots, rows)
-    silu_grad = lax.psum_scatter(silu_grad, "dp", scatter_dimension=0, tiled=True)
-    silu_grad = lax.all_to_all(silu_grad.reshape(lines, slots, rows), "fsdp", 0, 0, tiled=True)
+    silu_grad = matmul_nt(cut, ada_weight).reshape(devices, slots * rows)
+    flat = jnp.concatenate([silu_grad] + [term.reshape(devices, -1) for term in terms], axis=1)
+    width = -(-flat.shape[1] // 1024) * 128
+    flat = jnp.pad(flat, ((0, 0), (0, 8 * width - flat.shape[1])))
+    flat = exchange(flat.reshape(devices, 8, width), 3).reshape(devices, -1)
+    shared = jnp.sum(flat[:, slots * rows :], axis=0)
+    silu_grad = flat[:, : slots * rows].reshape(planes, lines, slots, rows).sum(axis=0)
     silu_grad = silu_grad.transpose(1, 0, 2).reshape(slots, lines * rows)
-    return ada_grad, ada_bias_grad, silu_grad
+    found, begin = [], 0
+    for term in terms:
+        found.append(shared[begin : begin + term.shape[0] // devices])
+        begin += term.shape[0] // devices
+    return ada_grad, ada_bias_grad, silu_grad, found
 
 
 def by_columns(values, parts):
@@ -426,13 +548,6 @@
     planes = lax.axis_size("dp")
     joined_w, up_w, down_w = gather_blocks(attn_weight, proj_weight, up_weight, down_weight)
     attn_columns = attn_weight.shape[1]
-    small = (ada_bias, attn_bias, out_bias, up_bias)
-    everyone = lax.all_gather(jnp.concatenate(small), AXES, axis=0)
-    biases, begin = [], 0
-    for vector in small:
-        biases.append(everyone[:, begin : begin + vector.shape[0]].reshape(-1))
-        begin += vector.shape[0]
-    ada_bfull, attn_bfull, out_bfull, up_bfull = biases
     slot_ids = jnp.arange(slot_count, dtype=jnp.int32)
     same_slot = segment[:, None] == slot_ids[None, :]
     slot_table = same_slot.astype(jnp.float32)
@@ -441,7 +556,10 @@
     condition_f = condition.astype(jnp.float32)
     silu_cond, silu_back = jax.vjp(jax.nn.silu, condition_f)
     silu_bf = silu_cond.astype(jnp.bfloat16)
-    modulation, silu_part = modulate_slots(silu_bf, ada_weight, ada_bfull)
+    silu_all, (ada_bfull, attn_bfull, out_bfull, up_bfull) = gather_small(
+        silu_bf, (ada_bias, attn_bias, out_bias, up_bias)
+    )
+    modulation, silu_part = modulate_slots(silu_all, ada_weight, ada_bfull)
     mod_rows = jnp.dot(
         slot_table, modulation, precision=lax.Precision.HIGHEST, preferred_element_type=jnp.float32
     )
@@ -540,21 +658,17 @@
         precision=lax.Precision.HIGHEST,
         preferred_element_type=jnp.float32,
     ).astype(jnp.bfloat16)
-    ada_weight_grad, ada_bias_grad, silu_grad = modulation_back(modulation_grad, silu_part, ada_weight)
-    condition_grad = silu_back(silu_grad)[0]
     out_bias_term = jnp.concatenate(
         [
             jnp.sum(grad_branch1, axis=0, dtype=jnp.float32),
             jnp.sum(grad_branch2, axis=0, dtype=jnp.float32),
         ]
     )
-    devices = planes * lax.axis_size("fsdp")
-    terms = (attn_bias_term, out_bias_term, up_bias_term)
-    shared = jnp.concatenate([term.reshape(devices, -1) for term in terms], axis=1)
-    shared = lax.psum_scatter(shared, AXES, scatter_dimension=0, tiled=True)[0]
-    attn_bias_grad, out_bias_grad, up_bias_grad = jnp.split(
-        shared, [attn_bias.shape[0], attn_bias.shape[0] + out_bias.shape[0]]
-    )
+    ada_weight_grad, ada_bias_grad, silu_grad, bias_grads = modulation_back(
+        modulation_grad, silu_part, ada_weight, (attn_bias_term, out_bias_term, up_bias_term)
+    )
+    attn_bias_grad, out_bias_grad, up_bias_grad = bias_grads
+    condition_grad = silu_back(silu_grad)[0]
     return (
         mixed,
         tokens_grad,

time: 1970 us -> 868 us (0.44)
  Pallas kernels: 969 us -> 95.4 us
  blocking collectives: 148 us -> 0 us
  local copies, waits for them, and re-layouts: 149 us -> 117 us
    pallas_call x3, Pallas kernels: 969 us -> 12.9 us  [assemble(): pl.pallas_call(partial(lay_out, plane_major), out_shape=jax.ShapeDtypeStr...]
    pallas_call x0 -> x4, Pallas kernels: none -> 82.5 us  [exchange(): pl.pallas_call(partial(trade, one_for_all), out_shape=jax.ShapeDtypeStruc...]
    unnamed x2 -> x0, blocking collectives: 76.5 us -> none
    all_gather x2 -> x0, blocking collectives: 71 us -> none  [the longest x1 55.6 us: modulate_slots(): everyone = lax.all_gather(silu_bf, AXES, axis=0, tiled=True)]
    unnamed x4 -> x0, waiting for transfers between devices: 21.9 us -> none
    unnamed x427 -> x324, local copies, waits for them, and re-layouts: 52 us -> 40.8 us
  transfers between devices with their start and end apart: 109 -> 104, of which waited for: 35 -> 33; matrix products, arithmetic and copies ran while one was open for 21% -> 44% of each run, Pallas kernels for 49% -> 11%
where the time goes in v2:
time: 868 us; the launch traced here: 857 us
  waiting for transfers between devices  277 us (32%)
  matrix products  188 us (22%)
  local copies, waits for them, and re-layouts  117 us (13%)
  other arithmetic  95.8 us (11%)
  Pallas kernels  95.4 us (11%)
  starting transfers between devices  79.9 us (9%)
    ppermute x104, waiting for transfers between devices, swap(): lax.ppermute(values, AXES, [(index, neighbour(index, axis)) for index in...  277 us
    pallas_call x4, Pallas kernels, exchange(): pl.pallas_call(partial(trade, one_for_all), out_shape=jax.ShapeDtypeStruc...  82.5 us
    ppermute x104, starting transfers between devices, swap(): lax.ppermute(values, AXES, [(index, neighbour(index, axis)) for index in...  79.9 us
    dot_general x33, matrix products, matmul_tn(): lax.dot_general(first_matrix, second_matrix, (((0,), (0,)), ((), ())), pr...  57.6 us
    dot_general x14, matrix products, matmul_nt(): lax.dot_general(first_matrix, second_matrix, (((1,), (1,)), ((), ())), pr...  43.1 us
    unnamed x324, local copies, waits for them, and re-layouts  40.8 us
  transfers between devices with their start and end apart: 104, of which 33 were waited for; matrix products, arithmetic and copies ran while one was open for 44% of the time, Pallas kernels for 11%

profile of v2, /device:TPU:0, one launch (start us, length us, event | category | flops | bytes accessed | tf_op | source)
XLA Modules:
  0.0 856.7 jit_solution(12745300044535122881)
XLA Ops:
  15.0 30.5 %shard_map.238 = bf16[32,16,384]{2,1,0:T(8,128)(2,1)S(1)} custom-call(bf16[16,384]{1,0:T(8,128)(2,1)S(1)} %reshape.616.values), custom_call_target="tpu_custom_call" | custom-call | bytes 3145728 | tf_op jit(solution)/shard_map/pallas_call | solution.py:452
  49.7 25.0 %shard_map.239 = f32[32,4,1728]{2,1,0:T(4,128)S(1)} custom-call(f32[32,4,1728]{2,1,0:T(4,128)S(1)} %reshape.619.values), custom_call_target="tpu_custom_call" | custom-call | bytes 7077888 | tf_op jit(solution)/shard_map/pallas_call | solution.py:452
  130.4 7.3 collective-permute-done.18
  137.7 8.0 collective-permute-start.35
  154.8 16.1 %collective-permute-done.36 = bf16[144,1152]{1,0:T(8,128)(2,1)S(1)} collective-permute-done((bf16[144,1152]{1,0:T(8,128)(2,1)S(1)}, bf16[144,1152]{1,0:T(8,128)(2,1)S(1)}, u32[]{:S(2)}, u32[]{:S(2)}) %collective-permute-start.36) | collective-permute-done | bytes 331808 | tf_op jit(solution)/shard_map/ppermute | solution.py:149
  170.9 10.3 %collective-permute-done.37 = bf16[144,1152]{1,0:T(8,128)(2,1)S(1)} collective-permute-done((bf16[144,1152]{1,0:T(8,128)(2,1)S(1)}, bf16[144,1152]{1,0:T(8,128)(2,1)S(1)}, u32[]{:S(2)}, u32[]{:S(2)}) %collective-permute-start.37) | collective-permute-done | bytes 331808 | tf_op jit(solution)/shard_map/ppermute | solution.py:149
  184.0 15.1 %collective-permute-done.3.refs_1_ = bf16[2,144,1152]{2,1,0:T(8,128)(2,1)S(1)} collective-permute-done((bf16[2,144,1152]{2,1,0:T(8,128)(2,1)S(1)}, bf16[2,144,1152]{2,1,0:T(8,128)(2,1)S(1)}, u32[]{:S(2)}, u32[]{:S(2)}) %collective-permute-start.3) | collective-permute-done | bytes 663584 | tf_op jit(solution)/shard_map/ppermute | solution.py:149
  200.4 9.8 %collective-permute-done.8.refs_7_ = bf16[2,144,1152]{2,1,0:T(8,128)(2,1)S(1)} collective-permute-done((bf16[2,144,1152]{2,1,0:T(8,128)(2,1)S(1)}, bf16[2,144,1152]{2,1,0:T(8,128)(2,1)S(1)}, u32[]{:S(2)}, u32[]{:S(2)}) %collective-permute-start.8) | collective-permute-done | bytes 663584 | tf_op jit(solution)/shard_map/ppermute | solution.py:149
  241.2 7.7 fusion.281
  248.9 8.4 fusion
  260.4 9.3 %fusion.54 = bf16[16,72,512]{2,1,0:T(8,128)(2,1)S(1)} fusion(bf16[512,16,72]{0,2,1:T(8,128)(2,1)} %bitcast.524, f32[16,512,512]{1,2,0:T(8,128)} %get-tuple-element.212, f32[16,512]{1,0:T(8,128)S(1)} %fusion, f32[16,512]{1,0:T(8,128)S(1)} %get-tuple-element.211), kind=kOutput, calls=%fused_computation.160 | convolution fusion | flops 617152512 | bytes 19202048 | tf_op jit(solution)/shard_map/while/body/eval_jaxpr/hqk,khd->qhd/dot_general | solution.py:68
  285.0 7.4 collective-permute-done.21.refs_2_
  293.5 12.4 %collective-permute-done.22.refs_3_ = bf16[2,144,1152]{2,1,0:T(8,128)(2,1)} collective-permute-done((bf16[2,144,1152]{2,1,0:T(8,128)(2,1)}, bf16[2,144,1152]{2,1,0:T(8,128)(2,1)}, u32[]{:S(2)}, u32[]{:S(2)}) %collective-permute-start.22) | collective-permute-done | bytes 663584 | tf_op jit(solution)/shard_map/ppermute | solution.py:149
  359.3 12.1 %collective-permute-done.39.refs_2_ = bf16[2,144,1152]{2,1,0:T(8,128)(2,1)S(1)} collective-permute-done((bf16[2,144,1152]{2,1,0:T(8,128)(2,1)S(1)}, bf16[2,144,1152]{2,1,0:T(8,128)(2,1)S(1)}, u32[]{:S(2)}, u32[]{:S(2)}) %collective-permute-start.39) | collective-permute-done | bytes 663584 | tf_op jit(solution)/shard_map/ppermute | solution.py:149
  372.0 12.9 %collective-permute-done.40.refs_3_ = bf16[2,144,1152]{2,1,0:T(8,128)(2,1)S(1)} collective-permute-done((bf16[2,144,1152]{2,1,0:T(8,128)(2,1)S(1)}, bf16[2,144,1152]{2,1,0:T(8,128)(2,1)S(1)}, u32[]{:S(2)}, u32[]{:S(2)}) %collective-permute-start.40) | collective-permute-done | bytes 663584 | tf_op jit(solution)/shard_map/ppermute | solution.py:149
  431.7 10.7 %fusion.258 = (f32[512]{0:T(512)S(1)}, f32[512,1152]{1,0:T(8,128)}, bf16[512,1152]{1,0:T(8,128)(2,1)}, f32[512,1152]{1,0:T(8,128)}) fusion(f32[512]{0:T(512)S(1)} %multiply_multiply_fusion.9, f32[512,1152]{1,0:T(8,128)S(1)} %copy-done.4, f32[512]{0:T(512)S(1)} %broadcast_multiply_fusion, f32[512]{0:T(512)S(1)} %fusion.247, ...), kind=kOutput, calls=%fused_computation.530 | convolution fusion | flops 1373109760 | bytes 27439616 | tf_op jit(solution)/shard_map/dot_general | solution.py:36
  485.9 9.1 %convert_reduce_fusion.3 = (f32[16,72]{1,0:T(8,128)S(1)}, bf16[16,72,512]{2,1,0:T(8,128)(2,1)S(1)}) fusion(bf16[512,16,72]{0,2,1:T(8,128)(2,1)} %bitcast.485, f32[16,512,512]{1,2,0:T(8,128)} %get-tuple-element.212, f32[16,512]{1,0:T(8,128)S(1)} %log_add_fusion), kind=kOutput, calls=%fused_computation.129 | convolution fusion | flops 614136704 | bytes 19173888 | tf_op jit(solution)/shard_map/while/body/eval_jaxpr/hqk,qhd->khd/dot_general | solution.py:113
  495.1 11.2 %multiply_reduce_fusion = (f32[16,512]{1,0:T(8,128)S(1)}, f32[16,512,512]{1,2,0:T(8,128)}) fusion(f32[16,512,512]{1,2,0:T(8,128)} %get-tuple-element.212, f32[16,512]{1,0:T(8,128)S(1)} %log_add_fusion, bf16[512,16,72]{0,2,1:T(8,128)(2,1)S(1)} %bitcast.486, bf16[512,16,72]{0,2,1:T(8,128)(2,1)S(1)} %bitcast.525), kind=kOutput, calls=%fused_computation.2 | convolution fusion | flops 616554496 | bytes 35979264 | tf_op jit(solution)/shard_map/while/body/eval_jaxpr/qhd,khd->hqk/dot_general | solution.py:99
  506.2 11.7 %multiply_convert_fusion = bf16[16,512,512]{1,2,0:T(8,128)(2,1)S(1)} fusion(f32[16,512,512]{1,2,0:T(8,128)} %get-tuple-element.218, f32[16,512,512]{1,2,0:T(8,128)} %get-tuple-element.212, f32[16,512]{1,0:T(8,128)S(1)} %get-tuple-element.217, f32[16,512]{1,0:T(8,128)S(1)} %log_add_fusion), kind=kLoop, calls=%fused_computation.1 | loop fusion | flops 16777216 | bytes 42008576 | tf_op jit(solution)/shard_map/while/body/eval_jaxpr/convert_element_type | solution.py:103
  564.4 16.7 %shard_map.243 = bf16[32,16,432]{2,1,0:T(8,128)(2,1)S(1)} custom-call(bf16[32,16,432]{2,1,0:T(8,128)(2,1)S(1)} %bitcast.447), custom_call_target="tpu_custom_call" | custom-call | bytes 3538944 | tf_op jit(solution)/shard_map/pallas_call | solution.py:452
  582.7 10.3 %shard_map.244 = f32[32,8,128]{2,1,0:T(8,128)S(1)} custom-call(f32[32,8,128]{2,1,0:T(8,128)S(1)} %bitcast.449), custom_call_target="tpu_custom_call" | custom-call | bytes 1048576 | tf_op jit(solution)/shard_map/pallas_call | solution.py:452
  643.8 14.4 %collective-permute-done.98 = bf16[2,144,1152]{2,1,0:T(8,128)(2,1)S(1)} collective-permute-done((bf16[2,144,1152]{2,1,0:T(8,128)(2,1)S(1)}, bf16[2,144,1152]{2,1,0:T(8,128)(2,1)S(1)}, u32[]{:S(2)}, u32[]{:S(2)}) %collective-permute-start.98) | collective-permute-done | bytes 663584 | tf_op jit(solution)/shard_map/ppermute | solution.py:149
  662.4 12.1 %collective-permute-done.74 = bf16[2,144,1152]{2,1,0:T(8,128)(2,1)S(1)} collective-permute-done((bf16[2,144,1152]{2,1,0:T(8,128)(2,1)S(1)}, bf16[2,144,1152]{2,1,0:T(8,128)(2,1)S(1)}, u32[]{:S(2)}, u32[]{:S(2)}) %collective-permute-start.74) | collective-permute-done | bytes 663584 | tf_op jit(solution)/shard_map/ppermute | solution.py:149
  681.4 8.6 %collective-permute-done.57 = bf16[2,144,1152]{2,1,0:T(8,128)(2,1)S(1)} collective-permute-done((bf16[2,144,1152]{2,1,0:T(8,128)(2,1)S(1)}, bf16[2,144,1152]{2,1,0:T(8,128)(2,1)S(1)}, u32[]{:S(2)}, u32[]{:S(2)}) %collective-permute-start.57) | collective-permute-done | bytes 663584 | tf_op jit(solution)/shard_map/ppermute | solution.py:149
  697.3 13.0 %collective-permute-done.95 = bf16[2,144,1152]{2,1,0:T(8,128)(2,1)S(1)} collective-permute-done((bf16[2,144,1152]{2,1,0:T(8,128)(2,1)S(1)}, bf16[2,144,1152]{2,1,0:T(8,128)(2,1)S(1)}, u32[]{:S(2)}, u32[]{:S(2)}) %collective-permute-start.95) | collective-permute-done | bytes 663584 | tf_op jit(solution)/shard_map/ppermute | solution.py:149
  727.0 11.7 %collective-permute-done.61 = bf16[2,144,1152]{2,1,0:T(8,128)(2,1)S(1)} collective-permute-done((bf16[2,144,1152]{2,1,0:T(8,128)(2,1)S(1)}, bf16[2,144,1152]{2,1,0:T(8,128)(2,1)S(1)}, u32[]{:S(2)}, u32[]{:S(2)}) %collective-permute-start.61) | collective-permute-done | bytes 663584 | tf_op jit(solution)/shard_map/ppermute | solution.py:149
  738.7 8.4 collective-permute-done.65
  759.6 19.9 %collective-permute-done.101 = bf16[144,1152]{1,0:T(8,128)(2,1)S(1)} collective-permute-done((bf16[144,1152]{1,0:T(8,128)(2,1)S(1)}, bf16[144,1152]{1,0:T(8,128)(2,1)S(1)}, u32[]{:S(2)}, u32[]{:S(2)}) %collective-permute-start.101) | collective-permute-done | bytes 331808 | tf_op jit(solution)/shard_map/ppermute | solution.py:149
  787.8 9.8 %collective-permute-done.71 = bf16[2,144,1152]{2,1,0:T(8,128)(2,1)} collective-permute-done((bf16[2,144,1152]{2,1,0:T(8,128)(2,1)}, bf16[2,144,1152]{2,1,0:T(8,128)(2,1)}, u32[]{:S(2)}, u32[]{:S(2)}) %collective-permute-start.71) | collective-permute-done | bytes 663584 | tf_op jit(solution)/shard_map/ppermute | solution.py:149
  802.7 7.8 collective-permute-done.82
  819.3 20.2 %collective-permute-done.67 = bf16[144,1152]{1,0:T(8,128)(2,1)S(1)} collective-permute-done((bf16[144,1152]{1,0:T(8,128)(2,1)S(1)}, bf16[144,1152]{1,0:T(8,128)(2,1)S(1)}, u32[]{:S(2)}, u32[]{:S(2)}) %collective-permute-start.67) | collective-permute-done | bytes 331808 | tf_op jit(solution)/shard_map/ppermute | solution.py:149
  842.3 13.1 %collective-permute-done.84 = bf16[144,1152]{1,0:T(8,128)(2,1)S(1)} collective-permute-done((bf16[144,1152]{1,0:T(8,128)(2,1)S(1)}, bf16[144,1152]{1,0:T(8,128)(2,1)S(1)}, u32[]{:S(2)}, u32[]{:S(2)}) %collective-permute-start.84) | collective-permute-done | bytes 331808 | tf_op jit(solution)/shard_map/ppermute | solution.py:149
  (753 shorter events, 452.2 us)
Async XLA Ops:
  2.7 108.3 %collective-permute-start.2 = (bf16[144,1152]{1,0:T(8,128)(2,1)}, bf16[144,1152]{1,0:T(8,128)(2,1)S(1)}, u32[]{:S(2)}, u32[]{:S(2)}) collective-permute-start(bf16[144,1152]{1,0:T(8,128)(2,1)} %get-tuple-element.80), channel_id=1, source_target_pairs={{0,2},{1,3},{2,4},{3,5},{4,6},{5,7},{6,0},{7,1},{8,10},{9,11},{10,... | collective-permute-start | bytes 995336 | tf_op jit(solution)/shard_map/ppermute | solution.py:149
  5.7 105.3 %collective-permute-start.1 = (bf16[144,1152]{1,0:T(8,128)(2,1)}, bf16[144,1152]{1,0:T(8,128)(2,1)}, u32[]{:S(2)}, u32[]{:S(2)}) collective-permute-start(bf16[144,1152]{1,0:T(8,128)(2,1)} %get-tuple-element.80), channel_id=1, source_target_pairs={{0,4},{1,5},{2,6},{3,7},{4,0},{5,1},{6,2},{7,3},{8,12},{9,13},{10,... | collective-permute-start | bytes 995336 | tf_op jit(solution)/shard_map/ppermute | solution.py:149
  8.3 102.7 %collective-permute-start = (bf16[144,1152]{1,0:T(8,128)(2,1)}, bf16[144,1152]{1,0:T(8,128)(2,1)}, u32[]{:S(2)}, u32[]{:S(2)}) collective-permute-start(bf16[144,1152]{1,0:T(8,128)(2,1)} %get-tuple-element.80), channel_id=1, source_target_pairs={{0,6},{1,7},{2,0},{3,1},{4,2},{5,3},{6,4},{7,5},{8,14},{9,15},{10,... | collective-permute-start | bytes 995336 | tf_op jit(solution)/shard_map/ppermute | solution.py:149
  11.4 98.1 %collective-permute-start.34 = (bf16[144,576]{1,0:T(8,128)(2,1)}, bf16[144,576]{1,0:T(8,128)(2,1)}, u32[]{:S(2)}, u32[]{:S(2)}) collective-permute-start(bf16[144,576]{1,0:T(8,128)(2,1)} %get-tuple-element.188), channel_id=1, source_target_pairs={{0,1},{1,0},{2,3},{3,2},{4,5},{5,4},{6,7},{7,6},{8,9},{9,8},{10,11... | collective-permute-start | bytes 497672 | tf_op jit(solution)/shard_map/ppermute | solution.py:149
  128.2 54.2 %collective-permute-start.13 = (bf16[2,144,1152]{2,1,0:T(8,128)(2,1)S(1)}, bf16[2,144,1152]{2,1,0:T(8,128)(2,1)S(1)}, u32[]{:S(2)}, u32[]{:S(2)}) collective-permute-start(bf16[2,144,1152]{2,1,0:T(8,128)(2,1)S(1)} %get-tuple-element.141.refs_4_), channel_id=1, source_target_pairs={{0,1},{1,0},{2,3},{3,2},{4,5},{5,4},{6,7},{7,6},{8,9},{9,8},{10,11... | collective-permute-start | bytes 1990664 | tf_op jit(solution)/shard_map/ppermute | solution.py:149
  128.2 55.2 %collective-permute-start.7 = (bf16[2,144,1152]{2,1,0:T(8,128)(2,1)S(1)}, bf16[2,144,1152]{2,1,0:T(8,128)(2,1)S(1)}, u32[]{:S(2)}, u32[]{:S(2)}) collective-permute-start(bf16[2,144,1152]{2,1,0:T(8,128)(2,1)S(1)} %get-tuple-element.141.refs_4_), channel_id=1, source_target_pairs={{0,16},{1,17},{2,18},{3,19},{4,20},{5,21},{6,22},{7,23},{8,24},{9,... | collective-permute-start | bytes 1990664 | tf_op jit(solution)/shard_map/ppermute | solution.py:149
  128.9 54.6 %collective-permute-start.6 = (bf16[2,144,1152]{2,1,0:T(8,128)(2,1)S(1)}, bf16[2,144,1152]{2,1,0:T(8,128)(2,1)S(1)}, u32[]{:S(2)}, u32[]{:S(2)}) collective-permute-start(bf16[2,144,1152]{2,1,0:T(8,128)(2,1)S(1)} %get-tuple-element.141.refs_4_), channel_id=1, source_target_pairs={{0,8},{1,9},{2,10},{3,11},{4,12},{5,13},{6,14},{7,15},{8,0},{9,1},... | collective-permute-start | bytes 1990664 | tf_op jit(solution)/shard_map/ppermute | solution.py:149
  137.7 61.9 %collective-permute-start.9 = (bf16[2,144,1152]{2,1,0:T(8,128)(2,1)S(1)}, bf16[2,144,1152]{2,1,0:T(8,128)(2,1)S(1)}, u32[]{:S(2)}, u32[]{:S(2)}) collective-permute-start(bf16[2,144,1152]{2,1,0:T(8,128)(2,1)S(1)} %get-tuple-element.142.refs_0_), channel_id=1, source_target_pairs={{0,1},{1,0},{2,3},{3,2},{4,5},{5,4},{6,7},{7,6},{8,9},{9,8},{10,11... | collective-permute-start | bytes 1990664 | tf_op jit(solution)/shard_map/ppermute | solution.py:149
  211.3 63.2 %collective-permute-start.30 = (bf16[2,144,1152]{2,1,0:T(8,128)(2,1)S(1)}, bf16[2,144,1152]{2,1,0:T(8,128)(2,1)}, u32[]{:S(2)}, u32[]{:S(2)}) collective-permute-start(bf16[2,144,1152]{2,1,0:T(8,128)(2,1)S(1)} %get-tuple-element.137.refs_4_), channel_id=1, source_target_pairs={{0,1},{1,0},{2,3},{3,2},{4,5},{5,4},{6,7},{7,6},{8,9},{9,8},{10,11... | collective-permute-start | bytes 1990664 | tf_op jit(solution)/shard_map/ppermute | solution.py:149
  211.9 63.9 %collective-permute-start.24 = (bf16[2,144,1152]{2,1,0:T(8,128)(2,1)S(1)}, bf16[2,144,1152]{2,1,0:T(8,128)(2,1)}, u32[]{:S(2)}, u32[]{:S(2)}) collective-permute-start(bf16[2,144,1152]{2,1,0:T(8,128)(2,1)S(1)} %get-tuple-element.137.refs_4_), channel_id=1, source_target_pairs={{0,16},{1,17},{2,18},{3,19},{4,20},{5,21},{6,22},{7,23},{8,24},{9,... | collective-permute-start | bytes 1990664 | tf_op jit(solution)/shard_map/ppermute | solution.py:149
  212.9 63.0 %collective-permute-start.23 = (bf16[2,144,1152]{2,1,0:T(8,128)(2,1)S(1)}, bf16[2,144,1152]{2,1,0:T(8,128)(2,1)}, u32[]{:S(2)}, u32[]{:S(2)}) collective-permute-start(bf16[2,144,1152]{2,1,0:T(8,128)(2,1)S(1)} %get-tuple-element.137.refs_4_), channel_id=1, source_target_pairs={{0,8},{1,9},{2,10},{3,11},{4,12},{5,13},{6,14},{7,15},{8,0},{9,1},... | collective-permute-start | bytes 1990664 | tf_op jit(solution)/shard_map/ppermute | solution.py:149
  213.4 71.7 %collective-permute-start.26 = (bf16[2,144,1152]{2,1,0:T(8,128)(2,1)S(1)}, bf16[2,144,1152]{2,1,0:T(8,128)(2,1)}, u32[]{:S(2)}, u32[]{:S(2)}) collective-permute-start(bf16[2,144,1152]{2,1,0:T(8,128)(2,1)S(1)} %get-tuple-element.138.refs_0_), channel_id=1, source_target_pairs={{0,1},{1,0},{2,3},{3,2},{4,5},{5,4},{6,7},{7,6},{8,9},{9,8},{10,11... | collective-permute-start | bytes 1990664 | tf_op jit(solution)/shard_map/ppermute | solution.py:149
  213.4 63.3 %collective-permute-start.20 = (bf16[2,144,1152]{2,1,0:T(8,128)(2,1)S(1)}, bf16[2,144,1152]{2,1,0:T(8,128)(2,1)}, u32[]{:S(2)}, u32[]{:S(2)}) collective-permute-start(bf16[2,144,1152]{2,1,0:T(8,128)(2,1)S(1)} %get-tuple-element.138.refs_0_), channel_id=1, source_target_pairs={{0,8},{1,9},{2,10},{3,11},{4,12},{5,13},{6,14},{7,15},{8,0},{9,1},... | collective-permute-start | bytes 1990664 | tf_op jit(solution)/shard_map/ppermute | solution.py:149
  285.0 32.7 %collective-permute-start.27 = (bf16[2,144,1152]{2,1,0:T(8,128)(2,1)}, bf16[2,144,1152]{2,1,0:T(8,128)(2,1)}, u32[]{:S(2)}, u32[]{:S(2)}) collective-permute-start(bf16[2,144,1152]{2,1,0:T(8,128)(2,1)} %collective-permute-done.20.refs_1_), channel_id=1, source_target_pairs={{0,1},{1,0},{2,3},{3,2},{4,5},{5,4},{6,7},{7,6},{8,9},{9,8},{10,11... | collective-permute-start | bytes 1990664 | tf_op jit(solution)/shard_map/ppermute | solution.py:149
  316.1 37.5 %collective-permute-start.48 = (bf16[2,144,1152]{2,1,0:T(8,128)(2,1)S(1)}, bf16[2,144,1152]{2,1,0:T(8,128)(2,1)S(1)}, u32[]{:S(2)}, u32[]{:S(2)}) collective-permute-start(bf16[2,144,1152]{2,1,0:T(8,128)(2,1)S(1)} %get-tuple-element.139.refs_4_), channel_id=1, source_target_pairs={{0,1},{1,0},{2,3},{3,2},{4,5},{5,4},{6,7},{7,6},{8,9},{9,8},{10,11... | collective-permute-start | bytes 1990664 | tf_op jit(solution)/shard_map/ppermute | solution.py:149
  316.7 37.9 %collective-permute-start.42 = (bf16[2,144,1152]{2,1,0:T(8,128)(2,1)S(1)}, bf16[2,144,1152]{2,1,0:T(8,128)(2,1)S(1)}, u32[]{:S(2)}, u32[]{:S(2)}) collective-permute-start(bf16[2,144,1152]{2,1,0:T(8,128)(2,1)S(1)} %get-tuple-element.139.refs_4_), channel_id=1, source_target_pairs={{0,16},{1,17},{2,18},{3,19},{4,20},{5,21},{6,22},{7,23},{8,24},{9,... | collective-permute-start | bytes 1990664 | tf_op jit(solution)/shard_map/ppermute | solution.py:149
  317.8 36.8 %collective-permute-start.41 = (bf16[2,144,1152]{2,1,0:T(8,128)(2,1)S(1)}, bf16[2,144,1152]{2,1,0:T(8,128)(2,1)S(1)}, u32[]{:S(2)}, u32[]{:S(2)}) collective-permute-start(bf16[2,144,1152]{2,1,0:T(8,128)(2,1)S(1)} %get-tuple-element.139.refs_4_), channel_id=1, source_target_pairs={{0,8},{1,9},{2,10},{3,11},{4,12},{5,13},{6,14},{7,15},{8,0},{9,1},... | collective-permute-start | bytes 1990664 | tf_op jit(solution)/shard_map/ppermute | solution.py:149
  318.8 40.5 %collective-permute-start.44 = (bf16[2,144,1152]{2,1,0:T(8,128)(2,1)S(1)}, bf16[2,144,1152]{2,1,0:T(8,128)(2,1)S(1)}, u32[]{:S(2)}, u32[]{:S(2)}) collective-permute-start(bf16[2,144,1152]{2,1,0:T(8,128)(2,1)S(1)} %get-tuple-element.140.refs_0_), channel_id=1, source_target_pairs={{0,1},{1,0},{2,3},{3,2},{4,5},{5,4},{6,7},{7,6},{8,9},{9,8},{10,11... | collective-permute-start | bytes 1990664 | tf_op jit(solution)/shard_map/ppermute | solution.py:149
  318.8 36.4 %collective-permute-start.38 = (bf16[2,144,1152]{2,1,0:T(8,128)(2,1)S(1)}, bf16[2,144,1152]{2,1,0:T(8,128)(2,1)S(1)}, u32[]{:S(2)}, u32[]{:S(2)}) collective-permute-start(bf16[2,144,1152]{2,1,0:T(8,128)(2,1)S(1)} %get-tuple-element.140.refs_0_), channel_id=1, source_target_pairs={{0,8},{1,9},{2,10},{3,11},{4,12},{5,13},{6,14},{7,15},{8,0},{9,1},... | collective-permute-start | bytes 1990664 | tf_op jit(solution)/shard_map/ppermute | solution.py:149
  387.3 240.9 %collective-permute-start.94 = (bf16[2,144,1152]{2,1,0:T(8,128)(2,1)}, bf16[2,144,1152]{2,1,0:T(8,128)(2,1)}, u32[]{:S(2)}, u32[]{:S(2)}) collective-permute-start(bf16[2,144,1152]{2,1,0:T(8,128)(2,1)} %pad_maximum_fusion.18), channel_id=1, source_target_pairs={{0,1},{1,0},{2,3},{3,2},{4,5},{5,4},{6,7},{7,6},{8,9},{9,8},{10,11... | collective-permute-start | bytes 1990664 | tf_op jit(solution)/shard_map/ppermute | solution.py:149
  387.8 255.9 %collective-permute-start.96 = (bf16[2,144,1152]{2,1,0:T(8,128)(2,1)}, bf16[2,144,1152]{2,1,0:T(8,128)(2,1)}, u32[]{:S(2)}, u32[]{:S(2)}) collective-permute-start(bf16[2,144,1152]{2,1,0:T(8,128)(2,1)} %pad_maximum_fusion.19), channel_id=1, source_target_pairs={{0,1},{1,0},{2,3},{3,2},{4,5},{5,4},{6,7},{7,6},{8,9},{9,8},{10,11... | collective-permute-start | bytes 1990664 | tf_op jit(solution)/shard_map/ppermute | solution.py:149
  387.9 241.9 %collective-permute-start.97 = (bf16[2,144,1152]{2,1,0:T(8,128)(2,1)}, bf16[2,144,1152]{2,1,0:T(8,128)(2,1)}, u32[]{:S(2)}, u32[]{:S(2)}) collective-permute-start(bf16[2,144,1152]{2,1,0:T(8,128)(2,1)} %pad_maximum_fusion.20), channel_id=1, source_target_pairs={{0,1},{1,0},{2,3},{3,2},{4,5},{5,4},{6,7},{7,6},{8,9},{9,8},{10,11... | collective-permute-start | bytes 1990664 | tf_op jit(solution)/shard_map/ppermute | solution.py:149
  388.3 303.1 %collective-permute-start.93 = (bf16[2,144,1152]{2,1,0:T(8,128)(2,1)}, bf16[2,144,1152]{2,1,0:T(8,128)(2,1)}, u32[]{:S(2)}, u32[]{:S(2)}) collective-permute-start(bf16[2,144,1152]{2,1,0:T(8,128)(2,1)} %pad_maximum_fusion.17), channel_id=1, source_target_pairs={{0,1},{1,0},{2,3},{3,2},{4,5},{5,4},{6,7},{7,6},{8,9},{9,8},{10,11... | collective-permute-start | bytes 1990664 | tf_op jit(solution)/shard_map/ppermute | solution.py:149
  388.4 243.3 %collective-permute-start.87 = (bf16[2,144,1152]{2,1,0:T(8,128)(2,1)}, bf16[2,144,1152]{2,1,0:T(8,128)(2,1)}, u32[]{:S(2)}, u32[]{:S(2)}) collective-permute-start(bf16[2,144,1152]{2,1,0:T(8,128)(2,1)} %pad_maximum_fusion.14), channel_id=1, source_target_pairs={{0,1},{1,0},{2,3},{3,2},{4,5},{5,4},{6,7},{7,6},{8,9},{9,8},{10,11... | collective-permute-start | bytes 1990664 | tf_op jit(solution)/shard_map/ppermute | solution.py:149
  710.3 37.4 %collective-permute-start.52 = (bf16[2,144,1152]{2,1,0:T(8,128)(2,1)S(1)}, bf16[2,144,1152]{2,1,0:T(8,128)(2,1)S(1)}, u32[]{:S(2)}, u32[]{:S(2)}) collective-permute-start(bf16[2,144,1152]{2,1,0:T(8,128)(2,1)S(1)} %bitcast.550), channel_id=1, source_target_pairs={{0,1},{1,0},{2,3},{3,2},{4,5},{5,4},{6,7},{7,6},{8,9},{9,8},{10,11... | collective-permute-start | bytes 1990664 | tf_op jit(solution)/shard_map/ppermute | solution.py:149
  738.7 46.7 %collective-permute-start.69 = (bf16[2,144,1152]{2,1,0:T(8,128)(2,1)}, bf16[2,144,1152]{2,1,0:T(8,128)(2,1)}, u32[]{:S(2)}, u32[]{:S(2)}) collective-permute-start(bf16[2,144,1152]{2,1,0:T(8,128)(2,1)} %bitcast.102), channel_id=1, source_target_pairs={{0,1},{1,0},{2,3},{3,2},{4,5},{5,4},{6,7},{7,6},{8,9},{9,8},{10,11... | collective-permute-start | bytes 1990664 | tf_op jit(solution)/shard_map/ppermute | solution.py:149
  747.1 52.3 %collective-permute-start.76 = (bf16[2,144,1152]{2,1,0:T(8,128)(2,1)}, bf16[2,144,1152]{2,1,0:T(8,128)(2,1)}, u32[]{:S(2)}, u32[]{:S(2)}) collective-permute-start(bf16[2,144,1152]{2,1,0:T(8,128)(2,1)} %bitcast.113), channel_id=1, source_target_pairs={{0,1},{1,0},{2,3},{3,2},{4,5},{5,4},{6,7},{7,6},{8,9},{9,8},{10,11... | collective-permute-start | bytes 1990664 | tf_op jit(solution)/shard_map/ppermute | solution.py:149
  758.7 42.0 %collective-permute-start.78 = (bf16[2,144,1152]{2,1,0:T(8,128)(2,1)}, bf16[2,144,1152]{2,1,0:T(8,128)(2,1)}, u32[]{:S(2)}, u32[]{:S(2)}) collective-permute-start(bf16[2,144,1152]{2,1,0:T(8,128)(2,1)} %add_convert_fusion.3), channel_id=1, source_target_pairs={{0,16},{1,17},{2,18},{3,19},{4,20},{5,21},{6,22},{7,23},{8,24},{9,... | collective-permute-start | bytes 1990664 | tf_op jit(solution)/shard_map/ppermute | solution.py:149
  797.6 43.8 %collective-permute-start.103 = (f32[144,576]{1,0:T(8,128)S(1)}, f32[144,576]{1,0:T(8,128)S(1)}, u32[]{:S(2)}, u32[]{:S(2)}) collective-permute-start(f32[144,576]{1,0:T(8,128)S(1)} %bitcast.580), channel_id=1, source_target_pairs={{0,1},{1,0},{2,3},{3,2},{4,5},{5,4},{6,7},{7,6},{8,9},{9,8},{10,11... | collective-permute-start | bytes 995336 | tf_op jit(solution)/shard_map/ppermute | solution.py:149
  799.4 40.1 %collective-permute-start.67 = (bf16[144,1152]{1,0:T(8,128)(2,1)S(1)}, bf16[144,1152]{1,0:T(8,128)(2,1)S(1)}, u32[]{:S(2)}, u32[]{:S(2)}) collective-permute-start(bf16[144,1152]{1,0:T(8,128)(2,1)S(1)} %get-tuple-element.135), channel_id=1, source_target_pairs={{0,4},{1,5},{2,6},{3,7},{4,0},{5,1},{6,2},{7,3},{8,12},{9,13},{10,... | collective-permute-start | bytes 995336 | tf_op jit(solution)/shard_map/ppermute | solution.py:149
  800.6 38.9 %collective-permute-start.68 = (bf16[144,1152]{1,0:T(8,128)(2,1)S(1)}, bf16[144,1152]{1,0:T(8,128)(2,1)S(1)}, u32[]{:S(2)}, u32[]{:S(2)}) collective-permute-start(bf16[144,1152]{1,0:T(8,128)(2,1)S(1)} %get-tuple-element.136), channel_id=1, source_target_pairs={{0,2},{1,3},{2,4},{3,5},{4,6},{5,7},{6,0},{7,1},{8,10},{9,11},{10,... | collective-permute-start | bytes 995336 | tf_op jit(solution)/shard_map/ppermute | solution.py:149
  812.5 43.0 %collective-permute-start.84 = (bf16[144,1152]{1,0:T(8,128)(2,1)S(1)}, bf16[144,1152]{1,0:T(8,128)(2,1)S(1)}, u32[]{:S(2)}, u32[]{:S(2)}) collective-permute-start(bf16[144,1152]{1,0:T(8,128)(2,1)S(1)} %get-tuple-element.124), channel_id=1, source_target_pairs={{0,4},{1,5},{2,6},{3,7},{4,0},{5,1},{6,2},{7,3},{8,12},{9,13},{10,... | collective-permute-start | bytes 995336 | tf_op jit(solution)/shard_map/ppermute | solution.py:149
  (220 other events, 2274.0 us)

commit v3 on v2

--- a/solution.py
+++ b/solution.py
@@ -186,172 +186,23 @@
     return (own, other)
 
 
-def lay_out(plane_major, *refs):
-    pieces, out, room, arrive, leave = refs[:16], refs[16], refs[17], refs[18], refs[19]
-    plane, _, core = place()
-    sides = (core, 1 - core)
-
-    def fill(block):
-        slot = block % 2
-        copies = []
-        for flip_core in range(2):
-            for step in range(2 if plane_major else 4):
-                if plane_major:
-                    source = pieces[flip_core * 8 + step * 4 + block]
-                    target = room.at[slot, pl.ds(2 * step, 2), sides[flip_core]]
-                else:
-                    source = pieces[flip_core * 8 + block // 2 * 4 + step].at[block % 2]
-                    target = room.at[slot, flipped(plane, step), sides[flip_core]]
-                copies.append(
-                    pltpu.make_async_copy(source, target, arrive.at[slot, len(copies)])
-                )
-        for copy in copies:
-            copy.start()
-        return copies
-
-    filling, draining = [fill(0), None], [None, None]
-    for block in range(4):
-        slot = block % 2
-        if block < 3:
-            if draining[1 - slot] is not None:
-                draining[1 - slot].wait()
-            filling[1 - slot] = fill(block + 1)
-        for copy in filling[slot]:
-            copy.wait()
-        at = flipped(plane, block) if plane_major else block
-        draining[slot] = pltpu.make_async_copy(room.at[slot], out.at[at], leave.at[slot])
-        draining[slot].start()
-    for copy in draining:
-        copy.wait()
-
-
-def assemble(pieces, plane_major):
-    flat = [piece for side in pieces for found in side for piece in found]
-    rows, columns = flat[0].shape[1:]
-    whole = pl.pallas_call(
-        partial(lay_out, plane_major),
-        out_shape=jax.ShapeDtypeStruct((4, 4, 2, rows, columns), flat[0].dtype),
-        in_specs=[pl.BlockSpec(memory_space=pl.ANY)] * 16,
-        out_specs=pl.BlockSpec(memory_space=pl.ANY),
-        scratch_shapes=[
-            pltpu.VMEM((2, 4, 2, rows, columns), flat[0].dtype),
-            pltpu.SemaphoreType.DMA((2, 8)),
-            pltpu.SemaphoreType.DMA((2,)),
-        ],
-        compiler_params=pltpu.CompilerParams(vmem_limit_bytes=16 * 2**20),
-        cost_estimate=pl.CostEstimate(
-            flops=0, bytes_accessed=2 * 32 * rows * columns * 2, transcendentals=0
-        ),
-    )(*flat)
-    return whole.reshape(4, 8 * rows, columns)
-
-
-def scatter_terms(sibling, own):
-    depth = place()[1]
-    totals = []
-    for half, (first, first_flip, second, second_flip) in enumerate(HALF_ORDERS):
-        summed = [
-            own[half][flip].astype(jnp.float32)
-            + swap(sibling[half][flip].astype(jnp.bfloat16), "core").astype(jnp.float32)
-            for flip in range(4)
-        ]
-        across = summed[second_flip] + swap(summed[3].astype(jnp.bfloat16), first).astype(jnp.float32)
-        home = summed[0] + swap(summed[first_flip].astype(jnp.bfloat16), first).astype(jnp.float32)
-        totals.append(home + swap(across.astype(jnp.bfloat16), second).astype(jnp.float32))
-    total = jnp.concatenate(totals)
-    result = lax.dynamic_index_in_dim(total, depth, axis=0, keepdims=False)
-    for turn in (1, 2, 3):
-        term = lax.dynamic_index_in_dim(total, (depth - turn) % 4, axis=0, keepdims=False)
-        result = result + swap(term.astype(jnp.bfloat16), turn).astype(jnp.float32)
-    return result
-
-
-def halves(terms):
-    return [[term[:2] for term in terms], [term[2:] for term in terms]]
-
-
-def core_columns(values):
-    rows, columns = values.shape
-    core = place()[2]
-    cut = values.reshape(rows, 4, 2, columns // 8)
-    return [
-        lax.dynamic_index_in_dim(cut, side, axis=2, keepdims=False).reshape(rows, columns // 2)
-        for side in (core, 1 - core)
-    ]
-
-
 def pick(values, index):
     return lax.dynamic_index_in_dim(values, index, axis=0, keepdims=False)
 
 
 def gather_blocks(attn_weight, proj_weight, up_weight, down_weight):
-    if not on_box():
-        parts = lax.axis_size("dp")
-        attn, proj, up, down = [
-            lax.all_gather(lax.all_gather(weight, "dp", axis=1, tiled=True), "fsdp", axis=0, tiled=True)
-            for weight in (attn_weight, proj_weight, up_weight, down_weight)
-        ]
-        width = attn.shape[0]
-
-        def by_block(weight):
-            return weight.reshape(weight.shape[0], parts, -1).transpose(1, 0, 2)
-
-        joined = jnp.concatenate([by_block(attn), by_block(proj)], axis=2)
-        return joined, by_block(up), by_block(down.T.reshape(width, -1))
-    core = place()[2]
-    rows, _ = up_weight.shape
-    joined_line = gather_line(jnp.concatenate([attn_weight, proj_weight], axis=1))
-    turned = down_weight.T.reshape(2, rows, down_weight.shape[0])
-    mine, theirs = pick(turned, core), pick(turned, 1 - core)
-    arrived = swap(theirs, "core")
-    down_shard = jnp.where(
-        core == 0,
-        jnp.concatenate([mine, arrived], axis=1),
-        jnp.concatenate([arrived, mine], axis=1),
-    )
-    up_shard, _ = lax.optimization_barrier((up_weight, joined_line[1:]))
-    up_line = gather_line(up_shard)
-    down_shard, _ = lax.optimization_barrier((down_shard, up_line[1:]))
-    down_line = gather_line(down_shard)
-    return (
-        assemble(gather_plane(joined_line), True),
-        assemble(gather_plane(up_line), True),
-        assemble(gather_plane(down_line), False),
-    )
-
-
-def scatter_down(hidden, grad_branch2):
-    if not on_box():
-        rows = hidden.shape[1]
-        flat = hidden.transpose(1, 0, 2).reshape(rows, -1)
-        return scatter_whole(matmul_tn(flat, grad_branch2))
-    plane, _, core = place()
-    width = grad_branch2.shape[1]
-    block = width // 8
-    columns = grad_branch2.reshape(-1, 4, 2, block)
-    order = jnp.stack([flipped(plane, flip) for flip in range(4)])
-    columns = jnp.take(columns, order, axis=1)
-    terms = []
-    for side in (1 - core, core):
-        lhs = lax.dynamic_index_in_dim(columns, side, axis=2, keepdims=False).reshape(-1, width // 2)
-        found = [matmul_tn(lhs, hidden[part]).reshape(4, block, -1) for part in range(4)]
-        if len(terms) == 0:
-            found = [value.astype(jnp.bfloat16) for value in found]
-        terms.append(
-            [
-                [jnp.stack([found[2 * half][flip], found[2 * half + 1][flip]]) for flip in range(4)]
-                for half in range(2)
-            ]
-        )
-    total = scatter_terms(terms[0], terms[1])
-    depth = total.shape[1] // 2
-    cut = total.reshape(block, 2, depth).transpose(1, 0, 2)
-    mine, theirs = pick(cut, core), pick(cut, 1 - core)
-    arrived = swap(theirs, "core")
-    whole = jnp.where(
-        core == 0, jnp.concatenate([mine, arrived]), jnp.concatenate([arrived, mine])
-    )
-    return whole.T
+    parts = lax.axis_size("dp")
+    attn, proj, up, down = [
+        lax.all_gather(lax.all_gather(weight, "dp", axis=1, tiled=True), "fsdp", axis=0, tiled=True)
+        for weight in (attn_weight, proj_weight, up_weight, down_weight)
+    ]
+    width = attn.shape[0]
+
+    def by_block(weight):
+        return weight.reshape(weight.shape[0], parts, -1).transpose(1, 0, 2)
+
+    joined = jnp.concatenate([by_block(attn), by_block(proj)], axis=2)
+    return joined, by_block(up), by_block(down.T.reshape(width, -1))
 
 
 def scatter_whole(gradient):
@@ -362,32 +213,10 @@
 
 
 def scatter_rows(pairs):
-    if not on_box():
-        return [
-            scatter_whole(matmul_tn(left, right.transpose(1, 0, 2).reshape(left.shape[0], -1)))
-            for left, right in pairs
-        ]
-    plane = place()[0]
-    cut = [core_columns(left) for left, _ in pairs]
-    terms = []
-    for side in (1, 0):
-        found = []
-        for flip in range(4):
-            products = [
-                matmul_tn(left[side], pick(right, flipped(plane, flip)))
-                for left, (_, right) in zip(cut, pairs)
-            ]
-            joined = jnp.concatenate(products, axis=1)
-            if side:
-                joined = joined.astype(jnp.bfloat16)
-            found.append(joined.reshape(4, -1, joined.shape[1]))
-        terms.append(halves(found))
-    total = scatter_terms(terms[0], terms[1])
-    results, begin = [], 0
-    for _, right in pairs:
-        results.append(total[:, begin : begin + right.shape[2]])
-        begin += right.shape[2]
-    return results
+    return [
+        scatter_whole(matmul_tn(left, right.transpose(1, 0, 2).reshape(left.shape[0], -1)))
+        for left, right in pairs
+    ]
 
 
 def trade(one_for_all, values, out, send_sems, recv_sems):
@@ -526,6 +355,755 @@
     return values.reshape(rows, parts, columns // parts).transpose(1, 0, 2)
 
 
+SLOPE = math.sqrt(2.0 / math.pi)
+WINDOW = 512
+
+
+def mm(left, right):
+    return jnp.dot(left, right, preferred_element_type=jnp.float32)
+
+
+def local_call(kernel, outs, ins, anys, scratch, megabytes):
+    return pl.pallas_call(
+        kernel,
+        out_shape=outs,
+        in_specs=[pl.BlockSpec(memory_space=pltpu.VMEM)] * len(ins)
+        + [pl.BlockSpec(memory_space=pl.ANY)] * len(anys),
+        out_specs=[
+            pl.BlockSpec(memory_space=pl.ANY if out.dtype == jnp.bfloat16 and out.ndim == 4 else pltpu.VMEM)
+            for out in outs
+        ],
+        scratch_shapes=scratch,
+        compiler_params=pltpu.CompilerParams(vmem_limit_bytes=megabytes * 2**20),
+        cost_estimate=pl.CostEstimate(flops=0, bytes_accessed=0, transcendentals=0),
+    )(*ins, *anys)
+
+
+def shaped(dims, kind=jnp.float32):
+    return jax.ShapeDtypeStruct(dims, kind)
+
+
+def load_blocks(pieces, room, sems, plane_major, natural=False, lanes=None):
+    plane, _, core = place()
+    sides = (core, 1 - core)
+    deep = pieces[0].shape[1]
+    blocks = [[] for _ in range(4)]
+    count = 0
+    for flip in range(4):
+        at = flipped(plane, flip)
+        for turn in range(2):
+            for depth in range(4):
+                source = pieces[turn * 8 + depth // 2 * 4 + flip].at[depth % 2]
+                if lanes is not None:
+                    source = source.at[:, lanes[0] : lanes[1]]
+                if plane_major:
+                    block, row, held = flip, depth * 2 + sides[turn], at if natural else flip
+                else:
+                    block, row, held = depth, at * 2 + sides[turn], depth
+                target = room.at[held, pl.ds(pl.multiple_of(row * deep, 16), deep)]
+                blocks[block].append(pltpu.make_async_copy(source, target, sems.at[count]))
+                count += 1
+    for block in blocks:
+        for copy in block:
+            copy.start()
+    return blocks
+
+
+def wait_all(copies):
+    for copy in copies:
+        copy.wait()
+
+
+def by_rows(count, step, body):
+    @pl.loop(0, count // step)
+    def _(index):
+        body(pl.ds(pl.multiple_of(index * step, step), step))
+
+
+def lane_index(rows, lanes):
+    return lax.broadcasted_iota(jnp.int32, (rows, lanes), 1)
+
+
+def window_of(block, width, total, span):
+    begin = min(block * width // 128 * 128, total - span)
+    return begin, block * width - begin
+
+
+def slot_rows(slots, table, column, width):
+    value = jnp.zeros((slots.shape[0], width), jnp.float32)
+    for slot in range(4):
+        value = value + jnp.where(slots == slot, table[slot : slot + 1, column * width : (column + 1) * width], 0.0)
+    return value
+
+
+def add_slots(out, slots, value):
+    for slot in range(4):
+        out[slot : slot + 1, :] += jnp.sum(jnp.where(slots == slot, value, 0.0), axis=0, keepdims=True)
+
+
+def centred(value):
+    center = value - jnp.mean(value, axis=-1, keepdims=True)
+    scale = lax.rsqrt(jnp.mean(center * center, axis=-1, keepdims=True) + 1e-06)
+    return center * scale, scale
+
+
+def norm_back(normed, scale, grad):
+    return scale * (
+        grad
+        - jnp.mean(grad, axis=-1, keepdims=True)
+        - normed * jnp.mean(grad * normed, axis=-1, keepdims=True)
+    )
+
+
+def project_kernel(normed, bias, *refs):
+    pieces, out, room, product, wide, sems = refs[:16], refs[16], refs[17], refs[18], refs[19], refs[20]
+    rows, width = normed.shape
+    columns = out.shape[1] // 4
+    for block in load_blocks(pieces, room, sems, True, natural=True):
+        wait_all(block)
+    span = product.shape[1]
+    for block in range(4):
+        product[...] = mm(normed[...], room[block, :, :span])
+        begin, offset = window_of(block, columns, out.shape[1], span)
+
+        def put(at):
+            moved = product[at, :]
+            if offset:
+                moved = pltpu.roll(moved, offset, 1)
+            lane = lane_index(moved.shape[0], span)
+            inside = (lane >= offset) & (lane < offset + columns)
+            wide[at, begin : begin + span] = jnp.where(inside, moved, wide[at, begin : begin + span])
+
+        by_rows(rows, 64, put)
+
+    def finish(at):
+        out[at, :] = (wide[at, :] + bias[...]).astype(jnp.bfloat16)
+
+    by_rows(rows, 64, finish)
+
+
+def project(normed, bias, pieces):
+    rows, width = normed.shape
+    total = bias.shape[1]
+    span = -(-total // 4 // 128) * 128 + 128
+    return local_call(
+        project_kernel,
+        [shaped((rows, total), jnp.bfloat16)],
+        [normed, bias],
+        pieces,
+        [
+            pltpu.VMEM((4, width, width), jnp.bfloat16),
+            pltpu.VMEM((rows, span), jnp.float32),
+            pltpu.VMEM((rows, total), jnp.float32),
+            pltpu.SemaphoreType.DMA((32,)),
+        ],
+        56,
+    )[0]
+
+
+def head_window(head, size, total):
+    begin = jnp.minimum(head * size // 128 * 128, total - 256)
+    begin = pl.multiple_of(begin, 128)
+    lane = lane_index(1, 256)
+    offset = head * size - begin
+    return begin, (lane >= offset) & (lane < offset + size)
+
+
+def attend_kernel(joined, slots, slot_line, out, stats, bar, wide):
+    rows, width = out.shape
+    size = width // HEADS
+    bar[...] = jnp.where(slots[...] == slot_line[...], 0.0, -1e30)
+    scale = 1.0 / math.sqrt(size)
+    stats[...] = jnp.zeros_like(stats)
+
+    @pl.loop(0, HEADS)
+    def _(head):
+        begin, inside = head_window(head, size, width)
+        query = jnp.where(inside, joined[:, pl.ds(begin, 256)], 0.0)
+        key = joined[:, pl.ds(pl.multiple_of(begin + width, 128), 256)]
+        value = joined[:, pl.ds(pl.multiple_of(begin + 2 * width, 128), 256)]
+        scores = matmul_nt(query, key) * scale + bar[...]
+        highest = jnp.max(scores, axis=1, keepdims=True)
+        powers = jnp.exp(scores - highest)
+        totals = jnp.sum(powers, axis=1, keepdims=True)
+        probs = (powers * (1.0 / totals)).astype(jnp.bfloat16)
+        found = mm(probs, value)
+        wide[:, pl.ds(begin, 256)] = jnp.where(inside, found, wide[:, pl.ds(begin, 256)])
+        lane = lane_index(rows, 128)
+        stats[...] = jnp.where(lane == head, highest + jnp.log(totals), stats[...])
+
+    out[...] = wide[...].astype(jnp.bfloat16)
+
+
+def attend(joined, slots):
+    rows, total = joined.shape
+    width = total // 3
+    return local_call(
+        attend_kernel,
+        [shaped((rows, width), jnp.bfloat16), shaped((rows, 128))],
+        [joined, slots.reshape(rows, 1), slots.reshape(1, rows)],
+        [],
+        [pltpu.VMEM((rows, rows), jnp.float32), pltpu.VMEM((rows, width), jnp.float32)],
+        40,
+    )
+
+
+def attend_back_kernel(joined, grad, stats, slots, slot_line, blocks, sums, bar, wide):
+    rows, width = grad.shape
+    size = width // HEADS
+    scale = 1.0 / math.sqrt(size)
+    bar[...] = jnp.where(slots[...] == slot_line[...], 0.0, -1e30)
+
+    @pl.loop(0, HEADS)
+    def _(head):
+        begin, inside = head_window(head, size, width)
+        columns = [pl.ds(pl.multiple_of(begin + part * width, 128), 256) for part in range(3)]
+        query = jnp.where(inside, joined[:, columns[0]], 0.0)
+        key = joined[:, columns[1]]
+        value = joined[:, columns[2]]
+        out_grad = jnp.where(inside, grad[:, columns[0]], 0.0)
+        lane = lane_index(rows, 128)
+        stat = jnp.sum(jnp.where(lane == head, stats[...], 0.0), axis=1, keepdims=True)
+        probs = jnp.exp(matmul_nt(query, key) * scale + bar[...] - stat)
+        prob_grad = matmul_nt(out_grad, value)
+        inner = jnp.sum(probs * prob_grad, axis=1, keepdims=True)
+        score_grad = (probs * (prob_grad - inner)).astype(jnp.bfloat16)
+        found = (
+            mm(score_grad, key) * scale,
+            matmul_tn(score_grad, query) * scale,
+            matmul_tn(probs.astype(jnp.bfloat16), out_grad),
+        )
+        for part in range(3):
+            wide[:, columns[part]] = jnp.where(inside, found[part], wide[:, columns[part]])
+
+    span = blocks.shape[2]
+    block_width = 3 * width // 4
+
+    def total(at):
+        sums[...] += jnp.sum(wide[at, :].astype(jnp.bfloat16).astype(jnp.float32), axis=0, keepdims=True)
+
+    sums[...] = jnp.zeros_like(sums)
+    by_rows(rows, 64, total)
+    for block in range(4):
+        begin, offset = window_of(block, block_width, 3 * width, span)
+
+        def cut(at):
+            moved = wide[at, begin : begin + span]
+            if offset:
+                moved = pltpu.roll(moved, span - offset, 1)
+            lane = lane_index(moved.shape[0], span)
+            blocks[block, at, :] = jnp.where(lane < block_width, moved, 0.0).astype(jnp.bfloat16)
+
+        by_rows(rows, 64, cut)
+
+
+def attend_back(joined, grad, stats, slots):
+    rows, total = joined.shape
+    span = -(-total // 4 // 128) * 128 + 128
+    return pl.pallas_call(
+        attend_back_kernel,
+        out_shape=[shaped((4, rows, span), jnp.bfloat16), shaped((1, total))],
+        scratch_shapes=[pltpu.VMEM((rows, rows), jnp.float32), pltpu.VMEM((rows, total), jnp.float32)],
+        compiler_params=pltpu.CompilerParams(vmem_limit_bytes=48 * 2**20),
+        cost_estimate=pl.CostEstimate(flops=0, bytes_accessed=0, transcendentals=0),
+    )(joined, grad, stats, slots.reshape(rows, 1), slots.reshape(1, rows))
+
+
+def branch_kernel(attended, start, slots, table, bias, *refs):
+    pieces, (branch, middle, normed, room, product, sems) = refs[:16], refs[16:]
+    rows, width = start.shape
+    columns = width // 4
+    for block in load_blocks(pieces, room, sems, True, natural=True, lanes=(width - WINDOW, width)):
+        wait_all(block)
+    for block in range(4):
+        product[...] = mm(attended[...], room[block])
+        begin, offset = window_of(block, columns, width, WINDOW)
+
+        def put(at):
+            moved = product[at, :]
+            if offset != WINDOW - columns:
+                moved = pltpu.roll(moved, columns + offset, 1)
+            lane = lane_index(moved.shape[0], WINDOW)
+            inside = (lane >= offset) & (lane < offset + columns)
+            branch[at, begin : begin + WINDOW] = jnp.where(
+                inside, moved, branch[at, begin : begin + WINDOW]
+            )
+
+        by_rows(rows, 64, put)
+
+    def finish(at):
+        slot = slots[at, :]
+        value = branch[at, :] + bias[...]
+        branch[at, :] = value
+        value = start[at, :] + slot_rows(slot, table, 2, width) * value
+        middle[at, :] = value
+        hat, _ = centred(value)
+        value = hat * (1.0 + slot_rows(slot, table, 4, width)) + slot_rows(slot, table, 3, width)
+        normed[at, :] = value.astype(jnp.bfloat16)
+
+    by_rows(rows, 64, finish)
+
+
+def branch_one(attended, start, slots, table, bias, pieces):
+    rows, width = start.shape
+    return local_call(
+        branch_kernel,
+        [shaped((rows, width)), shaped((rows, width)), shaped((rows, width), jnp.bfloat16)],
+        [attended, start, slots.reshape(rows, 1), table, bias],
+        pieces,
+        [
+            pltpu.VMEM((4, width, WINDOW), jnp.bfloat16),
+            pltpu.VMEM((rows, WINDOW), jnp.float32),
+            pltpu.SemaphoreType.DMA((32,)),
+        ],
+        48,
+    )
+
+
+def widen_kernel(normed, bias, *refs):
+    pieces, (hidden, before, room, sems) = refs[:16], refs[16:]
+    plane = place()[0]
+    rows = normed.shape[0]
+    blocks = load_blocks(pieces, room, sems, True)
+    for flip in range(4):
+        at = flipped(plane, flip)
+        wait_all(blocks[flip])
+        before[at] = mm(normed[...], room[flip]) + bias[at]
+
+        def act(some):
+            value = before[at, some, :]
+            bend = 1.0 + jnp.tanh(SLOPE * (value + 0.044715 * (value * value * value)))
+            hidden[at, some, :] = (value * (0.5 * bend)).astype(jnp.bfloat16)
+
+        by_rows(rows, 64, act)
+
+
+def widen(normed, bias, pieces):
+    rows, width = normed.shape
+    return pl.pallas_call(
+        widen_kernel,
+        out_shape=[shaped((4, rows, width), jnp.bfloat16), shaped((4, rows, width))],
+        in_specs=[pl.BlockSpec(memory_space=pltpu.VMEM)] * 2 + [pl.BlockSpec(memory_space=pl.ANY)] * 16,
+        scratch_shapes=[pltpu.VMEM((4, width, width), jnp.bfloat16), pltpu.SemaphoreType.DMA((32,))],
+        compiler_params=pltpu.CompilerParams(vmem_limit_bytes=56 * 2**20),
+        cost_estimate=pl.CostEstimate(flops=0, bytes_accessed=0, transcendentals=0),
+    )(normed, bias, *pieces)
+
+
+def narrow_kernel(hidden, middle, out_grad, slots, table, bias, before_all, *refs):
+    pieces, (mixed, branch_grad, pre_grad, sums, gate_sums, pre_sums, room, total, before, sems, more) = (
+        refs[:16],
+        refs[16:],
+    )
+    rows, width = middle.shape
+    blocks = load_blocks(pieces, room, sems, False)
+    copies = [pltpu.make_async_copy(before_all.at[part], before.at[part], more.at[part]) for part in range(4)]
+    for copy in copies:
+        copy.start()
+    for part in range(4):
+        wait_all(blocks[part])
+        term = matmul_nt(hidden[part], room[part])
+        if part == 0:
+            total[...] = term + bias[...]
+        else:
+            total[...] += term
+    sums[...] = jnp.zeros_like(sums)
+    gate_sums[...] = jnp.zeros_like(gate_sums)
+    pre_sums[...] = jnp.zeros_like(pre_sums)
+
+    def finish(at):
+        slot = slots[at, :]
+        gate = slot_rows(slot, table, 5, width)
+        branch = total[at, :]
+        grad = out_grad[at, :].astype(jnp.float32)
+        mixed[at, :] = (middle[at, :] + gate * branch).astype(jnp.bfloat16)
+        add_slots(gate_sums, slot, grad * branch)
+        value = (grad * gate).astype(jnp.bfloat16)
+        branch_grad[at, :] = value
+        sums[...] += jnp.sum(value.astype(jnp.float32), axis=0, keepdims=True)
+
+    by_rows(rows, 64, finish)
+    for part in range(4):
+        copies[part].wait()
+        total[...] = mm(branch_grad[...], room[part])
+
+        def act(at):
+            value = before[part, at, :]
+            square = value * value
+            bend = jnp.tanh(SLOPE * (value + 0.044715 * (square * value)))
+            slope = 0.5 * (1.0 + bend) + 0.5 * value * (1.0 - bend * bend) * (
+                SLOPE * (1.0 + 3.0 * 0.044715 * square)
+            )
+            value = (total[at, :] * slope).astype(jnp.bfloat16)
+            pre_grad[part, at, :] = value
+            pre_sums[part : part + 1, :] += jnp.sum(value.astype(jnp.float32), axis=0, keepdims=True)
+
+        by_rows(rows, 64, act)
+
+
+def narrow(hidden, before, middle, out_grad, slots, table, bias, pieces):
+    rows, width = middle.shape
+    return pl.pallas_call(
+        narrow_kernel,
+        out_shape=[
+            shaped((rows, width), jnp.bfloat16),
+            shaped((rows, width), jnp.bfloat16),
+            shaped((4, rows, width), jnp.bfloat16),
+            shaped((1, width)),
+            shaped((8, width)),
+            shaped((8, width)),
+        ],
+        in_specs=[pl.BlockSpec(memory_space=pltpu.VMEM)] * 6 + [pl.BlockSpec(memory_space=pl.ANY)] * 17,
+        scratch_shapes=[
+            pltpu.VMEM((4, width, width), jnp.bfloat16),
+            pltpu.VMEM((rows, width), jnp.float32),
+            pltpu.VMEM((4, rows, width), jnp.float32),
+            pltpu.SemaphoreType.DMA((32,)),
+            pltpu.SemaphoreType.DMA((4,)),
+        ],
+        compiler_params=pltpu.CompilerParams(vmem_limit_bytes=58 * 2**20),
+        cost_estimate=pl.CostEstimate(flops=0, bytes_accessed=0, transcendentals=0),
+    )(hidden, middle, out_grad, slots.reshape(rows, 1), table, bias, before, *pieces)
+
+
+def middle_kernel(pre_grad, middle, out_grad, branch, slots, table, *refs):
+    wide_pieces, joined_pieces = refs[:16], refs[16:32]
+    middle_grad, attended_grad, windows, slot_sums, sums, room, side, total, sems, more = refs[32:]
+    plane = place()[0]
+    rows, width = middle.shape
+    columns = width // 4
+    blocks = load_blocks(wide_pieces, room, sems, True)
+    side_blocks = load_blocks(
+        joined_pieces, side, more, True, natural=True, lanes=(width - WINDOW, width)
+    )
+    for flip in range(4):
+        wait_all(blocks[flip])
+        term = matmul_nt(pre_grad[flipped(plane, flip)], room[flip])
+        if flip == 0:
+            total[...] = term
+        else:
+            total[...] += term
+    slot_sums[...] = jnp.zeros_like(slot_sums)
+    sums[...] = jnp.zeros_like(sums)
+
+    def finish(at):
+        slot = slots[at, :]
+        grad = total[at, :]
+        hat, scale = centred(middle[at, :])
+        add_slots(slot_sums.at[1], slot, grad)
+        add_slots(slot_sums.at[2], slot, grad * hat)
+        grad = grad * (1.0 + slot_rows(slot, table, 4, width))
+        grad = out_grad[at, :].astype(jnp.float32) + norm_back(hat, scale, grad)
+        middle_grad[at, :] = grad
+        add_slots(slot_sums.at[0], slot, grad * branch[at, :])
+        value = (grad * slot_rows(slot, table, 2, width)).astype(jnp.bfloat16).astype(jnp.float32)
+        total[at, :] = value
+        sums[...] += jnp.sum(value, axis=0, keepdims=True)
+
+    by_rows(rows, 64, finish)
+    for block in range(4):
+        begin, offset = window_of(block, columns, width, WINDOW)
+
+        def cut(at):
+            moved = total[at, begin : begin + WINDOW]
+            if offset != WINDOW - columns:
+                moved = pltpu.roll(moved, (2 * WINDOW - columns - offset) % WINDOW, 1)
+            lane = lane_index(moved.shape[0], WINDOW)
+            moved = jnp.where(lane >= WINDOW - columns, moved, 0.0)
+            windows[block, at, :] = moved.astype(jnp.bfloat16)
+
+        by_rows(rows, 64, cut)
+    for block in side_blocks:
+        wait_all(block)
+    value = matmul_nt(windows[0], side[0])
+    for block in range(1, 4):
+        value = value + matmul_nt(windows[block], side[block])
+    attended_grad[...] = value.astype(jnp.bfloat16)
+
+
+def middle_back(pre_grad, middle, out_grad, branch, slots, table, wide_pieces, joined_pieces):
+    rows, width = middle.shape
+    return pl.pallas_call(
+        middle_kernel,
+        out_shape=[
+            shaped((rows, width)),
+            shaped((rows, width), jnp.bfloat16),
+            shaped((4, rows, WINDOW), jnp.bfloat16),
+            shaped((3, 8, width)),
+            shaped((1, width)),
+        ],
+        in_specs=[pl.BlockSpec(memory_space=pltpu.VMEM)] * 6 + [pl.BlockSpec(memory_space=pl.ANY)] * 32,
+        scratch_shapes=[
+            pltpu.VMEM((4, width, width), jnp.bfloat16),
+            pltpu.VMEM((4, width, WINDOW), jnp.bfloat16),
+            pltpu.VMEM((rows, width), jnp.float32),
+            pltpu.SemaphoreType.DMA((32,)),
+            pltpu.SemaphoreType.DMA((32,)),
+        ],
+        compiler_params=pltpu.CompilerParams(vmem_limit_bytes=58 * 2**20),
+        cost_estimate=pl.CostEstimate(flops=0, bytes_accessed=0, transcendentals=0),
+    )(pre_grad, middle, out_grad, branch, slots.reshape(rows, 1), table, *wide_pieces, *joined_pieces)
+
+
+def start_kernel(blocks, start, middle_grad, slots, table, *refs):
+    pieces, (grad_out, slot_sums, room, total, sems) = refs[:16], refs[16:]
+    plane = place()[0]
+    rows, width = start.shape
+    span = blocks.shape[2]
+    loads = load_blocks(pieces, room, sems, True, lanes=(0, span))
+    for flip in range(4):
+        wait_all(loads[flip])
+        term = matmul_nt(blocks[flipped(plane, flip)], room[flip])
+        if flip == 0:
+            total[...] = term
+        else:
+            total[...] += term
+    slot_sums[...] = jnp.zeros_like(slot_sums)
+
+    def finish(at):
+        slot = slots[at, :]
+        grad = total[at, :]
+        hat, scale = centred(start[at, :])
+        add_slots(slot_sums.at[0], slot, grad)
+        add_slots(slot_sums.at[1], slot, grad * hat)
+        grad = grad * (1.0 + slot_rows(slot, table, 1, width))
+        grad_out[at, :] = middle_grad[at, :] + norm_back(hat, scale, grad)
+
+    by_rows(rows, 64, finish)
+
+
+def start_back(blocks, start, middle_grad, slots, table, pieces):
+    rows, width = start.shape
+    return local_call(
+        start_kernel,
+        [shaped((rows, width)), shaped((2, 8, width))],
+        [blocks, start, middle_grad, slots.reshape(rows, 1), table],
+        pieces,
+        [
+            pltpu.VMEM((4, width, blocks.shape[2]), jnp.bfloat16),
+            pltpu.VMEM((rows, width), jnp.float32),
+            pltpu.SemaphoreType.DMA((32,)),
+        ],
+        48,
+    )
+
+
+SENT = ((0, (1, 3)), (0, (0, 2)), (1, (2, 3)), (1, (0, 1)))
+
+
+def outer_kernel(plane_major, lefts, spans, *refs):
+    left, right = refs[:lefts], refs[lefts : 2 * lefts]
+    outs, (room, sems) = refs[2 * lefts : 2 * lefts + 8], refs[2 * lefts + 8 :]
+    plane, _, core = place()
+    sides = (1 - core, core)
+    width = room.shape[1]
+    deep = width // 8
+    draining = [[], []]
+    for block in range(4):
+        slot = block % 2
+        wait_all(draining[slot])
+        index = flipped(plane, block) if plane_major else block
+        if lefts == 1:
+            room[slot] = mm(left[0][...], right[0][index]).astype(jnp.bfloat16)
+        else:
+            low, high = spans
+            head = mm(left[0][...], right[0][index])
+            tail = mm(left[1][...], right[1][index])
+            room[slot, :, :high] = head[:, :high].astype(jnp.bfloat16)
+            room[slot, :, high:low] = (head[:, high:low] + tail[:, : low - high]).astype(jnp.bfloat16)
+            room[slot, :, low:] = tail[:, low - high :].astype(jnp.bfloat16)
+        copies = []
+        for kind in range(2):
+            for number, (half, flips) in enumerate(SENT):
+                target = outs[4 * kind + number]
+                for place_in, flip in enumerate(flips):
+                    for step in range(2):
+                        depth = 2 * half + step
+                        if plane_major:
+                            if flip != block:
+                                continue
+                            row = depth * 2 + sides[kind]
+                        else:
+                            if depth != block:
+                                continue
+                            row = flipped(plane, flip) * 2 + sides[kind]
+                        source = room.at[slot, pl.ds(pl.multiple_of(row * deep, 16), deep)]
+                        copies.append(
+                            pltpu.make_async_copy(
+                                source, target.at[place_in, step], sems.at[slot, len(copies)]
+                            )
+                        )
+        for copy in copies:
+            copy.start()
+        draining[slot] = copies
+    wait_all(draining[0])
+    wait_all(draining[1])
+
+
+def outer(plane_major, lefts, rights, spans=None):
+    width = lefts[0].shape[0]
+    deep = width // 8
+    return pl.pallas_call(
+        partial(outer_kernel, plane_major, len(lefts), spans),
+        out_shape=[shaped((2, 2, deep, width), jnp.bfloat16)] * 8,
+        in_specs=[pl.BlockSpec(memory_space=pltpu.VMEM)] * (2 * len(lefts)),
+        out_specs=[pl.BlockSpec(memory_space=pl.ANY)] * 8,
+        scratch_shapes=[
+            pltpu.VMEM((2, width, width), jnp.bfloat16),
+            pltpu.SemaphoreType.DMA((2, 8)),
+        ],
+        compiler_params=pltpu.CompilerParams(vmem_limit_bytes=48 * 2**20),
+        cost_estimate=pl.CostEstimate(flops=0, bytes_accessed=0, transcendentals=0),
+    )(*lefts, *rights)
+
+
+def low_bits(value):
+    return value.astype(jnp.bfloat16)
+
+
+def wide(value):
+    return value.astype(jnp.float32)
+
+
+def scatter_pieces(pieces):
+    depth = place()[1]
+    summed = [wide(own) + wide(swap(other, "core")) for other, own in zip(pieces[:4], pieces[4:])]
+    totals = []
+    for half, (first, _, second, _) in enumerate(HALF_ORDERS):
+        sent, kept = summed[2 * half], summed[2 * half + 1]
+        arrived = wide(swap(low_bits(sent), first))
+        across = swap(low_bits(kept[1] + arrived[1]), second)
+        totals.append(kept[0] + arrived[0] + wide(across))
+    total = jnp.concatenate(totals)
+    result = pick(total, depth)
+    for turn in (1, 2, 3):
+        result = result + wide(swap(low_bits(pick(total, (depth - turn) % 4)), turn))
+    return result
+
+
+def box_device(
+    tokens,
+    condition,
+    kept_index,
+    segment,
+    grid_side,
+    ada_weight,
+    ada_bias,
+    attn_weight,
+    attn_bias,
+    proj_weight,
+    out_bias,
+    up_weight,
+    up_bias,
+    down_weight,
+    grad_out,
+):
+    rows, width = tokens.shape
+    slot_count = condition.shape[0]
+    core = place()[2]
+    columns = attn_weight.shape[1]
+    joined_line = gather_line(jnp.concatenate([attn_weight, proj_weight], axis=1))
+    turned = down_weight.T.reshape(2, up_weight.shape[0], down_weight.shape[0])
+    mine, theirs = pick(turned, core), pick(turned, 1 - core)
+    arrived = swap(theirs, "core")
+    down_shard = jnp.where(
+        core == 0,
+        jnp.concatenate([mine, arrived], axis=1),
+        jnp.concatenate([arrived, mine], axis=1),
+    )
+    up_shard, _ = lax.optimization_barrier((up_weight, joined_line[1:]))
+    up_line = gather_line(up_shard)
+    down_shard, _ = lax.optimization_barrier((down_shard, up_line[1:]))
+    down_line = gather_line(down_shard)
+
+    def flat(pieces):
+        return [piece for side in pieces for found in side for piece in found]
+
+    joined_pieces = flat(gather_plane(joined_line))
+    up_pieces = flat(gather_plane(up_line))
+    down_pieces = flat(gather_plane(down_line))
+
+    slot_ids = jnp.arange(slot_count, dtype=jnp.int32)
+    side_rows = jnp.sum(jnp.where(segment[:, None] == slot_ids[None, :], grid_side[None, :], 0), axis=1)
+    start = tokens.astype(jnp.float32) + position_code(kept_index, side_rows, width)
+    silu_cond, silu_back = jax.vjp(jax.nn.silu, condition.astype(jnp.float32))
+    silu_bf = silu_cond.astype(jnp.bfloat16)
+    silu_all, (ada_bfull, attn_bfull, out_bfull, up_bfull) = gather_small(
+        silu_bf, (ada_bias, attn_bias, out_bias, up_bias)
+    )
+    modulation, silu_part = modulate_slots(silu_all, ada_weight, ada_bfull)
+    table = jnp.pad(modulation, ((0, 8 - slot_count), (0, 0)))
+
+    def own_rows(part):
+        return sum(
+            jnp.where(segment[:, None] == slot, modulation[slot, part * width : (part + 1) * width], 0.0)
+            for slot in range(slot_count)
+        )
+
+    normed1 = norm_modulate(start, own_rows(0), own_rows(1)).astype(jnp.bfloat16)
+    zeros = jnp.zeros((width,), jnp.bfloat16)
+    joined_bias = jnp.concatenate([attn_bfull[:width], zeros, attn_bfull[width:]])
+    joined = project(normed1, joined_bias.astype(jnp.float32)[None], joined_pieces)
+    attended, stats = attend(joined, segment)
+    out_bias_f = out_bfull.astype(jnp.float32)
+    branch1, middle, normed2 = branch_one(
+        attended, start, segment, table, out_bias_f[None, :width], joined_pieces
+    )
+    hidden, before = widen(normed2, up_bfull.astype(jnp.float32).reshape(4, 1, -1), up_pieces)
+    mixed, grad_branch2, pre_grad, branch2_sums, gate2_sums, pre_sums = narrow(
+        hidden, before, middle, grad_out, segment, table, out_bias_f[None, width:], down_pieces
+    )
+    down_total = scatter_pieces(outer(False, [grad_branch2.T], [hidden]))
+    up_weight_grad = scatter_pieces(outer(True, [normed2.T], [pre_grad]))
+    half = down_total.shape[1] // 2
+    cut = down_total.reshape(-1, 2, half).transpose(1, 0, 2)
+    mine, theirs = pick(cut, core), pick(cut, 1 - core)
+    arrived = swap(theirs, "core")
+    down_weight_grad = jnp.where(
+        core == 0, jnp.concatenate([mine, arrived]), jnp.concatenate([arrived, mine])
+    ).T
+    middle_grad, attended_grad, windows, slot_sums2, branch1_sums = middle_back(
+        pre_grad, middle, grad_out, branch1, segment, table, up_pieces, joined_pieces
+    )
+    blocks, joined_sums = attend_back(joined, attended_grad, stats, segment)
+    joined_total = scatter_pieces(
+        outer(
+            True,
+            [normed1.T, attended.T],
+            [blocks, windows],
+            (blocks.shape[2], width - WINDOW),
+        )
+    )
+    tokens_grad, slot_sums1 = start_back(blocks, start, middle_grad, segment, table, joined_pieces)
+    modulation_grad = jnp.concatenate(
+        [slot_sums1[0], slot_sums1[1], slot_sums2[0], slot_sums2[1], slot_sums2[2], gate2_sums], axis=1
+    )[:slot_count].astype(jnp.bfloat16)
+    joined_sums = joined_sums[0]
+    terms = (
+        jnp.concatenate([joined_sums[:width], joined_sums[2 * width :]]),
+        jnp.concatenate([branch1_sums[0], branch2_sums[0]]),
+        pre_sums[:4].reshape(-1),
+    )
+    ada_weight_grad, ada_bias_grad, silu_grad, bias_grads = modulation_back(
+        modulation_grad, silu_part, ada_weight, terms
+    )
+    attn_bias_grad, out_bias_grad, up_bias_grad = bias_grads
+    return (
+        mixed,
+        tokens_grad,
+        silu_back(silu_grad)[0],
+        ada_weight_grad,
+        ada_bias_grad,
+        joined_total[:, :columns],
+        attn_bias_grad,
+        joined_total[:, columns:],
+        out_bias_grad,
+        up_weight_grad,
+        up_bias_grad,
+        down_weight_grad,
+    )
+
+
 def per_device(
     tokens,
     condition,
@@ -543,6 +1121,24 @@
     down_weight,
     grad_out,
 ):
+    if on_box():
+        return box_device(
+            tokens,
+            condition,
+            kept_index,
+            segment,
+            grid_side,
+            ada_weight,
+            ada_bias,
+            attn_weight,
+            attn_bias,
+            proj_weight,
+            out_bias,
+            up_weight,
+            up_bias,
+            down_weight,
+            grad_out,
+        )
     model_width = tokens.shape[1]
     slot_count = condition.shape[0]
     planes = lax.axis_size("dp")
@@ -603,7 +1199,7 @@
     out_grad = grad_out.astype(jnp.float32)
     grad_gate_two = out_grad * branch2
     grad_branch2 = (out_grad * gate_two).astype(jnp.bfloat16)
-    down_weight_grad = scatter_down(jnp.stack(hidden_parts), grad_branch2)
+    down_weight_grad = scatter_whole(matmul_tn(jnp.concatenate(hidden_parts, axis=1), grad_branch2))
     pre_parts = []
     for part in range(planes):
         hidden_grad = jnp.dot(grad_branch2, down_w[part], preferred_element_type=jnp.float32)

time: 868 us -> 810 us (0.933)
  Pallas kernels: 95.4 us -> 317 us
  matrix products: 188 us -> 2.91 us
  other arithmetic: 95.8 us -> 41.6 us
  local copies, waits for them, and re-layouts: 117 us -> 70.4 us
    pallas_call x3 -> x11, Pallas kernels: 12.9 us -> 233 us  [the longest x4 77.9 us: local_call(): pl.pallas_call(kernel, out_shape=outs, in_specs=[pl.BlockSpec(memory_spac...]
    dot_general x21 -> x0, matrix products: 87.4 us -> none  [the longest x4 13.5 us: per_device(): jnp.dot(grad_branch2, down_w[part], preferred_element_type=jnp.float32)]
    dot_general x33 -> x1, matrix products: 57.6 us -> 2.26 us  [matmul_tn(): lax.dot_general(first_matrix, second_matrix, (((0,), (0,)), ((), ())), pr...]
    dot_general x14 -> x1, matrix products: 43.1 us -> 0.31 us  [matmul_nt(): lax.dot_general(first_matrix, second_matrix, (((1,), (1,)), ((), ())), pr...]
    slice x31 -> x8, local copies, waits for them, and re-layouts: 36.2 us -> 3.65 us  [the longest x1 0.82 us: box_device(): joined_total[:, :columns]]
    convert_element_type x29 -> x27, other arithmetic: 30.6 us -> 15 us  [the longest x15 5.83 us: low_bits(): return value.astype(jnp.bfloat16)]
    reduce_sum x5 -> x1, other arithmetic: 14.6 us -> 0.09 us  [box_device(): jnp.sum(jnp.where(segment[:, None] == slot_ids[None, :], grid_side[None,...]
    unnamed x324 -> x261, local copies, waits for them, and re-layouts: 40.8 us -> 30.3 us
  transfers between devices with their start and end apart: 104 -> 86, of which waited for: 33 -> 31; matrix products, arithmetic and copies ran while one was open for 44% -> 11% of each run, Pallas kernels for 11% -> 21%
where the time goes in v3:
time: 810 us; the launch traced here: 802 us
  Pallas kernels  317 us (39%)
  waiting for transfers between devices  285 us (35%)
  starting transfers between devices  81.6 us (10%)
  local copies, waits for them, and re-layouts  70.4 us (9%)
  other arithmetic  41.6 us (5%)
    ppermute x86, waiting for transfers between devices, swap(): lax.ppermute(values, AXES, [(index, neighbour(index, axis)) for index in...  285 us
    pallas_call x4, Pallas kernels, exchange(): pl.pallas_call(partial(trade, one_for_all), out_shape=jax.ShapeDtypeStruc...  84.8 us
    ppermute x86, starting transfers between devices, swap(): lax.ppermute(values, AXES, [(index, neighbour(index, axis)) for index in...  81.6 us
    pallas_call x4, Pallas kernels, local_call(): pl.pallas_call(kernel, out_shape=outs, in_specs=[pl.BlockSpec(memory_spac...  77.9 us
    pallas_call x3, Pallas kernels, outer(): pl.pallas_call(partial(outer_kernel, plane_major, len(lefts), spans), out...  39.5 us
    pallas_call x1, Pallas kernels, narrow(): pl.pallas_call(narrow_kernel, out_shape=[shaped((rows, width), jnp.bfloat...  35.4 us
    pallas_call x1, Pallas kernels, middle_back(): pl.pallas_call(middle_kernel, out_shape=[shaped((rows, width)), shaped((r...  31.1 us
    unnamed x261, local copies, waits for them, and re-layouts  30.3 us
  transfers between devices with their start and end apart: 86, of which 31 were waited for; matrix products, arithmetic and copies ran while one was open for 11% of the time, Pallas kernels for 21%

profile of v3, /device:TPU:0, one launch (start us, length us, event | category | flops | bytes accessed | tf_op | source)
XLA Modules:
  0.0 801.6 jit_solution(1380081330159283407)
XLA Ops:
  15.0 30.5 %shard_map.238 = bf16[32,16,384]{2,1,0:T(8,128)(2,1)S(1)} custom-call(bf16[16,384]{1,0:T(8,128)(2,1)S(1)} %reshape.230.values), custom_call_target="tpu_custom_call" | custom-call | bytes 3145728 | tf_op jit(solution)/shard_map/pallas_call | solution.py:281
  46.9 25.0 %shard_map.239 = f32[32,4,1728]{2,1,0:T(4,128)S(1)} custom-call(f32[32,4,1728]{2,1,0:T(4,128)S(1)} %reshape.233.values), custom_call_target="tpu_custom_call" | custom-call | bytes 7077888 | tf_op jit(solution)/shard_map/pallas_call | solution.py:281
  109.5 8.0 collective-permute-start.35
  126.6 16.1 %collective-permute-done.36 = bf16[144,1152]{1,0:T(8,128)(2,1)S(1)} collective-permute-done((bf16[144,1152]{1,0:T(8,128)(2,1)S(1)}, bf16[144,1152]{1,0:T(8,128)(2,1)S(1)}, u32[]{:S(2)}, u32[]{:S(2)}) %collective-permute-start.36) | collective-permute-done | bytes 331808 | tf_op jit(solution)/shard_map/ppermute | solution.py:149
  143.0 10.3 %collective-permute-done.37 = bf16[144,1152]{1,0:T(8,128)(2,1)S(1)} collective-permute-done((bf16[144,1152]{1,0:T(8,128)(2,1)S(1)}, bf16[144,1152]{1,0:T(8,128)(2,1)S(1)}, u32[]{:S(2)}, u32[]{:S(2)}) %collective-permute-start.37) | collective-permute-done | bytes 331808 | tf_op jit(solution)/shard_map/ppermute | solution.py:149
  157.6 13.5 %collective-permute-done.4.refs_2_.refs_18_ = bf16[2,144,1152]{2,1,0:T(8,128)(2,1)S(1)} collective-permute-done((bf16[2,144,1152]{2,1,0:T(8,128)(2,1)S(1)}, bf16[2,144,1152]{2,1,0:T(8,128)(2,1)S(1)}, u32[]{:S(2)}, u32[]{:S(2)}) %collective-permute-start.4) | collective-permute-done | bytes 663584 | tf_op jit(solution)/shard_map/ppermute | solution.py:149
  174.4 11.1 %collective-permute-done.24.refs_6_ = bf16[2,144,1152]{2,1,0:T(8,128)(2,1)} collective-permute-done((bf16[2,144,1152]{2,1,0:T(8,128)(2,1)S(1)}, bf16[2,144,1152]{2,1,0:T(8,128)(2,1)}, u32[]{:S(2)}, u32[]{:S(2)}) %collective-permute-start.24) | collective-permute-done | bytes 663584 | tf_op jit(solution)/shard_map/ppermute | solution.py:149
  188.4 8.2 %collective-permute-done.21.refs_2_ = bf16[2,144,1152]{2,1,0:T(8,128)(2,1)} collective-permute-done((bf16[2,144,1152]{2,1,0:T(8,128)(2,1)S(1)}, bf16[2,144,1152]{2,1,0:T(8,128)(2,1)}, u32[]{:S(2)}, u32[]{:S(2)}) %collective-permute-start.21) | collective-permute-done | bytes 663584 | tf_op jit(solution)/shard_map/ppermute | solution.py:149
  201.9 9.1 %collective-permute-done.8.refs_7_.refs_23_ = bf16[2,144,1152]{2,1,0:T(8,128)(2,1)S(1)} collective-permute-done((bf16[2,144,1152]{2,1,0:T(8,128)(2,1)S(1)}, bf16[2,144,1152]{2,1,0:T(8,128)(2,1)S(1)}, u32[]{:S(2)}, u32[]{:S(2)}) %collective-permute-start.8) | collective-permute-done | bytes 663584 | tf_op jit(solution)/shard_map/ppermute | solution.py:149
  216.5 23.5 %collective-permute-done.5.refs_3_.refs_19_ = bf16[2,144,1152]{2,1,0:T(8,128)(2,1)S(1)} collective-permute-done((bf16[2,144,1152]{2,1,0:T(8,128)(2,1)S(1)}, bf16[2,144,1152]{2,1,0:T(8,128)(2,1)S(1)}, u32[]{:S(2)}, u32[]{:S(2)}) %collective-permute-start.5) | collective-permute-done | bytes 663584 | tf_op jit(solution)/shard_map/ppermute | solution.py:149
  281.8 7.4 collective-permute-done.43.refs_7_
  295.2 17.4 %shard_map.240.joined = bf16[512,3456]{1,0:T(8,128)(2,1)} custom-call(bf16[512,1152]{1,0:T(8,128)(2,1)} %copy.89.normed, f32[1,3456]{1,0:T(1,128)} %fusion.83.bias, bf16[2,144,1152]{2,1,0:T(8,128)(2,1)} %copy-done.7, bf16[2,144,1152]{2,1,0:T(8,128)(2,1)} %copy-done.21, bf16[2,144,1152]{2,1,0:T(8,128)(2,1)} %copy-done.18, bf16[2,144,1152]{2,1,0:T(8,128)(2,1)} %copy-done.27, ...), custom_call_target="tpu_custom_call" | custom-call | tf_op jit(solution)/shard_map/pallas_call | solution.py:367
  314.6 16.6 %shard_map.241 = (bf16[512,1152]{1,0:T(8,128)(2,1)S(1)}, f32[512,128]{1,0:T(8,128)S(1)}) custom-call(bf16[512,3456]{1,0:T(8,128)(2,1)S(1)} %copy-done.2, s32[512,1]{1,0:T(8,128)S(1)} %copy.90.slots, s32[1,512]{1,0:T(1,128)S(1)} %bitcast.185), custom_call_target="tpu_custom_call" | custom-call | tf_op jit(solution)/shard_map/pallas_call | solution.py:367
  340.7 24.8 %shard_map.242 = (f32[512,1152]{1,0:T(8,128)}, f32[512,1152]{1,0:T(8,128)}, bf16[512,1152]{1,0:T(8,128)(2,1)}) custom-call(bf16[512,1152]{1,0:T(8,128)(2,1)} %copy-done.33, f32[512,1152]{1,0:T(8,128)} %copy.91.start, s32[512,1]{1,0:T(8,128)S(1)} %copy.90.slots, f32[8,6912]{1,0:T(8,128)S(1)} %copy-done.30, f32[1,1152]{1,0:T(1,128)S(1)} %broadcast_in_dim.142.bias, ...), custom_call_target="tpu_custom_call" | custom-call | tf_op jit(solution)/shard_map/pallas_call | solution.py:367
  367.0 20.0 %shard_map.243 = (bf16[4,512,1152]{2,1,0:T(8,128)(2,1)}, f32[4,512,1152]{2,1,0:T(8,128)}) custom-call(bf16[512,1152]{1,0:T(8,128)(2,1)} %get-tuple-element.61.normed, f32[4,1,1152]{2,1,0:T(1,128)} %reshape.248.bias, bf16[2,144,1152]{2,1,0:T(8,128)(2,1)} %copy-done.51, bf16[2,144,1152]{2,1,0:T(8,128)(2,1)} %collective-permute-done.20.refs_1_, ...), custom_call_target="tpu_custom_call" | custom-call | tf_op jit(solution)/shard_map/pallas_call | solution.py:683
  387.1 35.4 %shard_map.244 = (bf16[512,1152]{1,0:T(8,128)(2,1)}, bf16[512,1152]{1,0:T(8,128)(2,1)}, bf16[4,512,1152]{2,1,0:T(8,128)(2,1)}, f32[1,1152]{1,0:T(1,128)}, f32[8,1152]{1,0:T(8,128)}, /*index=5*/f32[8,1152]{1,0:T(8,128)}) custom-call(bf16[4,512,1152]{2,1,0:T(8,128)(2,1)} %get-tuple-element.63.hidden.refs_1_, f32[512,1152]{1,0:T(8,128)} %get-tuple-element.64.middle, ...), custom_call_target="tpu_custom_call" | custom-call | tf_op jit(solution)/shard_map/pallas_call | solution.py:746
  422.6 31.1 %shard_map.245 = (f32[512,1152]{1,0:T(8,128)}, bf16[512,1152]{1,0:T(8,128)(2,1)}, bf16[4,512,512]{2,1,0:T(8,128)(2,1)}, f32[3,8,1152]{2,1,0:T(8,128)}, f32[1,1152]{1,0:T(1,128)}) custom-call(bf16[4,512,1152]{2,1,0:T(8,128)(2,1)} %get-tuple-element.68.pre_grad.refs_1_, f32[512,1152]{1,0:T(8,128)} %get-tuple-element.64.middle, bf16[512,1152]{1,0:T(8,128)(2,1)} %out_grad.3, ...), custom_call_target="tpu_custom_call" | custom-call | tf_op jit(solution)/shard_map/pallas_call | solution.py:826
  457.0 28.7 %shard_map.246 = (bf16[4,512,1024]{2,1,0:T(8,128)(2,1)}, f32[1,3456]{1,0:T(1,128)S(1)}) custom-call(bf16[512,3456]{1,0:T(8,128)(2,1)S(1)} %copy-done.3, bf16[512,1152]{1,0:T(8,128)(2,1)S(1)} %copy-done.35, f32[512,128]{1,0:T(8,128)S(1)} %copy-done.37, s32[512,1]{1,0:T(8,128)S(1)} %copy-done.11, s32[1,512]{1,0:T(1,128)S(1)} %bitcast.186), custom_call_target="tpu_custom_call" | custom-call | tf_op jit(solution)/shard_map/pallas_call | solution.py:603
  485.8 19.2 %shard_map.247 = (f32[512,1152]{1,0:T(8,128)}, f32[2,8,1152]{2,1,0:T(8,128)S(1)}) custom-call(bf16[4,512,1024]{2,1,0:T(8,128)(2,1)} %get-tuple-element.72.blocks.refs_2_, f32[512,1152]{1,0:T(8,128)} %copy.91.start, f32[512,1152]{1,0:T(8,128)} %get-tuple-element.73.middle_grad, s32[512,1]{1,0:T(8,128)S(1)} %copy-done.11, f32[8,6912]{1,0:T(8,128)S(1)} %copy-done.31, ...), custom_call_target="tpu_custom_call" | custom-call | tf_op jit(solution)/shard_map/pallas_call | solution.py:367
  505.5 18.8 %shard_map.248 = bf16[32,16,432]{2,1,0:T(8,128)(2,1)S(1)} custom-call(bf16[32,16,432]{2,1,0:T(8,128)(2,1)S(1)} %bitcast.180), custom_call_target="tpu_custom_call" | custom-call | bytes 3538944 | tf_op jit(solution)/shard_map/pallas_call | solution.py:281
  527.2 12.7 %shard_map.252 = (bf16[2,2,144,1152]{3,2,1,0:T(8,128)(2,1)S(1)}, bf16[2,2,144,1152]{3,2,1,0:T(8,128)(2,1)}, bf16[2,2,144,1152]{3,2,1,0:T(8,128)(2,1)S(1)}, bf16[...) custom-call(bf16[1152,512]{1,0:T(8,128)(2,1)S(1)} %bitcast.179, ...), custom_call_target="tpu_custom_call" | custom-call | tf_op jit(solution)/shard_map/pallas_call | solution.py:946
  542.1 10.4 %shard_map.249 = f32[32,8,128]{2,1,0:T(8,128)S(1)} custom-call(f32[32,8,128]{2,1,0:T(8,128)S(1)} %bitcast.182), custom_call_target="tpu_custom_call" | custom-call | bytes 1048576 | tf_op jit(solution)/shard_map/pallas_call | solution.py:281
  555.6 13.6 %shard_map.250 = (bf16[2,2,144,1152]{3,2,1,0:T(8,128)(2,1)S(1)}, bf16[2,2,144,1152]{3,2,1,0:T(8,128)(2,1)S(1)}, bf16[2,2,144,1152]{3,2,1,0:T(8,128)(2,1)}, bf16[...) custom-call(bf16[1152,512]{1,0:T(8,128)(2,1)S(1)} %copy-done.34, ...), custom_call_target="tpu_custom_call" | custom-call | tf_op jit(solution)/shard_map/pallas_call | solution.py:946
  569.7 13.2 %shard_map.251 = (bf16[2,2,144,1152]{3,2,1,0:T(8,128)(2,1)S(1)}, bf16[2,2,144,1152]{3,2,1,0:T(8,128)(2,1)S(1)}, bf16[2,2,144,1152]{3,2,1,0:T(8,128)(2,1)S(1)}, b...) custom-call(bf16[1152,512]{1,0:T(8,128)(2,1)S(1)} %bitcast.177, ...), custom_call_target="tpu_custom_call" | custom-call | tf_op jit(solution)/shard_map/pallas_call | solution.py:946
  606.5 24.9 %collective-permute-done.76 = bf16[2,2,144,1152]{3,2,1,0:T(8,128)(2,1)S(1)} collective-permute-done((bf16[2,2,144,1152]{3,2,1,0:T(8,128)(2,1)S(1)}, bf16[2,2,144,1152]{3,2,1,0:T(8,128)(2,1)S(1)}, u32[]{:S(2)}, u32[]{:S(2)}) %collective-permute-start.76) | collective-permute-done | bytes 1327136 | tf_op jit(solution)/shard_map/ppermute | solution.py:149
  634.2 25.6 %collective-permute-done.54 = bf16[2,2,144,1152]{3,2,1,0:T(8,128)(2,1)S(1)} collective-permute-done((bf16[2,2,144,1152]{3,2,1,0:T(8,128)(2,1)S(1)}, bf16[2,2,144,1152]{3,2,1,0:T(8,128)(2,1)S(1)}, u32[]{:S(2)}, u32[]{:S(2)}) %collective-permute-start.54) | collective-permute-done | bytes 1327136 | tf_op jit(solution)/shard_map/ppermute | solution.py:149
  662.6 25.6 %collective-permute-done.65 = bf16[2,2,144,1152]{3,2,1,0:T(8,128)(2,1)S(1)} collective-permute-done((bf16[2,2,144,1152]{3,2,1,0:T(8,128)(2,1)S(1)}, bf16[2,2,144,1152]{3,2,1,0:T(8,128)(2,1)S(1)}, u32[]{:S(2)}, u32[]{:S(2)}) %collective-permute-start.65) | collective-permute-done | bytes 1327136 | tf_op jit(solution)/shard_map/ppermute | solution.py:149
  691.1 12.9 %collective-permute-done.77 = bf16[2,144,1152]{2,1,0:T(8,128)(2,1)S(1)} collective-permute-done((bf16[2,144,1152]{2,1,0:T(8,128)(2,1)S(1)}, bf16[2,144,1152]{2,1,0:T(8,128)(2,1)S(1)}, u32[]{:S(2)}, u32[]{:S(2)}) %collective-permute-start.77) | collective-permute-done | bytes 663584 | tf_op jit(solution)/shard_map/ppermute | solution.py:149
  708.5 9.7 %collective-permute-done.55 = bf16[2,144,1152]{2,1,0:T(8,128)(2,1)S(1)} collective-permute-done((bf16[2,144,1152]{2,1,0:T(8,128)(2,1)S(1)}, bf16[2,144,1152]{2,1,0:T(8,128)(2,1)S(1)}, u32[]{:S(2)}, u32[]{:S(2)}) %collective-permute-start.55) | collective-permute-done | bytes 663584 | tf_op jit(solution)/shard_map/ppermute | solution.py:149
  722.4 9.0 %collective-permute-done.66 = bf16[2,144,1152]{2,1,0:T(8,128)(2,1)S(1)} collective-permute-done((bf16[2,144,1152]{2,1,0:T(8,128)(2,1)S(1)}, bf16[2,144,1152]{2,1,0:T(8,128)(2,1)S(1)}, u32[]{:S(2)}, u32[]{:S(2)}) %collective-permute-start.66) | collective-permute-done | bytes 663584 | tf_op jit(solution)/shard_map/ppermute | solution.py:149
  736.9 16.9 %collective-permute-done.83 = bf16[144,1152]{1,0:T(8,128)(2,1)S(1)} collective-permute-done((bf16[144,1152]{1,0:T(8,128)(2,1)S(1)}, bf16[144,1152]{1,0:T(8,128)(2,1)S(1)}, u32[]{:S(2)}, u32[]{:S(2)}) %collective-permute-start.83) | collective-permute-done | bytes 331808 | tf_op jit(solution)/shard_map/ppermute | solution.py:149
  765.4 18.7 %collective-permute-done.61 = bf16[144,1152]{1,0:T(8,128)(2,1)S(1)} collective-permute-done((bf16[144,1152]{1,0:T(8,128)(2,1)S(1)}, bf16[144,1152]{1,0:T(8,128)(2,1)S(1)}, u32[]{:S(2)}, u32[]{:S(2)}) %collective-permute-start.61) | collective-permute-done | bytes 331808 | tf_op jit(solution)/shard_map/ppermute | solution.py:149
  (545 shorter events, 230.7 us)
Async XLA Ops:
  2.7 79.9 %collective-permute-start.2 = (bf16[144,1152]{1,0:T(8,128)(2,1)}, bf16[144,1152]{1,0:T(8,128)(2,1)}, u32[]{:S(2)}, u32[]{:S(2)}) collective-permute-start(bf16[144,1152]{1,0:T(8,128)(2,1)} %get-tuple-element.119), channel_id=1, source_target_pairs={{0,2},{1,3},{2,4},{3,5},{4,6},{5,7},{6,0},{7,1},{8,10},{9,11},{10,... | collective-permute-start | bytes 995336 | tf_op jit(solution)/shard_map/ppermute | solution.py:149
  5.7 76.9 %collective-permute-start.1 = (bf16[144,1152]{1,0:T(8,128)(2,1)}, bf16[144,1152]{1,0:T(8,128)(2,1)}, u32[]{:S(2)}, u32[]{:S(2)}) collective-permute-start(bf16[144,1152]{1,0:T(8,128)(2,1)} %get-tuple-element.119), channel_id=1, source_target_pairs={{0,4},{1,5},{2,6},{3,7},{4,0},{5,1},{6,2},{7,3},{8,12},{9,13},{10,... | collective-permute-start | bytes 995336 | tf_op jit(solution)/shard_map/ppermute | solution.py:149
  8.3 74.3 %collective-permute-start = (bf16[144,1152]{1,0:T(8,128)(2,1)}, bf16[144,1152]{1,0:T(8,128)(2,1)}, u32[]{:S(2)}, u32[]{:S(2)}) collective-permute-start(bf16[144,1152]{1,0:T(8,128)(2,1)} %get-tuple-element.119), channel_id=1, source_target_pairs={{0,6},{1,7},{2,0},{3,1},{4,2},{5,3},{6,4},{7,5},{8,14},{9,15},{10,... | collective-permute-start | bytes 995336 | tf_op jit(solution)/shard_map/ppermute | solution.py:149
  11.4 69.7 %collective-permute-start.34 = (bf16[144,576]{1,0:T(8,128)(2,1)}, bf16[144,576]{1,0:T(8,128)(2,1)}, u32[]{:S(2)}, u32[]{:S(2)}) collective-permute-start(bf16[144,576]{1,0:T(8,128)(2,1)} %get-tuple-element.142), channel_id=1, source_target_pairs={{0,1},{1,0},{2,3},{3,2},{4,5},{5,4},{6,7},{7,6},{8,9},{9,8},{10,11... | collective-permute-start | bytes 497672 | tf_op jit(solution)/shard_map/ppermute | solution.py:149
  101.4 52.3 %collective-permute-start.13 = (bf16[2,144,1152]{2,1,0:T(8,128)(2,1)S(1)}, bf16[2,144,1152]{2,1,0:T(8,128)(2,1)S(1)}, u32[]{:S(2)}, u32[]{:S(2)}) collective-permute-start(bf16[2,144,1152]{2,1,0:T(8,128)(2,1)S(1)} %get-tuple-element.135.refs_4_.refs_20_), channel_id=1, source_target_pairs={{0,1},{1,0},{2,3},{3,2},{4,5},{5,4},{6,7},{7,6},{8,9},{9,8},{10,11... | collective-permute-start | bytes 1990664 | tf_op jit(solution)/shard_map/ppermute | solution.py:149
  101.5 53.8 %collective-permute-start.7 = (bf16[2,144,1152]{2,1,0:T(8,128)(2,1)S(1)}, bf16[2,144,1152]{2,1,0:T(8,128)(2,1)S(1)}, u32[]{:S(2)}, u32[]{:S(2)}) collective-permute-start(bf16[2,144,1152]{2,1,0:T(8,128)(2,1)S(1)} %get-tuple-element.135.refs_4_.refs_20_), channel_id=1, source_target_pairs={{0,16},{1,17},{2,18},{3,19},{4,20},{5,21},{6,22},{7,23},{8,24},{9,... | collective-permute-start | bytes 1990664 | tf_op jit(solution)/shard_map/ppermute | solution.py:149
  102.1 53.3 %collective-permute-start.6 = (bf16[2,144,1152]{2,1,0:T(8,128)(2,1)S(1)}, bf16[2,144,1152]{2,1,0:T(8,128)(2,1)S(1)}, u32[]{:S(2)}, u32[]{:S(2)}) collective-permute-start(bf16[2,144,1152]{2,1,0:T(8,128)(2,1)S(1)} %get-tuple-element.135.refs_4_.refs_20_), channel_id=1, source_target_pairs={{0,8},{1,9},{2,10},{3,11},{4,12},{5,13},{6,14},{7,15},{8,0},{9,1},... | collective-permute-start | bytes 1990664 | tf_op jit(solution)/shard_map/ppermute | solution.py:149
  109.5 47.1 %collective-permute-start.9 = (bf16[2,144,1152]{2,1,0:T(8,128)(2,1)S(1)}, bf16[2,144,1152]{2,1,0:T(8,128)(2,1)S(1)}, u32[]{:S(2)}, u32[]{:S(2)}) collective-permute-start(bf16[2,144,1152]{2,1,0:T(8,128)(2,1)S(1)} %get-tuple-element.136.refs_0_.refs_16_), channel_id=1, source_target_pairs={{0,1},{1,0},{2,3},{3,2},{4,5},{5,4},{6,7},{7,6},{8,9},{9,8},{10,11... | collective-permute-start | bytes 1990664 | tf_op jit(solution)/shard_map/ppermute | solution.py:149
  201.3 40.6 %collective-permute-start.48 = (bf16[2,144,1152]{2,1,0:T(8,128)(2,1)S(1)}, bf16[2,144,1152]{2,1,0:T(8,128)(2,1)S(1)}, u32[]{:S(2)}, u32[]{:S(2)}) collective-permute-start(bf16[2,144,1152]{2,1,0:T(8,128)(2,1)S(1)} %get-tuple-element.131.refs_4_), channel_id=1, source_target_pairs={{0,1},{1,0},{2,3},{3,2},{4,5},{5,4},{6,7},{7,6},{8,9},{9,8},{10,11... | collective-permute-start | bytes 1990664 | tf_op jit(solution)/shard_map/ppermute | solution.py:149
  281.7 105.4 %collective-permute-start.45 = (bf16[2,144,1152]{2,1,0:T(8,128)(2,1)}, bf16[2,144,1152]{2,1,0:T(8,128)(2,1)}, u32[]{:S(2)}, u32[]{:S(2)}) collective-permute-start(bf16[2,144,1152]{2,1,0:T(8,128)(2,1)} %collective-permute-done.38.refs_1_), channel_id=1, source_target_pairs={{0,1},{1,0},{2,3},{3,2},{4,5},{5,4},{6,7},{7,6},{8,9},{9,8},{10,11... | collective-permute-start | bytes 1990664 | tf_op jit(solution)/shard_map/ppermute | solution.py:149
  289.2 97.8 %collective-permute-start.49 = (bf16[2,144,1152]{2,1,0:T(8,128)(2,1)}, bf16[2,144,1152]{2,1,0:T(8,128)(2,1)}, u32[]{:S(2)}, u32[]{:S(2)}) collective-permute-start(bf16[2,144,1152]{2,1,0:T(8,128)(2,1)} %copy-done.76), channel_id=1, source_target_pairs={{0,1},{1,0},{2,3},{3,2},{4,5},{5,4},{6,7},{7,6},{8,9},{9,8},{10,11... | collective-permute-start | bytes 1990664 | tf_op jit(solution)/shard_map/ppermute | solution.py:149
  289.9 97.1 %collective-permute-start.46 = (bf16[2,144,1152]{2,1,0:T(8,128)(2,1)}, bf16[2,144,1152]{2,1,0:T(8,128)(2,1)}, u32[]{:S(2)}, u32[]{:S(2)}) collective-permute-start(bf16[2,144,1152]{2,1,0:T(8,128)(2,1)} %collective-permute-done.39.refs_2_), channel_id=1, source_target_pairs={{0,1},{1,0},{2,3},{3,2},{4,5},{5,4},{6,7},{7,6},{8,9},{9,8},{10,11... | collective-permute-start | bytes 1990664 | tf_op jit(solution)/shard_map/ppermute | solution.py:149
  289.9 97.1 %collective-permute-start.51 = (bf16[2,144,1152]{2,1,0:T(8,128)(2,1)}, bf16[2,144,1152]{2,1,0:T(8,128)(2,1)}, u32[]{:S(2)}, u32[]{:S(2)}) collective-permute-start(bf16[2,144,1152]{2,1,0:T(8,128)(2,1)} %collective-permute-done.43.refs_7_), channel_id=1, source_target_pairs={{0,1},{1,0},{2,3},{3,2},{4,5},{5,4},{6,7},{7,6},{8,9},{9,8},{10,11... | collective-permute-start | bytes 1990664 | tf_op jit(solution)/shard_map/ppermute | solution.py:149
  290.4 96.6 %collective-permute-start.47 = (bf16[2,144,1152]{2,1,0:T(8,128)(2,1)}, bf16[2,144,1152]{2,1,0:T(8,128)(2,1)}, u32[]{:S(2)}, u32[]{:S(2)}) collective-permute-start(bf16[2,144,1152]{2,1,0:T(8,128)(2,1)} %collective-permute-done.40.refs_3_), channel_id=1, source_target_pairs={{0,1},{1,0},{2,3},{3,2},{4,5},{5,4},{6,7},{7,6},{8,9},{9,8},{10,11... | collective-permute-start | bytes 1990664 | tf_op jit(solution)/shard_map/ppermute | solution.py:149
  539.9 47.3 %collective-permute-start.74 = (bf16[2,2,144,1152]{3,2,1,0:T(8,128)(2,1)}, bf16[2,2,144,1152]{3,2,1,0:T(8,128)(2,1)}, u32[]{:S(2)}, u32[]{:S(2)}) collective-permute-start(bf16[2,2,144,1152]{3,2,1,0:T(8,128)(2,1)} %get-tuple-element.101), channel_id=1, source_target_pairs={{0,1},{1,0},{2,3},{3,2},{4,5},{5,4},{6,7},{7,6},{8,9},{9,8},{10,11... | collective-permute-start | bytes 3981320 | tf_op jit(solution)/shard_map/ppermute | solution.py:149
  553.6 43.0 %collective-permute-start.75 = (bf16[2,2,144,1152]{3,2,1,0:T(8,128)(2,1)}, bf16[2,2,144,1152]{3,2,1,0:T(8,128)(2,1)}, u32[]{:S(2)}, u32[]{:S(2)}) collective-permute-start(bf16[2,2,144,1152]{3,2,1,0:T(8,128)(2,1)} %copy-done.40), channel_id=1, source_target_pairs={{0,1},{1,0},{2,3},{3,2},{4,5},{5,4},{6,7},{7,6},{8,9},{9,8},{10,11... | collective-permute-start | bytes 3981320 | tf_op jit(solution)/shard_map/ppermute | solution.py:149
  553.8 35.2 %collective-permute-start.78 = (bf16[2,2,144,1152]{3,2,1,0:T(8,128)(2,1)}, bf16[2,2,144,1152]{3,2,1,0:T(8,128)(2,1)S(1)}, u32[]{:S(2)}, u32[]{:S(2)}) collective-permute-start(bf16[2,2,144,1152]{3,2,1,0:T(8,128)(2,1)} %get-tuple-element.105), channel_id=1, source_target_pairs={{0,1},{1,0},{2,3},{3,2},{4,5},{5,4},{6,7},{7,6},{8,9},{9,8},{10,11... | collective-permute-start | bytes 3981320 | tf_op jit(solution)/shard_map/ppermute | solution.py:149
  554.2 45.1 %collective-permute-start.79 = (bf16[2,2,144,1152]{3,2,1,0:T(8,128)(2,1)}, bf16[2,2,144,1152]{3,2,1,0:T(8,128)(2,1)S(1)}, u32[]{:S(2)}, u32[]{:S(2)}) collective-permute-start(bf16[2,2,144,1152]{3,2,1,0:T(8,128)(2,1)} %copy-done.39), channel_id=1, source_target_pairs={{0,1},{1,0},{2,3},{3,2},{4,5},{5,4},{6,7},{7,6},{8,9},{9,8},{10,11... | collective-permute-start | bytes 3981320 | tf_op jit(solution)/shard_map/ppermute | solution.py:149
  602.2 57.6 %collective-permute-start.54 = (bf16[2,2,144,1152]{3,2,1,0:T(8,128)(2,1)S(1)}, bf16[2,2,144,1152]{3,2,1,0:T(8,128)(2,1)S(1)}, u32[]{:S(2)}, u32[]{:S(2)}) collective-permute-start(bf16[2,2,144,1152]{3,2,1,0:T(8,128)(2,1)S(1)} %add_convert_fusion.5), channel_id=1, source_target_pairs={{0,8},{1,9},{2,10},{3,11},{4,12},{5,13},{6,14},{7,15},{8,0},{9,1},... | collective-permute-start | bytes 3981320 | tf_op jit(solution)/shard_map/ppermute | solution.py:149
  603.5 57.8 %collective-permute-start.58 = (bf16[2,2,144,1152]{3,2,1,0:T(8,128)(2,1)S(1)}, bf16[2,2,144,1152]{3,2,1,0:T(8,128)(2,1)S(1)}, u32[]{:S(2)}, u32[]{:S(2)}) collective-permute-start(bf16[2,2,144,1152]{3,2,1,0:T(8,128)(2,1)S(1)} %add_convert_fusion.4), channel_id=1, source_target_pairs={{0,16},{1,17},{2,18},{3,19},{4,20},{5,21},{6,22},{7,23},{8,24},{9,... | collective-permute-start | bytes 3981320 | tf_op jit(solution)/shard_map/ppermute | solution.py:149
  605.0 83.3 %collective-permute-start.65 = (bf16[2,2,144,1152]{3,2,1,0:T(8,128)(2,1)S(1)}, bf16[2,2,144,1152]{3,2,1,0:T(8,128)(2,1)S(1)}, u32[]{:S(2)}, u32[]{:S(2)}) collective-permute-start(bf16[2,2,144,1152]{3,2,1,0:T(8,128)(2,1)S(1)} %add_convert_fusion.3), channel_id=1, source_target_pairs={{0,8},{1,9},{2,10},{3,11},{4,12},{5,13},{6,14},{7,15},{8,0},{9,1},... | collective-permute-start | bytes 3981320 | tf_op jit(solution)/shard_map/ppermute | solution.py:149
  631.3 58.4 %collective-permute-start.69 = (bf16[2,2,144,1152]{3,2,1,0:T(8,128)(2,1)S(1)}, bf16[2,2,144,1152]{3,2,1,0:T(8,128)(2,1)S(1)}, u32[]{:S(2)}, u32[]{:S(2)}) collective-permute-start(bf16[2,2,144,1152]{3,2,1,0:T(8,128)(2,1)S(1)} %add_convert_fusion.2), channel_id=1, source_target_pairs={{0,16},{1,17},{2,18},{3,19},{4,20},{5,21},{6,22},{7,23},{8,24},{9,... | collective-permute-start | bytes 3981320 | tf_op jit(solution)/shard_map/ppermute | solution.py:149
  632.9 71.1 %collective-permute-start.77 = (bf16[2,144,1152]{2,1,0:T(8,128)(2,1)S(1)}, bf16[2,144,1152]{2,1,0:T(8,128)(2,1)S(1)}, u32[]{:S(2)}, u32[]{:S(2)}) collective-permute-start(bf16[2,144,1152]{2,1,0:T(8,128)(2,1)S(1)} %fusion.23), channel_id=1, source_target_pairs={{0,16},{1,17},{2,18},{3,19},{4,20},{5,21},{6,22},{7,23},{8,24},{9,... | collective-permute-start | bytes 1990664 | tf_op jit(solution)/shard_map/ppermute | solution.py:149
  659.8 45.3 %collective-permute-start.81 = (bf16[2,144,1152]{2,1,0:T(8,128)(2,1)S(1)}, bf16[2,144,1152]{2,1,0:T(8,128)(2,1)S(1)}, u32[]{:S(2)}, u32[]{:S(2)}) collective-permute-start(bf16[2,144,1152]{2,1,0:T(8,128)(2,1)S(1)} %fusion.24), channel_id=1, source_target_pairs={{0,8},{1,9},{2,10},{3,11},{4,12},{5,13},{6,14},{7,15},{8,0},{9,1},... | collective-permute-start | bytes 1990664 | tf_op jit(solution)/shard_map/ppermute | solution.py:149
  661.3 56.9 %collective-permute-start.55 = (bf16[2,144,1152]{2,1,0:T(8,128)(2,1)S(1)}, bf16[2,144,1152]{2,1,0:T(8,128)(2,1)S(1)}, u32[]{:S(2)}, u32[]{:S(2)}) collective-permute-start(bf16[2,144,1152]{2,1,0:T(8,128)(2,1)S(1)} %fusion.19), channel_id=1, source_target_pairs={{0,16},{1,17},{2,18},{3,19},{4,20},{5,21},{6,22},{7,23},{8,24},{9,... | collective-permute-start | bytes 1990664 | tf_op jit(solution)/shard_map/ppermute | solution.py:149
  689.8 41.5 %collective-permute-start.66 = (bf16[2,144,1152]{2,1,0:T(8,128)(2,1)S(1)}, bf16[2,144,1152]{2,1,0:T(8,128)(2,1)S(1)}, u32[]{:S(2)}, u32[]{:S(2)}) collective-permute-start(bf16[2,144,1152]{2,1,0:T(8,128)(2,1)S(1)} %fusion.21), channel_id=1, source_target_pairs={{0,16},{1,17},{2,18},{3,19},{4,20},{5,21},{6,22},{7,23},{8,24},{9,... | collective-permute-start | bytes 1990664 | tf_op jit(solution)/shard_map/ppermute | solution.py:149
  718.2 35.5 %collective-permute-start.83 = (bf16[144,1152]{1,0:T(8,128)(2,1)S(1)}, bf16[144,1152]{1,0:T(8,128)(2,1)S(1)}, u32[]{:S(2)}, u32[]{:S(2)}) collective-permute-start(bf16[144,1152]{1,0:T(8,128)(2,1)S(1)} %get-tuple-element.123), channel_id=1, source_target_pairs={{0,4},{1,5},{2,6},{3,7},{4,0},{5,1},{6,2},{7,3},{8,12},{9,13},{10,... | collective-permute-start | bytes 995336 | tf_op jit(solution)/shard_map/ppermute | solution.py:149
  734.4 49.7 %collective-permute-start.61 = (bf16[144,1152]{1,0:T(8,128)(2,1)S(1)}, bf16[144,1152]{1,0:T(8,128)(2,1)S(1)}, u32[]{:S(2)}, u32[]{:S(2)}) collective-permute-start(bf16[144,1152]{1,0:T(8,128)(2,1)S(1)} %get-tuple-element.129), channel_id=1, source_target_pairs={{0,4},{1,5},{2,6},{3,7},{4,0},{5,1},{6,2},{7,3},{8,12},{9,13},{10,... | collective-permute-start | bytes 995336 | tf_op jit(solution)/shard_map/ppermute | solution.py:149
  735.8 48.3 %collective-permute-start.62 = (bf16[144,1152]{1,0:T(8,128)(2,1)S(1)}, bf16[144,1152]{1,0:T(8,128)(2,1)S(1)}, u32[]{:S(2)}, u32[]{:S(2)}) collective-permute-start(bf16[144,1152]{1,0:T(8,128)(2,1)S(1)} %get-tuple-element.130), channel_id=1, source_target_pairs={{0,2},{1,3},{2,4},{3,5},{4,6},{5,7},{6,0},{7,1},{8,10},{9,11},{10,... | collective-permute-start | bytes 995336 | tf_op jit(solution)/shard_map/ppermute | solution.py:149
  753.7 37.0 %collective-permute-start.71 = (bf16[144,1152]{1,0:T(8,128)(2,1)}, bf16[144,1152]{1,0:T(8,128)(2,1)}, u32[]{:S(2)}, u32[]{:S(2)}) collective-permute-start(bf16[144,1152]{1,0:T(8,128)(2,1)} %get-tuple-element.125), channel_id=1, source_target_pairs={{0,6},{1,7},{2,0},{3,1},{4,2},{5,3},{6,4},{7,5},{8,14},{9,15},{10,... | collective-permute-start | bytes 995336 | tf_op jit(solution)/shard_map/ppermute | solution.py:149
  753.7 44.3 %collective-permute-start.72 = (bf16[144,1152]{1,0:T(8,128)(2,1)}, bf16[144,1152]{1,0:T(8,128)(2,1)}, u32[]{:S(2)}, u32[]{:S(2)}) collective-permute-start(bf16[144,1152]{1,0:T(8,128)(2,1)} %get-tuple-element.126), channel_id=1, source_target_pairs={{0,4},{1,5},{2,6},{3,7},{4,0},{5,1},{6,2},{7,3},{8,12},{9,13},{10,... | collective-permute-start | bytes 995336 | tf_op jit(solution)/shard_map/ppermute | solution.py:149
  759.1 38.9 %collective-permute-start.73 = (bf16[144,1152]{1,0:T(8,128)(2,1)S(1)}, bf16[144,1152]{1,0:T(8,128)(2,1)}, u32[]{:S(2)}, u32[]{:S(2)}) collective-permute-start(bf16[144,1152]{1,0:T(8,128)(2,1)S(1)} %get-tuple-element.127), channel_id=1, source_target_pairs={{0,2},{1,3},{2,4},{3,5},{4,6},{5,7},{6,0},{7,1},{8,10},{9,11},{10,... | collective-permute-start | bytes 995336 | tf_op jit(solution)/shard_map/ppermute | solution.py:149
  (169 other events, 3164.7 us)

commit v4 on v3

--- a/solution.py
+++ b/solution.py
@@ -163,27 +163,6 @@
     if flip // 2:
         plane = plane + 2 - 4 * (plane // 2)
     return plane
-
-
-def gather_line(shard):
-    return [shard] + [swap(shard, turn) for turn in (1, 2, 3)]
-
-
-def gather_plane(line):
-    depth = place()[1]
-    ring = jnp.stack(line + line)
-    begin = (4 - depth) % 4
-    own = []
-    for half, (first, first_flip, second, second_flip) in enumerate(HALF_ORDERS):
-        piece = lax.dynamic_slice_in_dim(ring, begin + 2 * half, 2, axis=0)
-        beside = swap(piece, first)
-        across = [swap(piece, second), swap(beside, second)]
-        found = [piece, None, None, across[1]]
-        found[first_flip] = beside
-        found[second_flip] = across[0]
-        own.append(found)
-    other = [[swap(piece, "core") for piece in found] for found in own]
-    return (own, other)
 
 
 def pick(values, index):
@@ -383,30 +362,15 @@
     return jax.ShapeDtypeStruct(dims, kind)
 
 
-def load_blocks(pieces, room, sems, plane_major, natural=False, lanes=None):
-    plane, _, core = place()
-    sides = (core, 1 - core)
-    deep = pieces[0].shape[1]
-    blocks = [[] for _ in range(4)]
-    count = 0
-    for flip in range(4):
-        at = flipped(plane, flip)
-        for turn in range(2):
-            for depth in range(4):
-                source = pieces[turn * 8 + depth // 2 * 4 + flip].at[depth % 2]
-                if lanes is not None:
-                    source = source.at[:, lanes[0] : lanes[1]]
-                if plane_major:
-                    block, row, held = flip, depth * 2 + sides[turn], at if natural else flip
-                else:
-                    block, row, held = depth, at * 2 + sides[turn], depth
-                target = room.at[held, pl.ds(pl.multiple_of(row * deep, 16), deep)]
-                blocks[block].append(pltpu.make_async_copy(source, target, sems.at[count]))
-                count += 1
-    for block in blocks:
-        for copy in block:
-            copy.start()
-    return blocks
+def load_blocks(whole, room, sems, lanes=None):
+    copies = []
+    for block in range(4):
+        source = whole.at[block]
+        if lanes is not None:
+            source = source.at[:, lanes[0] : lanes[1]]
+        copies.append([pltpu.make_async_copy(source, room.at[block], sems.at[block])])
+        copies[-1][0].start()
+    return copies
 
 
 def wait_all(copies):
@@ -453,52 +417,6 @@
         - jnp.mean(grad, axis=-1, keepdims=True)
         - normed * jnp.mean(grad * normed, axis=-1, keepdims=True)
     )
-
-
-def project_kernel(normed, bias, *refs):
-    pieces, out, room, product, wide, sems = refs[:16], refs[16], refs[17], refs[18], refs[19], refs[20]
-    rows, width = normed.shape
-    columns = out.shape[1] // 4
-    for block in load_blocks(pieces, room, sems, True, natural=True):
-        wait_all(block)
-    span = product.shape[1]
-    for block in range(4):
-        product[...] = mm(normed[...], room[block, :, :span])
-        begin, offset = window_of(block, columns, out.shape[1], span)
-
-        def put(at):
-            moved = product[at, :]
-            if offset:
-                moved = pltpu.roll(moved, offset, 1)
-            lane = lane_index(moved.shape[0], span)
-            inside = (lane >= offset) & (lane < offset + columns)
-            wide[at, begin : begin + span] = jnp.where(inside, moved, wide[at, begin : begin + span])
-
-        by_rows(rows, 64, put)
-
-    def finish(at):
-        out[at, :] = (wide[at, :] + bias[...]).astype(jnp.bfloat16)
-
-    by_rows(rows, 64, finish)
-
-
-def project(normed, bias, pieces):
-    rows, width = normed.shape
-    total = bias.shape[1]
-    span = -(-total // 4 // 128) * 128 + 128
-    return local_call(
-        project_kernel,
-        [shaped((rows, total), jnp.bfloat16)],
-        [normed, bias],
-        pieces,
-        [
-            pltpu.VMEM((4, width, width), jnp.bfloat16),
-            pltpu.VMEM((rows, span), jnp.float32),
-            pltpu.VMEM((rows, total), jnp.float32),
-            pltpu.SemaphoreType.DMA((32,)),
-        ],
-        56,
-    )[0]
 
 
 def head_window(head, size, total):
@@ -507,45 +425,6 @@
     lane = lane_index(1, 256)
     offset = head * size - begin
     return begin, (lane >= offset) & (lane < offset + size)
-
-
-def attend_kernel(joined, slots, slot_line, out, stats, bar, wide):
-    rows, width = out.shape
-    size = width // HEADS
-    bar[...] = jnp.where(slots[...] == slot_line[...], 0.0, -1e30)
-    scale = 1.0 / math.sqrt(size)
-    stats[...] = jnp.zeros_like(stats)
-
-    @pl.loop(0, HEADS)
-    def _(head):
-        begin, inside = head_window(head, size, width)
-        query = jnp.where(inside, joined[:, pl.ds(begin, 256)], 0.0)
-        key = joined[:, pl.ds(pl.multiple_of(begin + width, 128), 256)]
-        value = joined[:, pl.ds(pl.multiple_of(begin + 2 * width, 128), 256)]
-        scores = matmul_nt(query, key) * scale + bar[...]
-        highest = jnp.max(scores, axis=1, keepdims=True)
-        powers = jnp.exp(scores - highest)
-        totals = jnp.sum(powers, axis=1, keepdims=True)
-        probs = (powers * (1.0 / totals)).astype(jnp.bfloat16)
-        found = mm(probs, value)
-        wide[:, pl.ds(begin, 256)] = jnp.where(inside, found, wide[:, pl.ds(begin, 256)])
-        lane = lane_index(rows, 128)
-        stats[...] = jnp.where(lane == head, highest + jnp.log(totals), stats[...])
-
-    out[...] = wide[...].astype(jnp.bfloat16)
-
-
-def attend(joined, slots):
-    rows, total = joined.shape
-    width = total // 3
-    return local_call(
-        attend_kernel,
-        [shaped((rows, width), jnp.bfloat16), shaped((rows, 128))],
-        [joined, slots.reshape(rows, 1), slots.reshape(1, rows)],
-        [],
-        [pltpu.VMEM((rows, rows), jnp.float32), pltpu.VMEM((rows, width), jnp.float32)],
-        40,
-    )
 
 
 def attend_back_kernel(joined, grad, stats, slots, slot_line, blocks, sums, bar, wide):
@@ -609,94 +488,10 @@
     )(joined, grad, stats, slots.reshape(rows, 1), slots.reshape(1, rows))
 
 
-def branch_kernel(attended, start, slots, table, bias, *refs):
-    pieces, (branch, middle, normed, room, product, sems) = refs[:16], refs[16:]
-    rows, width = start.shape
-    columns = width // 4
-    for block in load_blocks(pieces, room, sems, True, natural=True, lanes=(width - WINDOW, width)):
-        wait_all(block)
-    for block in range(4):
-        product[...] = mm(attended[...], room[block])
-        begin, offset = window_of(block, columns, width, WINDOW)
-
-        def put(at):
-            moved = product[at, :]
-            if offset != WINDOW - columns:
-                moved = pltpu.roll(moved, columns + offset, 1)
-            lane = lane_index(moved.shape[0], WINDOW)
-            inside = (lane >= offset) & (lane < offset + columns)
-            branch[at, begin : begin + WINDOW] = jnp.where(
-                inside, moved, branch[at, begin : begin + WINDOW]
-            )
-
-        by_rows(rows, 64, put)
-
-    def finish(at):
-        slot = slots[at, :]
-        value = branch[at, :] + bias[...]
-        branch[at, :] = value
-        value = start[at, :] + slot_rows(slot, table, 2, width) * value
-        middle[at, :] = value
-        hat, _ = centred(value)
-        value = hat * (1.0 + slot_rows(slot, table, 4, width)) + slot_rows(slot, table, 3, width)
-        normed[at, :] = value.astype(jnp.bfloat16)
-
-    by_rows(rows, 64, finish)
-
-
-def branch_one(attended, start, slots, table, bias, pieces):
-    rows, width = start.shape
-    return local_call(
-        branch_kernel,
-        [shaped((rows, width)), shaped((rows, width)), shaped((rows, width), jnp.bfloat16)],
-        [attended, start, slots.reshape(rows, 1), table, bias],
-        pieces,
-        [
-            pltpu.VMEM((4, width, WINDOW), jnp.bfloat16),
-            pltpu.VMEM((rows, WINDOW), jnp.float32),
-            pltpu.SemaphoreType.DMA((32,)),
-        ],
-        48,
-    )
-
-
-def widen_kernel(normed, bias, *refs):
-    pieces, (hidden, before, room, sems) = refs[:16], refs[16:]
-    plane = place()[0]
-    rows = normed.shape[0]
-    blocks = load_blocks(pieces, room, sems, True)
-    for flip in range(4):
-        at = flipped(plane, flip)
-        wait_all(blocks[flip])
-        before[at] = mm(normed[...], room[flip]) + bias[at]
-
-        def act(some):
-            value = before[at, some, :]
-            bend = 1.0 + jnp.tanh(SLOPE * (value + 0.044715 * (value * value * value)))
-            hidden[at, some, :] = (value * (0.5 * bend)).astype(jnp.bfloat16)
-
-        by_rows(rows, 64, act)
-
-
-def widen(normed, bias, pieces):
-    rows, width = normed.shape
-    return pl.pallas_call(
-        widen_kernel,
-        out_shape=[shaped((4, rows, width), jnp.bfloat16), shaped((4, rows, width))],
-        in_specs=[pl.BlockSpec(memory_space=pltpu.VMEM)] * 2 + [pl.BlockSpec(memory_space=pl.ANY)] * 16,
-        scratch_shapes=[pltpu.VMEM((4, width, width), jnp.bfloat16), pltpu.SemaphoreType.DMA((32,))],
-        compiler_params=pltpu.CompilerParams(vmem_limit_bytes=56 * 2**20),
-        cost_estimate=pl.CostEstimate(flops=0, bytes_accessed=0, transcendentals=0),
-    )(normed, bias, *pieces)
-
-
 def narrow_kernel(hidden, middle, out_grad, slots, table, bias, before_all, *refs):
-    pieces, (mixed, branch_grad, pre_grad, sums, gate_sums, pre_sums, room, total, before, sems, more) = (
-        refs[:16],
-        refs[16:],
-    )
+    whole, mixed, branch_grad, pre_grad, sums, gate_sums, pre_sums, room, total, before, sems, more = refs
     rows, width = middle.shape
-    blocks = load_blocks(pieces, room, sems, False)
+    blocks = load_blocks(whole, room, sems)
     copies = [pltpu.make_async_copy(before_all.at[part], before.at[part], more.at[part]) for part in range(4)]
     for copy in copies:
         copy.start()
@@ -741,7 +536,7 @@
         by_rows(rows, 64, act)
 
 
-def narrow(hidden, before, middle, out_grad, slots, table, bias, pieces):
+def narrow(hidden, before, middle, out_grad, slots, table, bias, whole):
     rows, width = middle.shape
     return pl.pallas_call(
         narrow_kernel,
@@ -753,7 +548,7 @@
             shaped((8, width)),
             shaped((8, width)),
         ],
-        in_specs=[pl.BlockSpec(memory_space=pltpu.VMEM)] * 6 + [pl.BlockSpec(memory_space=pl.ANY)] * 17,
+        in_specs=[pl.BlockSpec(memory_space=pltpu.VMEM)] * 6 + [pl.BlockSpec(memory_space=pl.ANY)] * 2,
         scratch_shapes=[
             pltpu.VMEM((4, width, width), jnp.bfloat16),
             pltpu.VMEM((rows, width), jnp.float32),
@@ -763,22 +558,19 @@
         ],
         compiler_params=pltpu.CompilerParams(vmem_limit_bytes=58 * 2**20),
         cost_estimate=pl.CostEstimate(flops=0, bytes_accessed=0, transcendentals=0),
-    )(hidden, middle, out_grad, slots.reshape(rows, 1), table, bias, before, *pieces)
+    )(hidden, middle, out_grad, slots.reshape(rows, 1), table, bias, before, whole)
 
 
 def middle_kernel(pre_grad, middle, out_grad, branch, slots, table, *refs):
-    wide_pieces, joined_pieces = refs[:16], refs[16:32]
-    middle_grad, attended_grad, windows, slot_sums, sums, room, side, total, sems, more = refs[32:]
-    plane = place()[0]
+    up_whole, joined_whole, middle_grad, attended_grad, windows = refs[:5]
+    slot_sums, sums, room, side, total, sems, more = refs[5:]
     rows, width = middle.shape
     columns = width // 4
-    blocks = load_blocks(wide_pieces, room, sems, True)
-    side_blocks = load_blocks(
-        joined_pieces, side, more, True, natural=True, lanes=(width - WINDOW, width)
-    )
+    blocks = load_blocks(up_whole, room, sems)
+    side_blocks = load_blocks(joined_whole, side, more, lanes=(width - WINDOW, width))
     for flip in range(4):
         wait_all(blocks[flip])
-        term = matmul_nt(pre_grad[flipped(plane, flip)], room[flip])
+        term = matmul_nt(pre_grad[flip], room[flip])
         if flip == 0:
             total[...] = term
         else:
@@ -821,7 +613,7 @@
     attended_grad[...] = value.astype(jnp.bfloat16)
 
 
-def middle_back(pre_grad, middle, out_grad, branch, slots, table, wide_pieces, joined_pieces):
+def middle_back(pre_grad, middle, out_grad, branch, slots, table, up_whole, joined_whole):
     rows, width = middle.shape
     return pl.pallas_call(
         middle_kernel,
@@ -832,7 +624,7 @@
             shaped((3, 8, width)),
             shaped((1, width)),
         ],
-        in_specs=[pl.BlockSpec(memory_space=pltpu.VMEM)] * 6 + [pl.BlockSpec(memory_space=pl.ANY)] * 32,
+        in_specs=[pl.BlockSpec(memory_space=pltpu.VMEM)] * 6 + [pl.BlockSpec(memory_space=pl.ANY)] * 2,
         scratch_shapes=[
             pltpu.VMEM((4, width, width), jnp.bfloat16),
             pltpu.VMEM((4, width, WINDOW), jnp.bfloat16),
@@ -842,18 +634,17 @@
         ],
         compiler_params=pltpu.CompilerParams(vmem_limit_bytes=58 * 2**20),
         cost_estimate=pl.CostEstimate(flops=0, bytes_accessed=0, transcendentals=0),
-    )(pre_grad, middle, out_grad, branch, slots.reshape(rows, 1), table, *wide_pieces, *joined_pieces)
+    )(pre_grad, middle, out_grad, branch, slots.reshape(rows, 1), table, up_whole, joined_whole)
 
 
 def start_kernel(blocks, start, middle_grad, slots, table, *refs):
-    pieces, (grad_out, slot_sums, room, total, sems) = refs[:16], refs[16:]
-    plane = place()[0]
+    whole, grad_out, slot_sums, room, total, sems = refs
     rows, width = start.shape
     span = blocks.shape[2]
-    loads = load_blocks(pieces, room, sems, True, lanes=(0, span))
+    loads = load_blocks(whole, room, sems, lanes=(0, span))
     for flip in range(4):
         wait_all(loads[flip])
-        term = matmul_nt(blocks[flipped(plane, flip)], room[flip])
+        term = matmul_nt(blocks[flip], room[flip])
         if flip == 0:
             total[...] = term
         else:
@@ -872,19 +663,372 @@
     by_rows(rows, 64, finish)
 
 
-def start_back(blocks, start, middle_grad, slots, table, pieces):
+def start_back(blocks, start, middle_grad, slots, table, whole):
     rows, width = start.shape
     return local_call(
         start_kernel,
         [shaped((rows, width)), shaped((2, 8, width))],
         [blocks, start, middle_grad, slots.reshape(rows, 1), table],
-        pieces,
+        [whole],
         [
             pltpu.VMEM((4, width, blocks.shape[2]), jnp.bfloat16),
             pltpu.VMEM((rows, width), jnp.float32),
             pltpu.SemaphoreType.DMA((32,)),
         ],
         48,
+    )
+
+
+def far_device(plane, depth, core):
+    return (plane, depth * 2 + core)
+
+
+class Gather:
+    def __init__(self, shards, wholes, send_sems, recv_sems, local_sems):
+        self.shards, self.wholes = shards, wholes
+        self.send_sems, self.recv_sems, self.local_sems = send_sems, recv_sems, local_sems
+        self.plane, self.depth, self.core = place()
+        self.started = []
+        self.kept = []
+        self.counts = [0, 0, 0]
+
+    def partners(self):
+        found = [
+            far_device(flipped(self.plane, 1), self.depth, self.core),
+            far_device(flipped(self.plane, 2), self.depth, self.core),
+            far_device(self.plane, self.depth, 1 - self.core),
+        ]
+        return found + [far_device(self.plane, (self.depth + d) % 4, self.core) for d in (1, 2, 3)]
+
+    def spot(self, weight, flip, back, other=False):
+        plane, depth = flipped(self.plane, flip), (self.depth + 4 - back) % 4
+        core = 1 - self.core if other else self.core
+        if weight < 2:
+            return self.wholes[weight].at[plane, depth, core]
+        return self.wholes[weight].at[depth, plane, core]
+
+    def send(self, weight, source, target, partner, kind, entry):
+        copy = pltpu.make_async_remote_copy(
+            src_ref=source,
+            dst_ref=target,
+            send_sem=self.send_sems.at[weight, self.counts[weight]],
+            recv_sem=self.recv_sems.at[weight, kind, entry],
+            device_id=partner,
+            device_id_type=pl.DeviceIdType.MESH,
+        )
+        self.counts[weight] += 1
+        copy.start()
+        self.started.append(copy)
+
+    def arrive(self, weight, region, kind, entry):
+        pltpu.make_async_remote_copy(
+            src_ref=region,
+            dst_ref=region,
+            send_sem=self.send_sems.at[weight, 0],
+            recv_sem=self.recv_sems.at[weight, kind, entry],
+            device_id=self.partners()[2],
+            device_id_type=pl.DeviceIdType.MESH,
+        ).wait_recv()
+
+    def pass_on(self, weight, source, flip, back):
+        target = self.spot(weight, flip, back)
+        beside = self.partners()
+        if flip == 0 or (flip == 2 and back % 2 == 1):
+            self.send(weight, source, target, beside[0], 1 if flip == 0 else 3, back)
+        if flip == 0 or (flip == 1 and back % 2 == 0):
+            self.send(weight, source, target, beside[1], 2 if flip == 0 else 3, back)
+        self.send(weight, source, target, beside[2], 4 + flip, back)
+
+    def open_plane(self, weight):
+        keep = pltpu.make_async_copy(
+            self.shards[weight], self.spot(weight, 0, 0), self.local_sems.at[weight]
+        )
+        keep.start()
+        self.kept.append(keep)
+        self.pass_on(weight, self.shards[weight], 0, 0)
+
+    def open_line(self, weight):
+        for d in (1, 3, 2):
+            target = self.spot(weight, 0, 0)
+            self.send(weight, self.shards[weight], target, self.partners()[2 + d], 0, d)
+
+    def on_line(self, weight, back):
+        region = self.spot(weight, 0, back)
+        self.arrive(weight, region, 0, back)
+        self.pass_on(weight, region, 0, back)
+
+    def on_plane(self, weight, flip, back):
+        region = self.spot(weight, flip, back)
+        self.arrive(weight, region, flip, back)
+        self.pass_on(weight, region, flip, back)
+
+    def steps(self, weight):
+        found = []
+        for back in (0, 1, 3, 2):
+            if back:
+                found.append(partial(self.on_line, weight, back))
+        for back in (0, 1, 3, 2):
+            found.append(partial(self.on_plane, weight, 1, back))
+            found.append(partial(self.on_plane, weight, 2, back))
+        for back in (0, 1, 3, 2):
+            found.append(partial(self.on_plane, weight, 3, back))
+        return found
+
+    def ready(self, weight):
+        for flip in range(4):
+            for back in (0, 1, 3, 2):
+                self.arrive(weight, self.spot(weight, flip, back, True), 4 + flip, back)
+        self.kept[weight].wait()
+
+    def finish(self):
+        for copy in self.started:
+            copy.wait_send()
+
+
+def greet(partners):
+    barrier = pltpu.get_barrier_semaphore()
+    for partner in partners:
+        pl.semaphore_signal(
+            barrier, inc=1, device_id=partner, device_id_type=pl.DeviceIdType.MESH
+        )
+    pl.semaphore_wait(barrier, len(partners))
+
+
+def forward_kernel(
+    normed,
+    start,
+    slots,
+    slot_line,
+    table,
+    joined_bias,
+    out_bias,
+    up_bias,
+    joined_shard,
+    up_shard,
+    down_shard,
+    joined_whole,
+    up_whole,
+    down_whole,
+    joined,
+    attended,
+    stats,
+    branch,
+    middle,
+    normed2,
+    hidden,
+    before,
+    room,
+    product,
+    wide_room,
+    bar,
+    before_room,
+    send_sems,
+    recv_sems,
+    local_sems,
+    load_sems,
+    store_sems,
+):
+    gather = Gather(
+        (joined_shard, up_shard, down_shard),
+        (joined_whole, up_whole, down_whole),
+        send_sems,
+        recv_sems,
+        local_sems,
+    )
+    greet(gather.partners())
+    gather.open_line(0)
+    for weight in range(3):
+        gather.open_plane(weight)
+    first = gather.steps(0)
+    for step in first[:3]:
+        step()
+    gather.open_line(1)
+    for step in first[3:]:
+        step()
+    later = gather.steps(1)[:3] + [partial(gather.open_line, 2)] + gather.steps(1)[3:]
+    later += gather.steps(2)
+
+    def tick(count=1):
+        for _ in range(count):
+            if later:
+                later.pop(0)()
+
+    rows, width = normed.shape
+    columns = joined.shape[1] // 4
+    size = room.shape[1]
+    gather.ready(0)
+    loads = [
+        pltpu.make_async_copy(
+            joined_whole.at[block], room.at[block], load_sems.at[block]
+        )
+        for block in range(4)
+    ]
+    for load in loads:
+        load.start()
+    tick(3)
+    span = product.shape[1]
+    for block in range(4):
+        loads[block].wait()
+        product[...] = mm(normed[...], room[block].reshape(width, width)[:, :span])
+        begin, offset = window_of(block, columns, joined.shape[1], span)
+
+        def put(at):
+            moved = product[at, :]
+            if offset:
+                moved = pltpu.roll(moved, offset, 1)
+            lane = lane_index(moved.shape[0], span)
+            inside = (lane >= offset) & (lane < offset + columns)
+            wide_room[at, begin : begin + span] = jnp.where(
+                inside, moved, wide_room[at, begin : begin + span]
+            )
+
+        by_rows(rows, 64, put)
+        tick()
+
+    def settle(at):
+        joined[at, :] = (wide_room[at, :] + joined_bias[...]).astype(jnp.bfloat16)
+
+    by_rows(rows, 64, settle)
+    bar[...] = jnp.where(slots[...] == slot_line[...], 0.0, -1e30)
+    stats[...] = jnp.zeros_like(stats)
+    head_size = width // HEADS
+    scale = 1.0 / math.sqrt(head_size)
+    for group in range(8):
+
+        @pl.loop(2 * group, 2 * group + 2)
+        def _(head):
+            at, inside = head_window(head, head_size, width)
+            query = jnp.where(inside, joined[:, pl.ds(at, 256)], 0.0)
+            key = joined[:, pl.ds(pl.multiple_of(at + width, 128), 256)]
+            value = joined[:, pl.ds(pl.multiple_of(at + 2 * width, 128), 256)]
+            scores = matmul_nt(query, key) * scale + bar[...]
+            highest = jnp.max(scores, axis=1, keepdims=True)
+            powers = jnp.exp(scores - highest)
+            totals = jnp.sum(powers, axis=1, keepdims=True)
+            probs = (powers * (1.0 / totals)).astype(jnp.bfloat16)
+            found = mm(probs, value)
+            wide_room[:, pl.ds(at, 256)] = jnp.where(inside, found, wide_room[:, pl.ds(at, 256)])
+            lane = lane_index(rows, 128)
+            stats[...] = jnp.where(lane == head, highest + jnp.log(totals), stats[...])
+
+        tick(2)
+
+    attended[...] = wide_room[:, :width].astype(jnp.bfloat16)
+    columns = width // 4
+    for block in range(4):
+        product[:, :WINDOW] = mm(attended[...], room[block].reshape(width, width)[:, width - WINDOW :])
+        begin, offset = window_of(block, columns, width, WINDOW)
+
+        def put(at):
+            moved = product[at, :WINDOW]
+            if offset != WINDOW - columns:
+                moved = pltpu.roll(moved, columns + offset, 1)
+            lane = lane_index(moved.shape[0], WINDOW)
+            inside = (lane >= offset) & (lane < offset + columns)
+            branch[at, begin : begin + WINDOW] = jnp.where(
+                inside, moved, branch[at, begin : begin + WINDOW]
+            )
+
+        by_rows(rows, 64, put)
+        tick()
+
+    def combine(at):
+        slot = slots[at, :]
+        value = branch[at, :] + out_bias[...]
+        branch[at, :] = value
+        value = start[at, :] + slot_rows(slot, table, 2, width) * value
+        middle[at, :] = value
+        hat, _ = centred(value)
+        value = hat * (1.0 + slot_rows(slot, table, 4, width)) + slot_rows(slot, table, 3, width)
+        normed2[at, :] = value.astype(jnp.bfloat16)
+
+    by_rows(rows, 64, combine)
+    while len(later) > 15:
+        tick()
+    gather.ready(1)
+    loads = [
+        pltpu.make_async_copy(up_whole.at[block], room.at[block], load_sems.at[block])
+        for block in range(4)
+    ]
+    for load in loads:
+        load.start()
+    stores = [None, None]
+    for block in range(4):
+        loads[block].wait()
+        slot = block % 2
+        if stores[slot] is not None:
+            stores[slot].wait()
+        before_room[slot] = mm(normed2[...], room[block].reshape(width, width)) + up_bias[block]
+        stores[slot] = pltpu.make_async_copy(
+            before_room.at[slot], before.at[block], store_sems.at[slot]
+        )
+        stores[slot].start()
+
+        def act(some):
+            value = before_room[slot, some, :]
+            bend = 1.0 + jnp.tanh(SLOPE * (value + 0.044715 * (value * value * value)))
+            hidden[block, some, :] = (value * (0.5 * bend)).astype(jnp.bfloat16)
+
+        by_rows(rows, 64, act)
+        tick(3)
+    while later:
+        tick()
+    for store in stores:
+        store.wait()
+    gather.ready(2)
+    gather.finish()
+
+
+def forward(normed, start, slots, table, joined_bias, out_bias, up_bias, shards):
+    rows, width = normed.shape
+    deep = width // 8
+    whole = shaped((4, 4, 2, deep, width), jnp.bfloat16)
+    vmem, away = pl.BlockSpec(memory_space=pltpu.VMEM), pl.BlockSpec(memory_space=pl.ANY)
+    return pl.pallas_call(
+        forward_kernel,
+        out_shape=[
+            whole,
+            whole,
+            whole,
+            shaped((rows, 3 * width), jnp.bfloat16),
+            shaped((rows, width), jnp.bfloat16),
+            shaped((rows, 128)),
+            shaped((rows, width)),
+            shaped((rows, width)),
+            shaped((rows, width), jnp.bfloat16),
+            shaped((4, rows, width), jnp.bfloat16),
+            shaped((4, rows, width)),
+        ],
+        in_specs=[vmem] * 8 + [away] * 3,
+        out_specs=[away] * 3 + [vmem] * 7 + [away],
+        scratch_shapes=[
+            pltpu.VMEM((4, 4, 2, deep, width), jnp.bfloat16),
+            pltpu.VMEM((rows, 1024), jnp.float32),
+            pltpu.VMEM((rows, 3 * width), jnp.float32),
+            pltpu.VMEM((rows, rows), jnp.float32),
+            pltpu.VMEM((2, rows, width), jnp.float32),
+            pltpu.SemaphoreType.DMA((3, 32)),
+            pltpu.SemaphoreType.DMA((3, 8, 4)),
+            pltpu.SemaphoreType.DMA((3,)),
+            pltpu.SemaphoreType.DMA((4,)),
+            pltpu.SemaphoreType.DMA((2,)),
+        ],
+        compiler_params=pltpu.CompilerParams(
+            collective_id=4, has_side_effects=True, vmem_limit_bytes=60 * 2**20
+        ),
+        cost_estimate=pl.CostEstimate(
+            flops=2 * 10 * rows * width * width, bytes_accessed=10**8, transcendentals=0
+        ),
+    )(
+        normed,
+        start,
+        slots.reshape(rows, 1),
+        slots.reshape(1, rows),
+        table,
+        joined_bias,
+        out_bias,
+        up_bias,
+        *shards,
     )
 
 
@@ -1002,7 +1146,6 @@
     slot_count = condition.shape[0]
     core = place()[2]
     columns = attn_weight.shape[1]
-    joined_line = gather_line(jnp.concatenate([attn_weight, proj_weight], axis=1))
     turned = down_weight.T.reshape(2, up_weight.shape[0], down_weight.shape[0])
     mine, theirs = pick(turned, core), pick(turned, 1 - core)
     arrived = swap(theirs, "core")
@@ -1011,18 +1154,6 @@
         jnp.concatenate([mine, arrived], axis=1),
         jnp.concatenate([arrived, mine], axis=1),
     )
-    up_shard, _ = lax.optimization_barrier((up_weight, joined_line[1:]))
-    up_line = gather_line(up_shard)
-    down_shard, _ = lax.optimization_barrier((down_shard, up_line[1:]))
-    down_line = gather_line(down_shard)
-
-    def flat(pieces):
-        return [piece for side in pieces for found in side for piece in found]
-
-    joined_pieces = flat(gather_plane(joined_line))
-    up_pieces = flat(gather_plane(up_line))
-    down_pieces = flat(gather_plane(down_line))
-
     slot_ids = jnp.arange(slot_count, dtype=jnp.int32)
     side_rows = jnp.sum(jnp.where(segment[:, None] == slot_ids[None, :], grid_side[None, :], 0), axis=1)
     start = tokens.astype(jnp.float32) + position_code(kept_index, side_rows, width)
@@ -1043,15 +1174,34 @@
     normed1 = norm_modulate(start, own_rows(0), own_rows(1)).astype(jnp.bfloat16)
     zeros = jnp.zeros((width,), jnp.bfloat16)
     joined_bias = jnp.concatenate([attn_bfull[:width], zeros, attn_bfull[width:]])
-    joined = project(normed1, joined_bias.astype(jnp.float32)[None], joined_pieces)
-    attended, stats = attend(joined, segment)
     out_bias_f = out_bfull.astype(jnp.float32)
-    branch1, middle, normed2 = branch_one(
-        attended, start, segment, table, out_bias_f[None, :width], joined_pieces
-    )
-    hidden, before = widen(normed2, up_bfull.astype(jnp.float32).reshape(4, 1, -1), up_pieces)
+    (
+        joined_whole,
+        up_whole,
+        down_whole,
+        joined,
+        attended,
+        stats,
+        branch1,
+        middle,
+        normed2,
+        hidden,
+        before,
+    ) = forward(
+        normed1,
+        start,
+        segment,
+        table,
+        joined_bias.astype(jnp.float32)[None],
+        out_bias_f[None, :width],
+        up_bfull.astype(jnp.float32).reshape(4, 1, -1),
+        (jnp.concatenate([attn_weight, proj_weight], axis=1), up_weight, down_shard),
+    )
+    joined_whole, up_whole, down_whole = [
+        whole.reshape(4, width, width) for whole in (joined_whole, up_whole, down_whole)
+    ]
     mixed, grad_branch2, pre_grad, branch2_sums, gate2_sums, pre_sums = narrow(
-        hidden, before, middle, grad_out, segment, table, out_bias_f[None, width:], down_pieces
+        hidden, before, middle, grad_out, segment, table, out_bias_f[None, width:], down_whole
     )
     down_total = scatter_pieces(outer(False, [grad_branch2.T], [hidden]))
     up_weight_grad = scatter_pieces(outer(True, [normed2.T], [pre_grad]))
@@ -1063,7 +1213,7 @@
         core == 0, jnp.concatenate([mine, arrived]), jnp.concatenate([arrived, mine])
     ).T
     middle_grad, attended_grad, windows, slot_sums2, branch1_sums = middle_back(
-        pre_grad, middle, grad_out, branch1, segment, table, up_pieces, joined_pieces
+        pre_grad, middle, grad_out, branch1, segment, table, up_whole, joined_whole
     )
     blocks, joined_sums = attend_back(joined, attended_grad, stats, segment)
     joined_total = scatter_pieces(
@@ -1074,7 +1224,7 @@
             (blocks.shape[2], width - WINDOW),
         )
     )
-    tokens_grad, slot_sums1 = start_back(blocks, start, middle_grad, segment, table, joined_pieces)
+    tokens_grad, slot_sums1 = start_back(blocks, start, middle_grad, segment, table, joined_whole)
     modulation_grad = jnp.concatenate(
         [slot_sums1[0], slot_sums1[1], slot_sums2[0], slot_sums2[1], slot_sums2[2], gate2_sums], axis=1
     )[:slot_count].astype(jnp.bfloat16)

time: 810 us -> 660 us (0.81)
  waiting for transfers between devices: 285 us -> 123 us
  Pallas kernels: 317 us -> 381 us
  local copies, waits for them, and re-layouts: 70.4 us -> 36 us
  other arithmetic: 41.6 us -> 30.2 us
    ppermute x86 -> x35, waiting for transfers between devices: 285 us -> 123 us  [swap(): lax.ppermute(values, AXES, [(index, neighbour(index, axis)) for index in...]
    pallas_call x1, Pallas kernels: 20 us -> 162 us  [forward(): pl.pallas_call(forward_kernel, out_shape=[whole, whole, whole, shaped((ro...]
    pallas_call x4 -> x1, Pallas kernels: 77.9 us -> 18.1 us  [local_call(): pl.pallas_call(kernel, out_shape=outs, in_specs=[pl.BlockSpec(memory_spac...]
    unnamed x261 -> x93, local copies, waits for them, and re-layouts: 30.3 us -> 7.91 us
    pallas_call x4, Pallas kernels: 84.8 us -> 67 us  [exchange(): pl.pallas_call(partial(trade, one_for_all), out_shape=jax.ShapeDtypeStruc...]
    ppermute x86 -> x35, starting transfers between devices: 81.6 us -> 75.9 us  [swap(): lax.ppermute(values, AXES, [(index, neighbour(index, axis)) for index in...]
  transfers between devices with their start and end apart: 86 -> 35, of which waited for: 31 -> 14; matrix products, arithmetic and copies ran while one was open for 11% -> 8% of each run, Pallas kernels for 21% -> 12%
where the time goes in v4:
time: 660 us; the launch traced here: 651 us
  Pallas kernels  381 us (58%)
  waiting for transfers between devices  123 us (19%)
  starting transfers between devices  75.9 us (12%)
  local copies, waits for them, and re-layouts  36 us (5%)
  other arithmetic  30.2 us (5%)
    pallas_call x1, Pallas kernels, forward(): pl.pallas_call(forward_kernel, out_shape=[whole, whole, whole, shaped((ro...  162 us
    ppermute x35, waiting for transfers between devices, swap(): lax.ppermute(values, AXES, [(index, neighbour(index, axis)) for index in...  123 us
    ppermute x35, starting transfers between devices, swap(): lax.ppermute(values, AXES, [(index, neighbour(index, axis)) for index in...  75.9 us
    pallas_call x4, Pallas kernels, exchange(): pl.pallas_call(partial(trade, one_for_all), out_shape=jax.ShapeDtypeStruc...  67 us
    pallas_call x3, Pallas kernels, outer(): pl.pallas_call(partial(outer_kernel, plane_major, len(lefts), spans), out...  39.8 us
    pallas_call x1, Pallas kernels, narrow(): pl.pallas_call(narrow_kernel, out_shape=[shaped((rows, width), jnp.bfloat...  35.6 us
    pallas_call x1, Pallas kernels, middle_back(): pl.pallas_call(middle_kernel, out_shape=[shaped((rows, width)), shaped((r...  30.2 us
    pallas_call x1, Pallas kernels, attend_back(): pl.pallas_call(attend_back_kernel, out_shape=[shaped((4, rows, span), jnp...  29 us
  transfers between devices with their start and end apart: 35, of which 14 were waited for; matrix products, arithmetic and copies ran while one was open for 8% of the time, Pallas kernels for 12%

profile of v4, /device:TPU:0, one launch (start us, length us, event | category | flops | bytes accessed | tf_op | source)
XLA Modules:
  0.0 650.7 jit_solution(379246923649869826)
XLA Ops:
  3.7 2.8 concatenate.68
  6.5 16.7 %shard_map.238 = bf16[32,16,384]{2,1,0:T(8,128)(2,1)S(1)} custom-call(bf16[16,384]{1,0:T(8,128)(2,1)S(1)} %reshape.238.values), custom_call_target="tpu_custom_call" | custom-call | bytes 3145728 | tf_op jit(solution)/shard_map/pallas_call | solution.py:260
  24.6 24.8 %shard_map.239 = f32[32,4,1728]{2,1,0:T(4,128)S(1)} custom-call(f32[32,4,1728]{2,1,0:T(4,128)S(1)} %reshape.241.values), custom_call_target="tpu_custom_call" | custom-call | bytes 7077888 | tf_op jit(solution)/shard_map/pallas_call | solution.py:260
  51.5 4.2 multiply_sine_fusion.1
  60.3 3.1 copy.87.start
  72.7 161.6 %shard_map.240 = (bf16[4,4,2,144,1152]{4,3,2,1,0:T(8,128)(2,1)}, bf16[4,4,2,144,1152]{4,3,2,1,0:T(8,128)(2,1)}, bf16[4,4,2,144,1152]{4,3,2,1,0:T(8,128)(2,1)}, b...) custom-call(bf16[512,1152]{1,0:T(8,128)(2,1)} %copy.86.normed, ...), custom_call_target="tpu_custom_call" | custom-call | flops 13589544960 | bytes 100000000 | tf_op jit(solution)/shard_map/pallas_call | solution.py:987
  234.3 35.6 %shard_map.241 = (bf16[512,1152]{1,0:T(8,128)(2,1)}, bf16[512,1152]{1,0:T(8,128)(2,1)}, bf16[4,512,1152]{2,1,0:T(8,128)(2,1)}, f32[1,1152]{1,0:T(1,128)}, f32[8,1152]{1,0:T(8,128)}, /*index=5*/f32[8,1152]{1,0:T(8,128)}) custom-call(bf16[4,512,1152]{2,1,0:T(8,128)(2,1)} %get-tuple-element.62.hidden.refs_1_, f32[512,1152]{1,0:T(8,128)} %get-tuple-element.63.middle, ...), custom_call_target="tpu_custom_call" | custom-call | tf_op jit(solution)/shard_map/pallas_call | solution.py:541
  269.9 30.2 %shard_map.242 = (f32[512,1152]{1,0:T(8,128)}, bf16[512,1152]{1,0:T(8,128)(2,1)}, bf16[4,512,512]{2,1,0:T(8,128)(2,1)}, f32[3,8,1152]{2,1,0:T(8,128)}, f32[1,1152]{1,0:T(1,128)}) custom-call(bf16[4,512,1152]{2,1,0:T(8,128)(2,1)} %get-tuple-element.68.pre_grad.refs_1_, f32[512,1152]{1,0:T(8,128)} %get-tuple-element.63.middle, bf16[512,1152]{1,0:T(8,128)(2,1)} %out_grad.3, ...), custom_call_target="tpu_custom_call" | custom-call | tf_op jit(solution)/shard_map/pallas_call | solution.py:618
  300.1 2.0 copy-done.5
  303.4 29.0 %shard_map.243 = (bf16[4,512,1024]{2,1,0:T(8,128)(2,1)}, f32[1,3456]{1,0:T(1,128)S(1)}) custom-call(bf16[512,3456]{1,0:T(8,128)(2,1)S(1)} %copy-done.5, bf16[512,1152]{1,0:T(8,128)(2,1)S(1)} %copy-done.7, f32[512,128]{1,0:T(8,128)S(1)} %copy-done.8, s32[512,1]{1,0:T(8,128)S(1)} %copy-done.3, s32[1,512]{1,0:T(1,128)S(1)} %bitcast.153), custom_call_target="tpu_custom_call" | custom-call | tf_op jit(solution)/shard_map/pallas_call | solution.py:482
  332.4 18.1 %shard_map.244 = (f32[512,1152]{1,0:T(8,128)}, f32[2,8,1152]{2,1,0:T(8,128)S(1)}) custom-call(bf16[4,512,1024]{2,1,0:T(8,128)(2,1)} %get-tuple-element.74.blocks.refs_2_, f32[512,1152]{1,0:T(8,128)S(1)} %copy-done.2, f32[512,1152]{1,0:T(8,128)S(1)} %copy-done.6, s32[512,1]{1,0:T(8,128)S(1)} %copy-done.3, f32[8,6912]{1,0:T(8,128)S(1)} %copy-done.4, ...), custom_call_target="tpu_custom_call" | custom-call | tf_op jit(solution)/shard_map/pallas_call | solution.py:346
  351.0 16.2 %shard_map.245 = bf16[32,16,432]{2,1,0:T(8,128)(2,1)S(1)} custom-call(bf16[32,16,432]{2,1,0:T(8,128)(2,1)S(1)} %bitcast.147), custom_call_target="tpu_custom_call" | custom-call | bytes 3538944 | tf_op jit(solution)/shard_map/pallas_call | solution.py:260
  369.9 13.0 %shard_map.247 = (bf16[2,2,144,1152]{3,2,1,0:T(8,128)(2,1)S(1)}, bf16[2,2,144,1152]{3,2,1,0:T(8,128)(2,1)}, bf16[2,2,144,1152]{3,2,1,0:T(8,128)(2,1)}, bf16[2,2,...) custom-call(bf16[1152,512]{1,0:T(8,128)(2,1)S(1)} %fusion.103.refs_0, ...), custom_call_target="tpu_custom_call" | custom-call | tf_op jit(solution)/shard_map/pallas_call | solution.py:1090
  385.0 9.2 %shard_map.246 = f32[32,8,128]{2,1,0:T(8,128)S(1)} custom-call(f32[32,8,128]{2,1,0:T(8,128)S(1)} %bitcast.149), custom_call_target="tpu_custom_call" | custom-call | bytes 1048576 | tf_op jit(solution)/shard_map/pallas_call | solution.py:260
  398.2 13.5 %shard_map.248 = (bf16[2,2,144,1152]{3,2,1,0:T(8,128)(2,1)S(1)}, bf16[2,2,144,1152]{3,2,1,0:T(8,128)(2,1)S(1)}, bf16[2,2,144,1152]{3,2,1,0:T(8,128)(2,1)S(1)}, b...) custom-call(bf16[1152,512]{1,0:T(8,128)(2,1)S(1)} %bitcast.145, ...), custom_call_target="tpu_custom_call" | custom-call | tf_op jit(solution)/shard_map/pallas_call | solution.py:1090
  412.1 13.3 %shard_map.249 = (bf16[2,2,144,1152]{3,2,1,0:T(8,128)(2,1)S(1)}, bf16[2,2,144,1152]{3,2,1,0:T(8,128)(2,1)S(1)}, bf16[2,2,144,1152]{3,2,1,0:T(8,128)(2,1)S(1)}, b...) custom-call(bf16[1152,512]{1,0:T(8,128)(2,1)S(1)} %bitcast.144, ...), custom_call_target="tpu_custom_call" | custom-call | tf_op jit(solution)/shard_map/pallas_call | solution.py:1090
  426.2 2.3 fusion.72
  448.3 24.4 %collective-permute-done.3 = bf16[2,2,144,1152]{3,2,1,0:T(8,128)(2,1)S(1)} collective-permute-done((bf16[2,2,144,1152]{3,2,1,0:T(8,128)(2,1)S(1)}, bf16[2,2,144,1152]{3,2,1,0:T(8,128)(2,1)S(1)}, u32[]{:S(2)}, u32[]{:S(2)}) %collective-permute-start.3) | collective-permute-done | bytes 1327136 | tf_op jit(solution)/shard_map/ppermute | solution.py:149
  476.0 25.1 %collective-permute-done.14 = bf16[2,2,144,1152]{3,2,1,0:T(8,128)(2,1)S(1)} collective-permute-done((bf16[2,2,144,1152]{3,2,1,0:T(8,128)(2,1)S(1)}, bf16[2,2,144,1152]{3,2,1,0:T(8,128)(2,1)S(1)}, u32[]{:S(2)}, u32[]{:S(2)}) %collective-permute-start.14) | collective-permute-done | bytes 1327136 | tf_op jit(solution)/shard_map/ppermute | solution.py:149
  504.5 25.1 %collective-permute-done.25 = bf16[2,2,144,1152]{3,2,1,0:T(8,128)(2,1)S(1)} collective-permute-done((bf16[2,2,144,1152]{3,2,1,0:T(8,128)(2,1)S(1)}, bf16[2,2,144,1152]{3,2,1,0:T(8,128)(2,1)S(1)}, u32[]{:S(2)}, u32[]{:S(2)}) %collective-permute-start.25) | collective-permute-done | bytes 1327136 | tf_op jit(solution)/shard_map/ppermute | solution.py:149
  532.9 13.0 %collective-permute-done.4 = bf16[2,144,1152]{2,1,0:T(8,128)(2,1)S(1)} collective-permute-done((bf16[2,144,1152]{2,1,0:T(8,128)(2,1)S(1)}, bf16[2,144,1152]{2,1,0:T(8,128)(2,1)S(1)}, u32[]{:S(2)}, u32[]{:S(2)}) %collective-permute-start.4) | collective-permute-done | bytes 663584 | tf_op jit(solution)/shard_map/ppermute | solution.py:149
  547.5 2.4 collective-permute-start.9
  549.9 10.2 %collective-permute-done.15 = bf16[2,144,1152]{2,1,0:T(8,128)(2,1)S(1)} collective-permute-done((bf16[2,144,1152]{2,1,0:T(8,128)(2,1)S(1)}, bf16[2,144,1152]{2,1,0:T(8,128)(2,1)S(1)}, u32[]{:S(2)}, u32[]{:S(2)}) %collective-permute-start.15) | collective-permute-done | bytes 663584 | tf_op jit(solution)/shard_map/ppermute | solution.py:149
  564.5 8.8 %collective-permute-done.26 = bf16[2,144,1152]{2,1,0:T(8,128)(2,1)S(1)} collective-permute-done((bf16[2,144,1152]{2,1,0:T(8,128)(2,1)S(1)}, bf16[2,144,1152]{2,1,0:T(8,128)(2,1)S(1)}, u32[]{:S(2)}, u32[]{:S(2)}) %collective-permute-start.26) | collective-permute-done | bytes 663584 | tf_op jit(solution)/shard_map/ppermute | solution.py:149
  573.3 2.4 collective-permute-start.20
  578.5 6.3 collective-permute-done.10
  584.9 26.3 %collective-permute-start.33 = (bf16[144,1152]{1,0:T(8,128)(2,1)S(1)}, bf16[144,1152]{1,0:T(8,128)(2,1)S(1)}, u32[]{:S(2)}, u32[]{:S(2)}) collective-permute-start(bf16[144,1152]{1,0:T(8,128)(2,1)S(1)} %get-tuple-element.126), channel_id=1, source_target_pairs={{0,2},{1,3},{2,4},{3,5},{4,6},{5,7},{6,0},{7,1},{8,10},{9,11},{10,... | collective-permute-start | bytes 995336 | tf_op jit(solution)/shard_map/ppermute | solution.py:149
  611.4 22.1 %collective-permute-start.22 = (bf16[144,1152]{1,0:T(8,128)(2,1)S(1)}, bf16[144,1152]{1,0:T(8,128)(2,1)}, u32[]{:S(2)}, u32[]{:S(2)}) collective-permute-start(bf16[144,1152]{1,0:T(8,128)(2,1)S(1)} %get-tuple-element.129), channel_id=1, source_target_pairs={{0,2},{1,3},{2,4},{3,5},{4,6},{5,7},{6,0},{7,1},{8,10},{9,11},{10,... | collective-permute-start | bytes 995336 | tf_op jit(solution)/shard_map/ppermute | solution.py:149
  633.5 6.4 collective-permute-done.32
  642.6 2.5 reshape.257
  645.0 2.1 constant_dynamic-slice_fusion.1
  647.3 2.3 fusion.42
  (266 shorter events, 74.0 us)
Async XLA Ops:
  2.5 68.2 %collective-permute-start = (bf16[144,576]{1,0:T(8,128)(2,1)}, bf16[144,576]{1,0:T(8,128)(2,1)}, u32[]{:S(2)}, u32[]{:S(2)}) collective-permute-start(bf16[144,576]{1,0:T(8,128)(2,1)} %get-tuple-element.138), channel_id=1, source_target_pairs={{0,1},{1,0},{2,3},{3,2},{4,5},{5,4},{6,7},{7,6},{8,9},{9,8},{10,11... | collective-permute-start | bytes 497672 | tf_op jit(solution)/shard_map/ppermute | solution.py:149
  384.0 45.6 %collective-permute-start.1 = (bf16[2,2,144,1152]{3,2,1,0:T(8,128)(2,1)}, bf16[2,2,144,1152]{3,2,1,0:T(8,128)(2,1)}, u32[]{:S(2)}, u32[]{:S(2)}) collective-permute-start(bf16[2,2,144,1152]{3,2,1,0:T(8,128)(2,1)} %get-tuple-element.87), channel_id=1, source_target_pairs={{0,1},{1,0},{2,3},{3,2},{4,5},{5,4},{6,7},{7,6},{8,9},{9,8},{10,11... | collective-permute-start | bytes 3981320 | tf_op jit(solution)/shard_map/ppermute | solution.py:149
  397.5 41.8 %collective-permute-start.2 = (bf16[2,2,144,1152]{3,2,1,0:T(8,128)(2,1)}, bf16[2,2,144,1152]{3,2,1,0:T(8,128)(2,1)S(1)}, u32[]{:S(2)}, u32[]{:S(2)}) collective-permute-start(bf16[2,2,144,1152]{3,2,1,0:T(8,128)(2,1)} %copy-done.11), channel_id=1, source_target_pairs={{0,1},{1,0},{2,3},{3,2},{4,5},{5,4},{6,7},{7,6},{8,9},{9,8},{10,11... | collective-permute-start | bytes 3981320 | tf_op jit(solution)/shard_map/ppermute | solution.py:149
  397.7 33.8 %collective-permute-start.5 = (bf16[2,2,144,1152]{3,2,1,0:T(8,128)(2,1)}, bf16[2,2,144,1152]{3,2,1,0:T(8,128)(2,1)}, u32[]{:S(2)}, u32[]{:S(2)}) collective-permute-start(bf16[2,2,144,1152]{3,2,1,0:T(8,128)(2,1)} %get-tuple-element.91), channel_id=1, source_target_pairs={{0,1},{1,0},{2,3},{3,2},{4,5},{5,4},{6,7},{7,6},{8,9},{9,8},{10,11... | collective-permute-start | bytes 3981320 | tf_op jit(solution)/shard_map/ppermute | solution.py:149
  398.1 42.6 %collective-permute-start.6 = (bf16[2,2,144,1152]{3,2,1,0:T(8,128)(2,1)}, bf16[2,2,144,1152]{3,2,1,0:T(8,128)(2,1)S(1)}, u32[]{:S(2)}, u32[]{:S(2)}) collective-permute-start(bf16[2,2,144,1152]{3,2,1,0:T(8,128)(2,1)} %get-tuple-element.93), channel_id=1, source_target_pairs={{0,1},{1,0},{2,3},{3,2},{4,5},{5,4},{6,7},{7,6},{8,9},{9,8},{10,11... | collective-permute-start | bytes 3981320 | tf_op jit(solution)/shard_map/ppermute | solution.py:149
  411.7 22.0 %collective-permute-start.12 = (bf16[2,2,144,1152]{3,2,1,0:T(8,128)(2,1)S(1)}, bf16[2,2,144,1152]{3,2,1,0:T(8,128)(2,1)S(1)}, u32[]{:S(2)}, u32[]{:S(2)}) collective-permute-start(bf16[2,2,144,1152]{3,2,1,0:T(8,128)(2,1)S(1)} %get-tuple-element.96), channel_id=1, source_target_pairs={{0,1},{1,0},{2,3},{3,2},{4,5},{5,4},{6,7},{7,6},{8,9},{9,8},{10,11... | collective-permute-start | bytes 3981320 | tf_op jit(solution)/shard_map/ppermute | solution.py:149
  429.7 13.0 %collective-permute-start.13 = (bf16[2,2,144,1152]{3,2,1,0:T(8,128)(2,1)S(1)}, bf16[2,2,144,1152]{3,2,1,0:T(8,128)(2,1)S(1)}, u32[]{:S(2)}, u32[]{:S(2)}) collective-permute-start(bf16[2,2,144,1152]{3,2,1,0:T(8,128)(2,1)S(1)} %get-tuple-element.98), channel_id=1, source_target_pairs={{0,1},{1,0},{2,3},{3,2},{4,5},{5,4},{6,7},{7,6},{8,9},{9,8},{10,11... | collective-permute-start | bytes 3981320 | tf_op jit(solution)/shard_map/ppermute | solution.py:149
  435.4 3.3 collective-permute-start.27
  436.8 7.2 %collective-permute-start.17 = (bf16[2,2,144,1152]{3,2,1,0:T(8,128)(2,1)S(1)}, bf16[2,2,144,1152]{3,2,1,0:T(8,128)(2,1)S(1)}, u32[]{:S(2)}, u32[]{:S(2)}) collective-permute-start(bf16[2,2,144,1152]{3,2,1,0:T(8,128)(2,1)S(1)} %get-tuple-element.102), channel_id=1, source_target_pairs={{0,1},{1,0},{2,3},{3,2},{4,5},{5,4},{6,7},{7,6},{8,9},{9,8},{10,11... | collective-permute-start | bytes 3981320 | tf_op jit(solution)/shard_map/ppermute | solution.py:149
  438.7 6.6 %collective-permute-start.24 = (bf16[2,2,144,1152]{3,2,1,0:T(8,128)(2,1)S(1)}, bf16[2,2,144,1152]{3,2,1,0:T(8,128)(2,1)S(1)}, u32[]{:S(2)}, u32[]{:S(2)}) collective-permute-start(bf16[2,2,144,1152]{3,2,1,0:T(8,128)(2,1)S(1)} %get-tuple-element.107), channel_id=1, source_target_pairs={{0,1},{1,0},{2,3},{3,2},{4,5},{5,4},{6,7},{7,6},{8,9},{9,8},{10,11... | collective-permute-start | bytes 3981320 | tf_op jit(solution)/shard_map/ppermute | solution.py:149
  439.3 7.5 %collective-permute-start.28 = (bf16[2,2,144,1152]{3,2,1,0:T(8,128)(2,1)S(1)}, bf16[2,2,144,1152]{3,2,1,0:T(8,128)(2,1)S(1)}, u32[]{:S(2)}, u32[]{:S(2)}) collective-permute-start(bf16[2,2,144,1152]{3,2,1,0:T(8,128)(2,1)S(1)} %get-tuple-element.111), channel_id=1, source_target_pairs={{0,1},{1,0},{2,3},{3,2},{4,5},{5,4},{6,7},{7,6},{8,9},{9,8},{10,11... | collective-permute-start | bytes 3981320 | tf_op jit(solution)/shard_map/ppermute | solution.py:149
  440.7 32.0 %collective-permute-start.3 = (bf16[2,2,144,1152]{3,2,1,0:T(8,128)(2,1)S(1)}, bf16[2,2,144,1152]{3,2,1,0:T(8,128)(2,1)S(1)}, u32[]{:S(2)}, u32[]{:S(2)}) collective-permute-start(bf16[2,2,144,1152]{3,2,1,0:T(8,128)(2,1)S(1)} %add_convert_fusion.5), channel_id=1, source_target_pairs={{0,8},{1,9},{2,10},{3,11},{4,12},{5,13},{6,14},{7,15},{8,0},{9,1},... | collective-permute-start | bytes 3981320 | tf_op jit(solution)/shard_map/ppermute | solution.py:149
  442.7 32.1 %collective-permute-start.7 = (bf16[2,2,144,1152]{3,2,1,0:T(8,128)(2,1)S(1)}, bf16[2,2,144,1152]{3,2,1,0:T(8,128)(2,1)S(1)}, u32[]{:S(2)}, u32[]{:S(2)}) collective-permute-start(bf16[2,2,144,1152]{3,2,1,0:T(8,128)(2,1)S(1)} %add_convert_fusion.4), channel_id=1, source_target_pairs={{0,16},{1,17},{2,18},{3,19},{4,20},{5,21},{6,22},{7,23},{8,24},{9,... | collective-permute-start | bytes 3981320 | tf_op jit(solution)/shard_map/ppermute | solution.py:149
  444.0 57.1 %collective-permute-start.14 = (bf16[2,2,144,1152]{3,2,1,0:T(8,128)(2,1)S(1)}, bf16[2,2,144,1152]{3,2,1,0:T(8,128)(2,1)S(1)}, u32[]{:S(2)}, u32[]{:S(2)}) collective-permute-start(bf16[2,2,144,1152]{3,2,1,0:T(8,128)(2,1)S(1)} %add_convert_fusion.3), channel_id=1, source_target_pairs={{0,8},{1,9},{2,10},{3,11},{4,12},{5,13},{6,14},{7,15},{8,0},{9,1},... | collective-permute-start | bytes 3981320 | tf_op jit(solution)/shard_map/ppermute | solution.py:149
  445.4 57.8 %collective-permute-start.18 = (bf16[2,2,144,1152]{3,2,1,0:T(8,128)(2,1)S(1)}, bf16[2,2,144,1152]{3,2,1,0:T(8,128)(2,1)S(1)}, u32[]{:S(2)}, u32[]{:S(2)}) collective-permute-start(bf16[2,2,144,1152]{3,2,1,0:T(8,128)(2,1)S(1)} %add_convert_fusion.2), channel_id=1, source_target_pairs={{0,16},{1,17},{2,18},{3,19},{4,20},{5,21},{6,22},{7,23},{8,24},{9,... | collective-permute-start | bytes 3981320 | tf_op jit(solution)/shard_map/ppermute | solution.py:149
  446.8 82.7 %collective-permute-start.25 = (bf16[2,2,144,1152]{3,2,1,0:T(8,128)(2,1)S(1)}, bf16[2,2,144,1152]{3,2,1,0:T(8,128)(2,1)S(1)}, u32[]{:S(2)}, u32[]{:S(2)}) collective-permute-start(bf16[2,2,144,1152]{3,2,1,0:T(8,128)(2,1)S(1)} %add_convert_fusion.1), channel_id=1, source_target_pairs={{0,8},{1,9},{2,10},{3,11},{4,12},{5,13},{6,14},{7,15},{8,0},{9,1},... | collective-permute-start | bytes 3981320 | tf_op jit(solution)/shard_map/ppermute | solution.py:149
  472.7 58.9 %collective-permute-start.29 = (bf16[2,2,144,1152]{3,2,1,0:T(8,128)(2,1)S(1)}, bf16[2,2,144,1152]{3,2,1,0:T(8,128)(2,1)S(1)}, u32[]{:S(2)}, u32[]{:S(2)}) collective-permute-start(bf16[2,2,144,1152]{3,2,1,0:T(8,128)(2,1)S(1)} %add_convert_fusion), channel_id=1, source_target_pairs={{0,16},{1,17},{2,18},{3,19},{4,20},{5,21},{6,22},{7,23},{8,24},{9,... | collective-permute-start | bytes 3981320 | tf_op jit(solution)/shard_map/ppermute | solution.py:149
  474.8 71.1 %collective-permute-start.4 = (bf16[2,144,1152]{2,1,0:T(8,128)(2,1)S(1)}, bf16[2,144,1152]{2,1,0:T(8,128)(2,1)S(1)}, u32[]{:S(2)}, u32[]{:S(2)}) collective-permute-start(bf16[2,144,1152]{2,1,0:T(8,128)(2,1)S(1)} %fusion.19), channel_id=1, source_target_pairs={{0,16},{1,17},{2,18},{3,19},{4,20},{5,21},{6,22},{7,23},{8,24},{9,... | collective-permute-start | bytes 1990664 | tf_op jit(solution)/shard_map/ppermute | solution.py:149
  501.2 45.8 %collective-permute-start.8 = (bf16[2,144,1152]{2,1,0:T(8,128)(2,1)S(1)}, bf16[2,144,1152]{2,1,0:T(8,128)(2,1)S(1)}, u32[]{:S(2)}, u32[]{:S(2)}) collective-permute-start(bf16[2,144,1152]{2,1,0:T(8,128)(2,1)S(1)} %fusion.20), channel_id=1, source_target_pairs={{0,8},{1,9},{2,10},{3,11},{4,12},{5,13},{6,14},{7,15},{8,0},{9,1},... | collective-permute-start | bytes 1990664 | tf_op jit(solution)/shard_map/ppermute | solution.py:149
  503.2 56.9 %collective-permute-start.15 = (bf16[2,144,1152]{2,1,0:T(8,128)(2,1)S(1)}, bf16[2,144,1152]{2,1,0:T(8,128)(2,1)S(1)}, u32[]{:S(2)}, u32[]{:S(2)}) collective-permute-start(bf16[2,144,1152]{2,1,0:T(8,128)(2,1)S(1)} %fusion.21), channel_id=1, source_target_pairs={{0,16},{1,17},{2,18},{3,19},{4,20},{5,21},{6,22},{7,23},{8,24},{9,... | collective-permute-start | bytes 1990664 | tf_op jit(solution)/shard_map/ppermute | solution.py:149
  529.6 32.0 %collective-permute-start.19 = (bf16[2,144,1152]{2,1,0:T(8,128)(2,1)S(1)}, bf16[2,144,1152]{2,1,0:T(8,128)(2,1)S(1)}, u32[]{:S(2)}, u32[]{:S(2)}) collective-permute-start(bf16[2,144,1152]{2,1,0:T(8,128)(2,1)S(1)} %fusion.22), channel_id=1, source_target_pairs={{0,8},{1,9},{2,10},{3,11},{4,12},{5,13},{6,14},{7,15},{8,0},{9,1},... | collective-permute-start | bytes 1990664 | tf_op jit(solution)/shard_map/ppermute | solution.py:149
  531.6 41.6 %collective-permute-start.26 = (bf16[2,144,1152]{2,1,0:T(8,128)(2,1)S(1)}, bf16[2,144,1152]{2,1,0:T(8,128)(2,1)S(1)}, u32[]{:S(2)}, u32[]{:S(2)}) collective-permute-start(bf16[2,144,1152]{2,1,0:T(8,128)(2,1)S(1)} %fusion.23), channel_id=1, source_target_pairs={{0,16},{1,17},{2,18},{3,19},{4,20},{5,21},{6,22},{7,23},{8,24},{9,... | collective-permute-start | bytes 1990664 | tf_op jit(solution)/shard_map/ppermute | solution.py:149
  545.9 30.1 %collective-permute-start.30 = (bf16[2,144,1152]{2,1,0:T(8,128)(2,1)S(1)}, bf16[2,144,1152]{2,1,0:T(8,128)(2,1)S(1)}, u32[]{:S(2)}, u32[]{:S(2)}) collective-permute-start(bf16[2,144,1152]{2,1,0:T(8,128)(2,1)S(1)} %fusion.24), channel_id=1, source_target_pairs={{0,8},{1,9},{2,10},{3,11},{4,12},{5,13},{6,14},{7,15},{8,0},{9,1},... | collective-permute-start | bytes 1990664 | tf_op jit(solution)/shard_map/ppermute | solution.py:149
  547.5 29.0 %collective-permute-start.9 = (bf16[144,1152]{1,0:T(8,128)(2,1)S(1)}, bf16[144,1152]{1,0:T(8,128)(2,1)S(1)}, u32[]{:S(2)}, u32[]{:S(2)}) collective-permute-start(bf16[144,1152]{1,0:T(8,128)(2,1)S(1)} %get-tuple-element.130), channel_id=1, source_target_pairs={{0,6},{1,7},{2,0},{3,1},{4,2},{5,3},{6,4},{7,5},{8,14},{9,15},{10,... | collective-permute-start | bytes 995336 | tf_op jit(solution)/shard_map/ppermute | solution.py:149
  560.1 24.8 %collective-permute-start.10 = (bf16[144,1152]{1,0:T(8,128)(2,1)S(1)}, bf16[144,1152]{1,0:T(8,128)(2,1)S(1)}, u32[]{:S(2)}, u32[]{:S(2)}) collective-permute-start(bf16[144,1152]{1,0:T(8,128)(2,1)S(1)} %get-tuple-element.131), channel_id=1, source_target_pairs={{0,4},{1,5},{2,6},{3,7},{4,0},{5,1},{6,2},{7,3},{8,12},{9,13},{10,... | collective-permute-start | bytes 995336 | tf_op jit(solution)/shard_map/ppermute | solution.py:149
  561.6 23.3 %collective-permute-start.11 = (bf16[144,1152]{1,0:T(8,128)(2,1)S(1)}, bf16[144,1152]{1,0:T(8,128)(2,1)S(1)}, u32[]{:S(2)}, u32[]{:S(2)}) collective-permute-start(bf16[144,1152]{1,0:T(8,128)(2,1)S(1)} %get-tuple-element.132), channel_id=1, source_target_pairs={{0,2},{1,3},{2,4},{3,5},{4,6},{5,7},{6,0},{7,1},{8,10},{9,11},{10,... | collective-permute-start | bytes 995336 | tf_op jit(solution)/shard_map/ppermute | solution.py:149
  573.3 74.0 %collective-permute-start.20 = (bf16[144,1152]{1,0:T(8,128)(2,1)}, bf16[144,1152]{1,0:T(8,128)(2,1)}, u32[]{:S(2)}, u32[]{:S(2)}) collective-permute-start(bf16[144,1152]{1,0:T(8,128)(2,1)} %get-tuple-element.127), channel_id=1, source_target_pairs={{0,6},{1,7},{2,0},{3,1},{4,2},{5,3},{6,4},{7,5},{8,14},{9,15},{10,... | collective-permute-start | bytes 995336 | tf_op jit(solution)/shard_map/ppermute | solution.py:149
  575.9 71.4 %collective-permute-start.21 = (bf16[144,1152]{1,0:T(8,128)(2,1)}, bf16[144,1152]{1,0:T(8,128)(2,1)}, u32[]{:S(2)}, u32[]{:S(2)}) collective-permute-start(bf16[144,1152]{1,0:T(8,128)(2,1)} %get-tuple-element.128), channel_id=1, source_target_pairs={{0,4},{1,5},{2,6},{3,7},{4,0},{5,1},{6,2},{7,3},{8,12},{9,13},{10,... | collective-permute-start | bytes 995336 | tf_op jit(solution)/shard_map/ppermute | solution.py:149
  576.5 34.9 %collective-permute-start.31 = (bf16[144,1152]{1,0:T(8,128)(2,1)S(1)}, bf16[144,1152]{1,0:T(8,128)(2,1)S(1)}, u32[]{:S(2)}, u32[]{:S(2)}) collective-permute-start(bf16[144,1152]{1,0:T(8,128)(2,1)S(1)} %get-tuple-element.124), channel_id=1, source_target_pairs={{0,6},{1,7},{2,0},{3,1},{4,2},{5,3},{6,4},{7,5},{8,14},{9,15},{10,... | collective-permute-start | bytes 995336 | tf_op jit(solution)/shard_map/ppermute | solution.py:149
  584.9 55.0 %collective-permute-start.32 = (bf16[144,1152]{1,0:T(8,128)(2,1)S(1)}, bf16[144,1152]{1,0:T(8,128)(2,1)S(1)}, u32[]{:S(2)}, u32[]{:S(2)}) collective-permute-start(bf16[144,1152]{1,0:T(8,128)(2,1)S(1)} %get-tuple-element.125), channel_id=1, source_target_pairs={{0,4},{1,5},{2,6},{3,7},{4,0},{5,1},{6,2},{7,3},{8,12},{9,13},{10,... | collective-permute-start | bytes 995336 | tf_op jit(solution)/shard_map/ppermute | solution.py:149
  584.9 55.0 %collective-permute-start.33 = (bf16[144,1152]{1,0:T(8,128)(2,1)S(1)}, bf16[144,1152]{1,0:T(8,128)(2,1)S(1)}, u32[]{:S(2)}, u32[]{:S(2)}) collective-permute-start(bf16[144,1152]{1,0:T(8,128)(2,1)S(1)} %get-tuple-element.126), channel_id=1, source_target_pairs={{0,2},{1,3},{2,4},{3,5},{4,6},{5,7},{6,0},{7,1},{8,10},{9,11},{10,... | collective-permute-start | bytes 995336 | tf_op jit(solution)/shard_map/ppermute | solution.py:149
  611.4 35.9 %collective-permute-start.22 = (bf16[144,1152]{1,0:T(8,128)(2,1)S(1)}, bf16[144,1152]{1,0:T(8,128)(2,1)}, u32[]{:S(2)}, u32[]{:S(2)}) collective-permute-start(bf16[144,1152]{1,0:T(8,128)(2,1)S(1)} %get-tuple-element.129), channel_id=1, source_target_pairs={{0,2},{1,3},{2,4},{3,5},{4,6},{5,7},{6,0},{7,1},{8,10},{9,11},{10,... | collective-permute-start | bytes 995336 | tf_op jit(solution)/shard_map/ppermute | solution.py:149
  (44 other events, 396.4 us)

commit v5 on v4

--- a/solution.py
+++ b/solution.py
@@ -342,40 +342,8 @@
     return jnp.dot(left, right, preferred_element_type=jnp.float32)
 
 
-def local_call(kernel, outs, ins, anys, scratch, megabytes):
-    return pl.pallas_call(
-        kernel,
-        out_shape=outs,
-        in_specs=[pl.BlockSpec(memory_space=pltpu.VMEM)] * len(ins)
-        + [pl.BlockSpec(memory_space=pl.ANY)] * len(anys),
-        out_specs=[
-            pl.BlockSpec(memory_space=pl.ANY if out.dtype == jnp.bfloat16 and out.ndim == 4 else pltpu.VMEM)
-            for out in outs
-        ],
-        scratch_shapes=scratch,
-        compiler_params=pltpu.CompilerParams(vmem_limit_bytes=megabytes * 2**20),
-        cost_estimate=pl.CostEstimate(flops=0, bytes_accessed=0, transcendentals=0),
-    )(*ins, *anys)
-
-
 def shaped(dims, kind=jnp.float32):
     return jax.ShapeDtypeStruct(dims, kind)
-
-
-def load_blocks(whole, room, sems, lanes=None):
-    copies = []
-    for block in range(4):
-        source = whole.at[block]
-        if lanes is not None:
-            source = source.at[:, lanes[0] : lanes[1]]
-        copies.append([pltpu.make_async_copy(source, room.at[block], sems.at[block])])
-        copies[-1][0].start()
-    return copies
-
-
-def wait_all(copies):
-    for copy in copies:
-        copy.wait()
 
 
 def by_rows(count, step, body):
@@ -425,258 +393,6 @@
     lane = lane_index(1, 256)
     offset = head * size - begin
     return begin, (lane >= offset) & (lane < offset + size)
-
-
-def attend_back_kernel(joined, grad, stats, slots, slot_line, blocks, sums, bar, wide):
-    rows, width = grad.shape
-    size = width // HEADS
-    scale = 1.0 / math.sqrt(size)
-    bar[...] = jnp.where(slots[...] == slot_line[...], 0.0, -1e30)
-
-    @pl.loop(0, HEADS)
-    def _(head):
-        begin, inside = head_window(head, size, width)
-        columns = [pl.ds(pl.multiple_of(begin + part * width, 128), 256) for part in range(3)]
-        query = jnp.where(inside, joined[:, columns[0]], 0.0)
-        key = joined[:, columns[1]]
-        value = joined[:, columns[2]]
-        out_grad = jnp.where(inside, grad[:, columns[0]], 0.0)
-        lane = lane_index(rows, 128)
-        stat = jnp.sum(jnp.where(lane == head, stats[...], 0.0), axis=1, keepdims=True)
-        probs = jnp.exp(matmul_nt(query, key) * scale + bar[...] - stat)
-        prob_grad = matmul_nt(out_grad, value)
-        inner = jnp.sum(probs * prob_grad, axis=1, keepdims=True)
-        score_grad = (probs * (prob_grad - inner)).astype(jnp.bfloat16)
-        found = (
-            mm(score_grad, key) * scale,
-            matmul_tn(score_grad, query) * scale,
-            matmul_tn(probs.astype(jnp.bfloat16), out_grad),
-        )
-        for part in range(3):
-            wide[:, columns[part]] = jnp.where(inside, found[part], wide[:, columns[part]])
-
-    span = blocks.shape[2]
-    block_width = 3 * width // 4
-
-    def total(at):
-        sums[...] += jnp.sum(wide[at, :].astype(jnp.bfloat16).astype(jnp.float32), axis=0, keepdims=True)
-
-    sums[...] = jnp.zeros_like(sums)
-    by_rows(rows, 64, total)
-    for block in range(4):
-        begin, offset = window_of(block, block_width, 3 * width, span)
-
-        def cut(at):
-            moved = wide[at, begin : begin + span]
-            if offset:
-                moved = pltpu.roll(moved, span - offset, 1)
-            lane = lane_index(moved.shape[0], span)
-            blocks[block, at, :] = jnp.where(lane < block_width, moved, 0.0).astype(jnp.bfloat16)
-
-        by_rows(rows, 64, cut)
-
-
-def attend_back(joined, grad, stats, slots):
-    rows, total = joined.shape
-    span = -(-total // 4 // 128) * 128 + 128
-    return pl.pallas_call(
-        attend_back_kernel,
-        out_shape=[shaped((4, rows, span), jnp.bfloat16), shaped((1, total))],
-        scratch_shapes=[pltpu.VMEM((rows, rows), jnp.float32), pltpu.VMEM((rows, total), jnp.float32)],
-        compiler_params=pltpu.CompilerParams(vmem_limit_bytes=48 * 2**20),
-        cost_estimate=pl.CostEstimate(flops=0, bytes_accessed=0, transcendentals=0),
-    )(joined, grad, stats, slots.reshape(rows, 1), slots.reshape(1, rows))
-
-
-def narrow_kernel(hidden, middle, out_grad, slots, table, bias, before_all, *refs):
-    whole, mixed, branch_grad, pre_grad, sums, gate_sums, pre_sums, room, total, before, sems, more = refs
-    rows, width = middle.shape
-    blocks = load_blocks(whole, room, sems)
-    copies = [pltpu.make_async_copy(before_all.at[part], before.at[part], more.at[part]) for part in range(4)]
-    for copy in copies:
-        copy.start()
-    for part in range(4):
-        wait_all(blocks[part])
-        term = matmul_nt(hidden[part], room[part])
-        if part == 0:
-            total[...] = term + bias[...]
-        else:
-            total[...] += term
-    sums[...] = jnp.zeros_like(sums)
-    gate_sums[...] = jnp.zeros_like(gate_sums)
-    pre_sums[...] = jnp.zeros_like(pre_sums)
-
-    def finish(at):
-        slot = slots[at, :]
-        gate = slot_rows(slot, table, 5, width)
-        branch = total[at, :]
-        grad = out_grad[at, :].astype(jnp.float32)
-        mixed[at, :] = (middle[at, :] + gate * branch).astype(jnp.bfloat16)
-        add_slots(gate_sums, slot, grad * branch)
-        value = (grad * gate).astype(jnp.bfloat16)
-        branch_grad[at, :] = value
-        sums[...] += jnp.sum(value.astype(jnp.float32), axis=0, keepdims=True)
-
-    by_rows(rows, 64, finish)
-    for part in range(4):
-        copies[part].wait()
-        total[...] = mm(branch_grad[...], room[part])
-
-        def act(at):
-            value = before[part, at, :]
-            square = value * value
-            bend = jnp.tanh(SLOPE * (value + 0.044715 * (square * value)))
-            slope = 0.5 * (1.0 + bend) + 0.5 * value * (1.0 - bend * bend) * (
-                SLOPE * (1.0 + 3.0 * 0.044715 * square)
-            )
-            value = (total[at, :] * slope).astype(jnp.bfloat16)
-            pre_grad[part, at, :] = value
-            pre_sums[part : part + 1, :] += jnp.sum(value.astype(jnp.float32), axis=0, keepdims=True)
-
-        by_rows(rows, 64, act)
-
-
-def narrow(hidden, before, middle, out_grad, slots, table, bias, whole):
-    rows, width = middle.shape
-    return pl.pallas_call(
-        narrow_kernel,
-        out_shape=[
-            shaped((rows, width), jnp.bfloat16),
-            shaped((rows, width), jnp.bfloat16),
-            shaped((4, rows, width), jnp.bfloat16),
-            shaped((1, width)),
-            shaped((8, width)),
-            shaped((8, width)),
-        ],
-        in_specs=[pl.BlockSpec(memory_space=pltpu.VMEM)] * 6 + [pl.BlockSpec(memory_space=pl.ANY)] * 2,
-        scratch_shapes=[
-            pltpu.VMEM((4, width, width), jnp.bfloat16),
-            pltpu.VMEM((rows, width), jnp.float32),
-            pltpu.VMEM((4, rows, width), jnp.float32),
-            pltpu.SemaphoreType.DMA((32,)),
-            pltpu.SemaphoreType.DMA((4,)),
-        ],
-        compiler_params=pltpu.CompilerParams(vmem_limit_bytes=58 * 2**20),
-        cost_estimate=pl.CostEstimate(flops=0, bytes_accessed=0, transcendentals=0),
-    )(hidden, middle, out_grad, slots.reshape(rows, 1), table, bias, before, whole)
-
-
-def middle_kernel(pre_grad, middle, out_grad, branch, slots, table, *refs):
-    up_whole, joined_whole, middle_grad, attended_grad, windows = refs[:5]
-    slot_sums, sums, room, side, total, sems, more = refs[5:]
-    rows, width = middle.shape
-    columns = width // 4
-    blocks = load_blocks(up_whole, room, sems)
-    side_blocks = load_blocks(joined_whole, side, more, lanes=(width - WINDOW, width))
-    for flip in range(4):
-        wait_all(blocks[flip])
-        term = matmul_nt(pre_grad[flip], room[flip])
-        if flip == 0:
-            total[...] = term
-        else:
-            total[...] += term
-    slot_sums[...] = jnp.zeros_like(slot_sums)
-    sums[...] = jnp.zeros_like(sums)
-
-    def finish(at):
-        slot = slots[at, :]
-        grad = total[at, :]
-        hat, scale = centred(middle[at, :])
-        add_slots(slot_sums.at[1], slot, grad)
-        add_slots(slot_sums.at[2], slot, grad * hat)
-        grad = grad * (1.0 + slot_rows(slot, table, 4, width))
-        grad = out_grad[at, :].astype(jnp.float32) + norm_back(hat, scale, grad)
-        middle_grad[at, :] = grad
-        add_slots(slot_sums.at[0], slot, grad * branch[at, :])
-        value = (grad * slot_rows(slot, table, 2, width)).astype(jnp.bfloat16).astype(jnp.float32)
-        total[at, :] = value
-        sums[...] += jnp.sum(value, axis=0, keepdims=True)
-
-    by_rows(rows, 64, finish)
-    for block in range(4):
-        begin, offset = window_of(block, columns, width, WINDOW)
-
-        def cut(at):
-            moved = total[at, begin : begin + WINDOW]
-            if offset != WINDOW - columns:
-                moved = pltpu.roll(moved, (2 * WINDOW - columns - offset) % WINDOW, 1)
-            lane = lane_index(moved.shape[0], WINDOW)
-            moved = jnp.where(lane >= WINDOW - columns, moved, 0.0)
-            windows[block, at, :] = moved.astype(jnp.bfloat16)
-
-        by_rows(rows, 64, cut)
-    for block in side_blocks:
-        wait_all(block)
-    value = matmul_nt(windows[0], side[0])
-    for block in range(1, 4):
-        value = value + matmul_nt(windows[block], side[block])
-    attended_grad[...] = value.astype(jnp.bfloat16)
-
-
-def middle_back(pre_grad, middle, out_grad, branch, slots, table, up_whole, joined_whole):
-    rows, width = middle.shape
-    return pl.pallas_call(
-        middle_kernel,
-        out_shape=[
-            shaped((rows, width)),
-            shaped((rows, width), jnp.bfloat16),
-            shaped((4, rows, WINDOW), jnp.bfloat16),
-            shaped((3, 8, width)),
-            shaped((1, width)),
-        ],
-        in_specs=[pl.BlockSpec(memory_space=pltpu.VMEM)] * 6 + [pl.BlockSpec(memory_space=pl.ANY)] * 2,
-        scratch_shapes=[
-            pltpu.VMEM((4, width, width), jnp.bfloat16),
-            pltpu.VMEM((4, width, WINDOW), jnp.bfloat16),
-            pltpu.VMEM((rows, width), jnp.float32),
-            pltpu.SemaphoreType.DMA((32,)),
-            pltpu.SemaphoreType.DMA((32,)),
-        ],
-        compiler_params=pltpu.CompilerParams(vmem_limit_bytes=58 * 2**20),
-        cost_estimate=pl.CostEstimate(flops=0, bytes_accessed=0, transcendentals=0),
-    )(pre_grad, middle, out_grad, branch, slots.reshape(rows, 1), table, up_whole, joined_whole)
-
-
-def start_kernel(blocks, start, middle_grad, slots, table, *refs):
-    whole, grad_out, slot_sums, room, total, sems = refs
-    rows, width = start.shape
-    span = blocks.shape[2]
-    loads = load_blocks(whole, room, sems, lanes=(0, span))
-    for flip in range(4):
-        wait_all(loads[flip])
-        term = matmul_nt(blocks[flip], room[flip])
-        if flip == 0:
-            total[...] = term
-        else:
-            total[...] += term
-    slot_sums[...] = jnp.zeros_like(slot_sums)
-
-    def finish(at):
-        slot = slots[at, :]
-        grad = total[at, :]
-        hat, scale = centred(start[at, :])
-        add_slots(slot_sums.at[0], slot, grad)
-        add_slots(slot_sums.at[1], slot, grad * hat)
-        grad = grad * (1.0 + slot_rows(slot, table, 1, width))
-        grad_out[at, :] = middle_grad[at, :] + norm_back(hat, scale, grad)
-
-    by_rows(rows, 64, finish)
-
-
-def start_back(blocks, start, middle_grad, slots, table, whole):
-    rows, width = start.shape
-    return local_call(
-        start_kernel,
-        [shaped((rows, width)), shaped((2, 8, width))],
-        [blocks, start, middle_grad, slots.reshape(rows, 1), table],
-        [whole],
-        [
-            pltpu.VMEM((4, width, blocks.shape[2]), jnp.bfloat16),
-            pltpu.VMEM((rows, width), jnp.float32),
-            pltpu.SemaphoreType.DMA((32,)),
-        ],
-        48,
-    )
 
 
 def far_device(plane, depth, core):
@@ -1032,75 +748,6 @@
     )
 
 
-SENT = ((0, (1, 3)), (0, (0, 2)), (1, (2, 3)), (1, (0, 1)))
-
-
-def outer_kernel(plane_major, lefts, spans, *refs):
-    left, right = refs[:lefts], refs[lefts : 2 * lefts]
-    outs, (room, sems) = refs[2 * lefts : 2 * lefts + 8], refs[2 * lefts + 8 :]
-    plane, _, core = place()
-    sides = (1 - core, core)
-    width = room.shape[1]
-    deep = width // 8
-    draining = [[], []]
-    for block in range(4):
-        slot = block % 2
-        wait_all(draining[slot])
-        index = flipped(plane, block) if plane_major else block
-        if lefts == 1:
-            room[slot] = mm(left[0][...], right[0][index]).astype(jnp.bfloat16)
-        else:
-            low, high = spans
-            head = mm(left[0][...], right[0][index])
-            tail = mm(left[1][...], right[1][index])
-            room[slot, :, :high] = head[:, :high].astype(jnp.bfloat16)
-            room[slot, :, high:low] = (head[:, high:low] + tail[:, : low - high]).astype(jnp.bfloat16)
-            room[slot, :, low:] = tail[:, low - high :].astype(jnp.bfloat16)
-        copies = []
-        for kind in range(2):
-            for number, (half, flips) in enumerate(SENT):
-                target = outs[4 * kind + number]
-                for place_in, flip in enumerate(flips):
-                    for step in range(2):
-                        depth = 2 * half + step
-                        if plane_major:
-                            if flip != block:
-                                continue
-                            row = depth * 2 + sides[kind]
-                        else:
-                            if depth != block:
-                                continue
-                            row = flipped(plane, flip) * 2 + sides[kind]
-                        source = room.at[slot, pl.ds(pl.multiple_of(row * deep, 16), deep)]
-                        copies.append(
-                            pltpu.make_async_copy(
-                                source, target.at[place_in, step], sems.at[slot, len(copies)]
-                            )
-                        )
-        for copy in copies:
-            copy.start()
-        draining[slot] = copies
-    wait_all(draining[0])
-    wait_all(draining[1])
-
-
-def outer(plane_major, lefts, rights, spans=None):
-    width = lefts[0].shape[0]
-    deep = width // 8
-    return pl.pallas_call(
-        partial(outer_kernel, plane_major, len(lefts), spans),
-        out_shape=[shaped((2, 2, deep, width), jnp.bfloat16)] * 8,
-        in_specs=[pl.BlockSpec(memory_space=pltpu.VMEM)] * (2 * len(lefts)),
-        out_specs=[pl.BlockSpec(memory_space=pl.ANY)] * 8,
-        scratch_shapes=[
-            pltpu.VMEM((2, width, width), jnp.bfloat16),
-            pltpu.SemaphoreType.DMA((2, 8)),
-        ],
-        compiler_params=pltpu.CompilerParams(vmem_limit_bytes=48 * 2**20),
-        cost_estimate=pl.CostEstimate(flops=0, bytes_accessed=0, transcendentals=0),
-    )(*lefts, *rights)
-
-
 def low_bits(value):
     return value.astype(jnp.bfloat16)
 
@@ -1109,20 +756,591 @@
     return value.astype(jnp.float32)
 
 
-def scatter_pieces(pieces):
-    depth = place()[1]
-    summed = [wide(own) + wide(swap(other, "core")) for other, own in zip(pieces[:4], pieces[4:])]
-    totals = []
-    for half, (first, _, second, _) in enumerate(HALF_ORDERS):
-        sent, kept = summed[2 * half], summed[2 * half + 1]
-        arrived = wide(swap(low_bits(sent), first))
-        across = swap(low_bits(kept[1] + arrived[1]), second)
-        totals.append(kept[0] + arrived[0] + wide(across))
-    total = jnp.concatenate(totals)
-    result = pick(total, depth)
-    for turn in (1, 2, 3):
-        result = result + wide(swap(low_bits(pick(total, (depth - turn) % 4)), turn))
-    return result
+class Scatter:
+    def __init__(self, own, lands, stage, outs, send_sems, recv_sems, stage_sems):
+        self.own, self.lands, self.stage, self.outs = own, lands, stage, outs
+        self.send_sems, self.recv_sems, self.stage_sems = send_sems, recv_sems, stage_sems
+        self.plane, self.depth, self.core = place()
+        self.started = []
+        self.counts = [0] * len(lands)
+        self.queue, self.held, self.turn = [], [], 0
+
+    def partners(self):
+        found = [
+            far_device(flipped(self.plane, 1), self.depth, self.core),
+            far_device(flipped(self.plane, 2), self.depth, self.core),
+            far_device(self.plane, self.depth, 1 - self.core),
+        ]
+        return found + [far_device(self.plane, (self.depth + d) % 4, self.core) for d in (1, 2, 3)]
+
+    def sending(self, weight, source, index, partner, number):
+        return pltpu.make_async_remote_copy(
+            src_ref=source,
+            dst_ref=self.lands[weight].at[index],
+            send_sem=self.send_sems.at[weight, number],
+            recv_sem=self.recv_sems.at[weight, index],
+            device_id=self.partners()[partner],
+            device_id_type=pl.DeviceIdType.MESH,
+        )
+
+    def send(self, weight, source, index, partner):
+        copy = self.sending(weight, source, index, partner, self.counts[weight])
+        self.counts[weight] += 1
+        copy.start()
+        return copy
+
+    def term(self, weight, flip, back, rows_of, line_rows):
+        plane, depth = flipped(self.plane, flip), (self.depth + 4 - back) % 4
+        base = (depth if line_rows else plane) * 2
+        self.own[weight, flip, back] = rows_of(base + self.core)[...]
+        return self.send(weight, rows_of(base + 1 - self.core), flip * 4 + back, 2)
+
+    def open(self, weight):
+        order = (2, 1, 3, 0)
+        near = {back: (1, 2) if back % 2 == 0 else (2, 1) for back in order}
+        for back in order:
+            for flip in (3, near[back][0]):
+                goes = (flip, back, 16 + (4 if flip == 3 else 0) + back, 0 if back % 2 == 0 else 1)
+                self.queue.append((weight, flip * 4 + back, flip, back, goes))
+        for back in order:
+            for flip in (near[back][1], 0):
+                self.queue.append((weight, flip * 4 + back, flip, back, None))
+        for back in order:
+            flip = near[back][1]
+            goes = (flip, back, 24 + back, 1 if back % 2 == 0 else 0)
+            self.queue.append((weight, 20 + back, flip, back, goes))
+            self.queue.append((weight, 16 + back, 0, back, None))
+        for back in order:
+            goes = (0, back, 28 + back, 2 + 4 - back) if back else None
+            self.queue.append((weight, 24 + back, 0, back, goes))
+        for back in (2, 1, 3):
+            self.queue.append((weight, 28 + back, 0, 0, "last" if back == 3 else None))
+
+    def fetch(self, job):
+        weight, index = job[0], job[1]
+        region = self.lands[weight].at[index]
+        pltpu.make_async_remote_copy(
+            src_ref=region,
+            dst_ref=region,
+            send_sem=self.send_sems.at[weight, 0],
+            recv_sem=self.recv_sems.at[weight, index],
+            device_id=self.partners()[2],
+            device_id_type=pl.DeviceIdType.MESH,
+        ).wait_recv()
+        self.staging(weight, index, self.turn).start()
+        self.held.append((job, self.turn))
+        self.turn = (self.turn + 1) % 2
+
+    def staging(self, weight, index, turn):
+        return pltpu.make_async_copy(
+            self.lands[weight].at[index], self.stage.at[turn], self.stage_sems.at[turn]
+        )
+
+    def merge(self):
+        (weight, index, flip, back, goes), turn = self.held.pop(0)
+        self.staging(weight, index, turn).wait()
+        total = wide(self.own[weight, flip, back]) + wide(self.stage[turn])
+        if index >= 28:
+            if index == 30:
+                self.outs[weight][...] = total
+            else:
+                self.outs[weight][...] += wide(self.stage[turn])
+            return
+        self.own[weight, flip, back] = low_bits(total)
+        if goes is not None:
+            self.started.append((weight, goes, self.counts[weight]))
+            self.send(weight, self.own.at[weight, goes[0], goes[1]], goes[2], goes[3])
+
+    def tick(self, count=1):
+        for _ in range(count):
+            if self.held:
+                self.merge()
+            if self.queue:
+                self.fetch(self.queue.pop(0))
+
+    def drain(self):
+        while self.queue or self.held:
+            self.tick()
+        for weight, (flip, back, index, partner), number in self.started:
+            source = self.own.at[weight, flip, back]
+            self.sending(weight, source, index, partner, number).wait_send()
+
+
+def multiply_rows(out, left, right, step=384):
+    @pl.loop(0, left.shape[0] // step)
+    def _(index):
+        at = pl.ds(pl.multiple_of(index * step, step), step)
+        out[at, :] = mm(left[at, :], right[...]).astype(jnp.bfloat16)
+
+
+def deep_rows(room, slot, deep):
+    def rows_of(row):
+        return room.at[slot, pl.ds(pl.multiple_of(row * deep, 16), deep)]
+
+    return rows_of
+
+
+def backward_kernel(
+    hidden_in,
+    before_in,
+    joined_in,
+    joined_whole,
+    up_whole,
+    down_whole,
+    middle,
+    out_grad,
+    branch,
+    normed_t,
+    stats,
+    slots,
+    slot_line,
+    table,
+    bias,
+    down_land,
+    up_land,
+    blocks,
+    mixed,
+    middle_grad,
+    windows,
+    slot_sums,
+    branch_sums,
+    pre_sums,
+    joined_sums,
+    down_out,
+    up_out,
+    own,
+    stage,
+    room,
+    acts,
+    grads,
+    grads_t,
+    attended_grad,
+    send_sems,
+    recv_sems,
+    stage_sems,
+    load_sems,
+    more_sems,
+):
+    rows, width = middle.shape
+    deep = width // 8
+    scatter = Scatter(
+        own, (down_land, up_land), stage, (down_out, up_out), send_sems, recv_sems, stage_sems
+    )
+    greet(scatter.partners())
+    slot_sums[...] = jnp.zeros_like(slot_sums)
+    branch_sums[...] = jnp.zeros_like(branch_sums)
+    pre_sums[...] = jnp.zeros_like(pre_sums)
+    joined_sums[...] = jnp.zeros_like(joined_sums)
+
+    def dense(weights, before, total):
+        plan = [(down_whole, part) for part in range(4)] * 2 + [(up_whole, part) for part in range(4)]
+
+        def load(step):
+            whole, part = plan[step]
+            copy = pltpu.make_async_copy(
+                whole.at[part], weights.at[step % 2], load_sems.at[step % 2]
+            )
+            copy.start()
+            return copy
+
+        loads = {0: load(0)}
+        acting = [
+            pltpu.make_async_copy(hidden_in.at[part], acts.at[part], more_sems.at[part])
+            for part in range(4)
+        ]
+        for copy in acting:
+            copy.start()
+
+        def next_weight(step):
+            if step + 1 < len(plan):
+                loads[step + 1] = load(step + 1)
+            loads[step].wait()
+            return weights.at[step % 2]
+
+        for part in range(4):
+            acting[part].wait()
+            term = matmul_nt(acts[part], next_weight(part)[...])
+            total[...] = term + bias[...] if part == 0 else total[...] + term
+
+        def settle(at):
+            slot = slots[at, :]
+            gate = slot_rows(slot, table, 5, width)
+            value = total[at, :]
+            grad = wide(out_grad[at, :])
+            mixed[at, :] = low_bits(middle[at, :] + gate * value)
+            add_slots(slot_sums.at[3], slot, grad * value)
+            value = low_bits(grad * gate)
+            grads[at, :] = value
+            branch_sums[1:2, :] += jnp.sum(wide(value), axis=0, keepdims=True)
+
+        by_rows(rows, 64, settle)
+        grads_t[...] = grads[...].T
+        waits = [[], []]
+        for number, back in enumerate((2, 1, 3, 0)):
+            slot = number % 2
+            for copy in waits[slot]:
+                copy.wait_send()
+            multiply_rows(room.at[slot], grads_t, acts.at[(scatter.depth + 4 - back) % 4])
+            rows_of = deep_rows(room, slot, deep)
+            waits[slot] = [scatter.term(0, flip, back, rows_of, False) for flip in (3, 1, 2, 0)]
+        scatter.open(0)
+        befores = [
+            pltpu.make_async_copy(before_in.at[part], before.at[part % 2], more_sems.at[part])
+            for part in range(4)
+        ]
+        befores[0].start()
+        for part in range(4):
+            if part < 3:
+                befores[part + 1].start()
+            total[...] = mm(grads[...], next_weight(4 + part)[...])
+            befores[part].wait()
+
+            def act(at):
+                value = before[part % 2, at, :]
+                square = value * value
+                bend = jnp.tanh(SLOPE * (value + 0.044715 * (square * value)))
+                slope = 0.5 * (1.0 + bend) + 0.5 * value * (1.0 - bend * bend) * (
+                    SLOPE * (1.0 + 3.0 * 0.044715 * square)
+                )
+                value = low_bits(total[at, :] * slope)
+                acts[part, at, :] = value
+                pre_sums[part : part + 1, :] += jnp.sum(wide(value), axis=0, keepdims=True)
+
+            by_rows(rows, 64, act)
+            scatter.tick(3)
+        for number, flip in enumerate((3, 1, 2, 0)):
+            slot = number % 2
+            for copy in waits[slot]:
+                copy.wait_send()
+            multiply_rows(room.at[slot], normed_t, acts.at[flipped(scatter.plane, flip)])
+            rows_of = deep_rows(room, slot, deep)
+            waits[slot] = [scatter.term(1, flip, back, rows_of, True) for back in (2, 1, 3, 0)]
+            scatter.tick(3)
+        scatter.open(1)
+        for part in range(4):
+            term = matmul_nt(acts[part], next_weight(8 + part)[...])
+            total[...] = term if part == 0 else total[...] + term
+            scatter.tick(1)
+
+        def turn(at):
+            slot = slots[at, :]
+            grad = total[at, :]
+            hat, scale = centred(middle[at, :])
+            add_slots(slot_sums.at[1], slot, grad)
+            add_slots(slot_sums.at[2], slot, grad * hat)
+            grad = grad * (1.0 + slot_rows(slot, table, 4, width))
+            grad = wide(out_grad[at, :]) + norm_back(hat, scale, grad)
+            middle_grad[at, :] = grad
+            add_slots(slot_sums.at[0], slot, grad * branch[at, :])
+            value = wide(low_bits(grad * slot_rows(slot, table, 2, width)))
+            total[at, :] = value
+            branch_sums[0:1, :] += jnp.sum(value, axis=0, keepdims=True)
+
+        by_rows(rows, 64, turn)
+        scatter.tick(2)
+        for slot in range(2):
+            for copy in waits[slot]:
+                copy.wait_send()
+        columns = width // 4
+        span = pl.ds(width - WINDOW, WINDOW)
+        sides = []
+        for block in range(4):
+            copy = pltpu.make_async_copy(
+                joined_whole.at[block, :, span],
+                weights.at[block // 2, :, pl.ds(block % 2 * WINDOW, WINDOW)],
+                more_sems.at[block],
+            )
+            copy.start()
+            sides.append(copy)
+        for block in range(4):
+            begin, offset = window_of(block, columns, width, WINDOW)
+
+            def cut(at):
+                moved = total[at, begin : begin + WINDOW]
+                if offset != WINDOW - columns:
+                    moved = pltpu.roll(moved, (2 * WINDOW - columns - offset) % WINDOW, 1)
+                lane = lane_index(moved.shape[0], WINDOW)
+                moved = jnp.where(lane >= WINDOW - columns, moved, 0.0)
+                windows[block, at, :] = low_bits(moved)
+
+            by_rows(rows, 64, cut)
+            scatter.tick(1)
+        for block in range(4):
+            sides[block].wait()
+            side = weights[block // 2, :, block % 2 * WINDOW : (block % 2 + 1) * WINDOW]
+            term = matmul_nt(windows[block], side)
+            total[...] = term if block == 0 else total[...] + term
+        attended_grad[...] = low_bits(total[...])
+        scatter.tick(2)
+
+    pl.run_scoped(
+        dense,
+        pltpu.VMEM((2, width, width), jnp.bfloat16),
+        pltpu.VMEM((2, rows, width), jnp.float32),
+        pltpu.VMEM((rows, width), jnp.float32),
+    )
+
+    def heads(joined, found_room, bar, cuts):
+        load = pltpu.make_async_copy(joined_in, joined, load_sems.at[0])
+        load.start()
+        size = width // HEADS
+        scale = 1.0 / math.sqrt(size)
+        bar[...] = jnp.where(slots[...] == slot_line[...], 0.0, -1e30)
+        load.wait()
+        for head_static in range(0, HEADS, 2):
+
+            @pl.loop(head_static, head_static + 2)
+            def _(head):
+                begin, inside = head_window(head, size, width)
+                columns = [pl.ds(pl.multiple_of(begin + part * width, 128), 256) for part in range(3)]
+                query = jnp.where(inside, joined[:, columns[0]], 0.0)
+                key = joined[:, columns[1]]
+                value = joined[:, columns[2]]
+                out_part = jnp.where(inside, attended_grad[:, columns[0]], 0.0)
+                lane = lane_index(rows, 128)
+                stat = jnp.sum(jnp.where(lane == head, stats[...], 0.0), axis=1, keepdims=True)
+                probs = jnp.exp(matmul_nt(query, key) * scale + bar[...] - stat)
+                prob_grad = matmul_nt(out_part, value)
+                inner = jnp.sum(probs * prob_grad, axis=1, keepdims=True)
+                score_grad = low_bits(probs * (prob_grad - inner))
+                found = (
+                    mm(score_grad, key) * scale,
+                    matmul_tn(score_grad, query) * scale,
+                    matmul_tn(low_bits(probs), out_part),
+                )
+                for part in range(3):
+                    found_room[:, columns[part]] = jnp.where(
+                        inside, found[part], found_room[:, columns[part]]
+                    )
+
+            scatter.tick(4)
+
+        span = cuts.shape[2]
+        block_width = 3 * width // 4
+
+        def add_up(at):
+            joined_sums[...] += jnp.sum(wide(low_bits(found_room[at, :])), axis=0, keepdims=True)
+
+        by_rows(rows, 64, add_up)
+        stores = []
+        for block in range(4):
+            begin, offset = window_of(block, block_width, 3 * width, span)
+            if block >= 2:
+                stores[block - 2].wait()
+
+            def cut(at):
+                moved = found_room[at, begin : begin + span]
+                if offset:
+                    moved = pltpu.roll(moved, span - offset, 1)
+                lane = lane_index(moved.shape[0], span)
+                cuts[block % 2, at, :] = low_bits(jnp.where(lane < block_width, moved, 0.0))
+
+            by_rows(rows, 64, cut)
+            stores.append(
+                pltpu.make_async_copy(cuts.at[block % 2], blocks.at[block], more_sems.at[block])
+            )
+            stores[block].start()
+            scatter.tick(1)
+        stores[2].wait()
+        stores[3].wait()
+
+    pl.run_scoped(
+        heads,
+        pltpu.VMEM((rows, 3 * width), jnp.bfloat16),
+        pltpu.VMEM((rows, 3 * width), jnp.float32),
+        pltpu.VMEM((rows, rows), jnp.float32),
+        pltpu.VMEM((2, rows, 1024), jnp.bfloat16),
+    )
+    scatter.drain()
+
+
+def backward(hidden, before, joined, wholes, middle, out_grad, branch, normed_t, stats, slots, table, bias):
+    rows, width = middle.shape
+    deep = width // 8
+    vmem, away = pl.BlockSpec(memory_space=pltpu.VMEM), pl.BlockSpec(memory_space=pl.ANY)
+    land = shaped((32, deep, width), jnp.bfloat16)
+    return pl.pallas_call(
+        backward_kernel,
+        out_shape=[
+            land,
+            land,
+            shaped((4, rows, 1024), jnp.bfloat16),
+            shaped((rows, width), jnp.bfloat16),
+            shaped((rows, width)),
+            shaped((4, rows, WINDOW), jnp.bfloat16),
+            shaped((4, 8, width)),
+            shaped((8, width)),
+            shaped((8, width)),
+            shaped((1, 3 * width)),
+            shaped((deep, width)),
+            shaped((deep, width)),
+        ],
+        in_specs=[away] * 6 + [vmem] * 9,
+        out_specs=[away] * 3 + [vmem] * 9,
+        scratch_shapes=[
+            pltpu.VMEM((2, 4, 4, deep, width), jnp.bfloat16),
+            pltpu.VMEM((2, deep, width), jnp.bfloat16),
+            pltpu.VMEM((2, width, width), jnp.bfloat16),
+            pltpu.VMEM((4, rows, width), jnp.bfloat16),
+            pltpu.VMEM((rows, width), jnp.bfloat16),
+            pltpu.VMEM((width, rows), jnp.bfloat16),
+            pltpu.VMEM((rows, width), jnp.bfloat16),
+            pltpu.SemaphoreType.DMA((2, 32)),
+            pltpu.SemaphoreType.DMA((2, 32)),
+            pltpu.SemaphoreType.DMA((2,)),
+            pltpu.SemaphoreType.DMA((2,)),
+            pltpu.SemaphoreType.DMA((4,)),
+        ],
+        compiler_params=pltpu.CompilerParams(
+            collective_id=5, has_side_effects=True, vmem_limit_bytes=62 * 2**20
+        ),
+        cost_estimate=pl.CostEstimate(
+            flops=2 * 22 * rows * width * width, bytes_accessed=10**8, transcendentals=0
+        ),
+    )(
+        hidden,
+        before,
+        joined,
+        *wholes,
+        middle,
+        out_grad,
+        branch,
+        normed_t,
+        stats,
+        slots.reshape(rows, 1),
+        slots.reshape(1, rows),
+        table,
+        bias,
+    )
+
+
+def ending_kernel(
+    joined_whole,
+    blocks,
+    windows,
+    normed_t,
+    attended_t,
+    start,
+    middle_grad,
+    slots,
+    table,
+    land,
+    grad_out,
+    slot_sums,
+    joined_out,
+    own,
+    stage,
+    room,
+    weights,
+    total,
+    send_sems,
+    recv_sems,
+    stage_sems,
+    load_sems,
+):
+    rows, width = start.shape
+    deep = width // 8
+    span = blocks.shape[2]
+    scatter = Scatter(own, (land,), stage, (joined_out,), send_sems, recv_sems, stage_sems)
+    greet(scatter.partners())
+    low, high = span, width - WINDOW
+    loads = [
+        pltpu.make_async_copy(joined_whole.at[part, :, pl.ds(0, span)], weights.at[part], load_sems.at[part])
+        for part in range(4)
+    ]
+    for load in loads:
+        load.start()
+    waits = [[], []]
+    for number, flip in enumerate((3, 1, 2, 0)):
+        slot = number % 2
+        for copy in waits[slot]:
+            copy.wait_send()
+        at = flipped(scatter.plane, flip)
+
+        @pl.loop(0, 3)
+        def _(index):
+            some = pl.ds(pl.multiple_of(index * (width // 3), width // 3), width // 3)
+            head = mm(normed_t[some, :], blocks[at])
+            tail = mm(attended_t[some, :], windows[at])
+            room[slot, some, :high] = low_bits(head[:, :high])
+            room[slot, some, high:low] = low_bits(head[:, high:low] + tail[:, : low - high])
+            room[slot, some, low:] = low_bits(tail[:, low - high :])
+
+        rows_of = deep_rows(room, slot, deep)
+        waits[slot] = [scatter.term(0, flip, back, rows_of, True) for back in (2, 1, 3, 0)]
+    scatter.open(0)
+    slot_sums[...] = jnp.zeros_like(slot_sums)
+    for part in range(4):
+        loads[part].wait()
+        term = matmul_nt(blocks[part], weights[part])
+        total[...] = term if part == 0 else total[...] + term
+        scatter.tick(3)
+
+    def turn(at):
+        slot = slots[at, :]
+        grad = total[at, :]
+        hat, scale = centred(start[at, :])
+        add_slots(slot_sums.at[0], slot, grad)
+        add_slots(slot_sums.at[1], slot, grad * hat)
+        grad = grad * (1.0 + slot_rows(slot, table, 1, width))
+        grad_out[at, :] = middle_grad[at, :] + norm_back(hat, scale, grad)
+
+    for part in range(4):
+
+        @pl.loop(0, rows // 256)
+        def _(index):
+            begin = part * (rows // 4) + index * 64
+            turn(pl.ds(pl.multiple_of(begin, 64), 64))
+
+        scatter.tick(3)
+    for slot in range(2):
+        for copy in waits[slot]:
+            copy.wait_send()
+    scatter.drain()
+
+
+def ending(joined_whole, blocks, windows, normed_t, attended_t, start, middle_grad, slots, table):
+    rows, width = start.shape
+    deep = width // 8
+    vmem, away = pl.BlockSpec(memory_space=pltpu.VMEM), pl.BlockSpec(memory_space=pl.ANY)
+    return pl.pallas_call(
+        ending_kernel,
+        out_shape=[
+            shaped((32, deep, width), jnp.bfloat16),
+            shaped((rows, width)),
+            shaped((2, 8, width)),
+            shaped((deep, width)),
+        ],
+        in_specs=[away] + [vmem] * 8,
+        out_specs=[away] + [vmem] * 3,
+        scratch_shapes=[
+            pltpu.VMEM((1, 4, 4, deep, width), jnp.bfloat16),
+            pltpu.VMEM((2, deep, width), jnp.bfloat16),
+            pltpu.VMEM((2, width, width), jnp.bfloat16),
+            pltpu.VMEM((4, width, blocks.shape[2]), jnp.bfloat16),
+            pltpu.VMEM((rows, width), jnp.float32),
+            pltpu.SemaphoreType.DMA((1, 32)),
+            pltpu.SemaphoreType.DMA((1, 32)),
+            pltpu.SemaphoreType.DMA((2,)),
+            pltpu.SemaphoreType.DMA((4,)),
+        ],
+        compiler_params=pltpu.CompilerParams(
+            collective_id=6, has_side_effects=True, vmem_limit_bytes=56 * 2**20
+        ),
+        cost_estimate=pl.CostEstimate(
+            flops=2 * 7 * rows * width * width, bytes_accessed=3 * 10**7, transcendentals=0
+        ),
+    )(
+        joined_whole,
+        blocks,
+        windows,
+        normed_t,
+        attended_t,
+        start,
+        middle_grad,
+        slots.reshape(rows, 1),
+        table,
+    )
 
 
 def box_device(
@@ -1197,14 +1415,34 @@
         up_bfull.astype(jnp.float32).reshape(4, 1, -1),
         (jnp.concatenate([attn_weight, proj_weight], axis=1), up_weight, down_shard),
     )
-    joined_whole, up_whole, down_whole = [
-        whole.reshape(4, width, width) for whole in (joined_whole, up_whole, down_whole)
-    ]
-    mixed, grad_branch2, pre_grad, branch2_sums, gate2_sums, pre_sums = narrow(
-        hidden, before, middle, grad_out, segment, table, out_bias_f[None, width:], down_whole
-    )
-    down_total = scatter_pieces(outer(False, [grad_branch2.T], [hidden]))
-    up_weight_grad = scatter_pieces(outer(True, [normed2.T], [pre_grad]))
+    wholes = [whole.reshape(4, width, width) for whole in (joined_whole, up_whole, down_whole)]
+    (
+        _,
+        _,
+        blocks,
+        mixed,
+        middle_grad,
+        windows,
+        slot_sums2,
+        branch_sums,
+        pre_sums,
+        joined_sums,
+        down_total,
+        up_weight_grad,
+    ) = backward(
+        hidden,
+        before,
+        joined,
+        wholes,
+        middle,
+        grad_out,
+        branch1,
+        normed2.T,
+        stats,
+        segment,
+        table,
+        out_bias_f[None, width:],
+    )
     half = down_total.shape[1] // 2
     cut = down_total.reshape(-1, 2, half).transpose(1, 0, 2)
     mine, theirs = pick(cut, core), pick(cut, 1 - core)
@@ -1212,26 +1450,16 @@
     down_weight_grad = jnp.where(
         core == 0, jnp.concatenate([mine, arrived]), jnp.concatenate([arrived, mine])
     ).T
-    middle_grad, attended_grad, windows, slot_sums2, branch1_sums = middle_back(
-        pre_grad, middle, grad_out, branch1, segment, table, up_whole, joined_whole
-    )
-    blocks, joined_sums = attend_back(joined, attended_grad, stats, segment)
-    joined_total = scatter_pieces(
-        outer(
-            True,
-            [normed1.T, attended.T],
-            [blocks, windows],
-            (blocks.shape[2], width - WINDOW),
-        )
-    )
-    tokens_grad, slot_sums1 = start_back(blocks, start, middle_grad, segment, table, joined_whole)
+    _, tokens_grad, slot_sums1, joined_total = ending(
+        wholes[0], blocks, windows, normed1.T, attended.T, start, middle_grad, segment, table
+    )
     modulation_grad = jnp.concatenate(
-        [slot_sums1[0], slot_sums1[1], slot_sums2[0], slot_sums2[1], slot_sums2[2], gate2_sums], axis=1
+        [slot_sums1[0], slot_sums1[1]] + [slot_sums2[part] for part in range(4)], axis=1
     )[:slot_count].astype(jnp.bfloat16)
     joined_sums = joined_sums[0]
     terms = (
         jnp.concatenate([joined_sums[:width], joined_sums[2 * width :]]),
-        jnp.concatenate([branch1_sums[0], branch2_sums[0]]),
+        branch_sums[:2].reshape(-1),
         pre_sums[:4].reshape(-1),
     )
     ada_weight_grad, ada_bias_grad, silu_grad, bias_grads = modulation_back(

time: 660 us -> 602 us (0.912)
  Pallas kernels: 381 us -> 514 us
  waiting for transfers between devices: 123 us -> 0.01 us
  starting transfers between devices: 75.9 us -> 0.62 us
  other arithmetic: 30.2 us -> 38.4 us
    pallas_call x7 -> x2, Pallas kernels: 153 us -> 282 us  [the longest x1 192 us: backward(): pl.pallas_call(backward_kernel, out_shape=[land, land, shaped((4, rows, 1...]
    ppermute x35 -> x2, waiting for transfers between devices: 123 us -> 0.01 us  [swap(): lax.ppermute(values, AXES, [(index, neighbour(index, axis)) for index in...]
    ppermute x35 -> x2, starting transfers between devices: 75.9 us -> 0.62 us  [swap(): lax.ppermute(values, AXES, [(index, neighbour(index, axis)) for index in...]
    add x15 -> x0, other arithmetic: 9.24 us -> none  [the longest x6 4.53 us: scatter_pieces(): wide(own) + wide(swap(other, 'core'))]
    convert_element_type x1, other arithmetic: 1.91 us -> 10.8 us  [box_device(): norm_modulate(start, own_rows(0), own_rows(1)).astype(jnp.bfloat16)]
    transpose x1, other arithmetic: 1.91 us -> 9.94 us  [box_device(): _, tokens_grad, slot_sums1, joined_total = ending(wholes[0], blocks, wind...]
    cos x0 -> x1, other arithmetic: none -> 6.98 us  [position_code(): jnp.cos(line_pos)]
  transfers between devices with their start and end apart: 35 -> 2, of which waited for: 14 -> 0; matrix products, arithmetic and copies ran while one was open for 8% -> 9% of each run, Pallas kernels for 12% -> 7%
where the time goes in v5:
time: 602 us; the launch traced here: 590 us
  Pallas kernels  514 us (85%)
  other arithmetic  38.4 us (6%)
  local copies, waits for them, and re-layouts  32.1 us (5%)
    pallas_call x1, Pallas kernels, backward(): pl.pallas_call(backward_kernel, out_shape=[land, land, shaped((4, rows, 1...  192 us
    pallas_call x1, Pallas kernels, forward(): pl.pallas_call(forward_kernel, out_shape=[whole, whole, whole, shaped((ro...  162 us
    pallas_call x1, Pallas kernels, ending(): pl.pallas_call(ending_kernel, out_shape=[shaped((32, deep, width), jnp.bf...  90.3 us
    pallas_call x4, Pallas kernels, exchange(): pl.pallas_call(partial(trade, one_for_all), out_shape=jax.ShapeDtypeStruc...  70.7 us
  transfers between devices with their start and end apart: 2, of which 0 were waited for; matrix products, arithmetic and copies ran while one was open for 9% of the time, Pallas kernels for 7%

profile of v5, /device:TPU:0, one launch (start us, length us, event | category | flops | bytes accessed | tf_op | source)
XLA Modules:
  0.0 590.4 jit_solution(6331455559478296846)
XLA Ops:
  0.7 1.8 dynamic-slice_bitcast_fusion.1
  2.9 0.7 fusion.12
  3.7 2.8 concatenate.51
  6.5 16.7 %shard_map.238 = bf16[32,16,384]{2,1,0:T(8,128)(2,1)S(1)} custom-call(bf16[16,384]{1,0:T(8,128)(2,1)S(1)} %reshape.204.values), custom_call_target="tpu_custom_call" | custom-call | bytes 3145728 | tf_op jit(solution)/shard_map/pallas_call | solution.py:260
  26.1 7.0 %multiply_cosine_fusion = (f32[512,288]{1,0:T(8,128)}, f32[512,288]{1,0:T(8,128)}, f32[512,288]{1,0:T(8,128)}, f32[512,288]{1,0:T(8,128)}) fusion(f32[512]{0:T(512)S(1)} %get-tuple-element.82, f32[288]{0:T(512)S(1)} %negate_power_fusion, f32[512]{0:T(512)S(1)} %get-tuple-element.83), kind=kLoop, calls=%fused_computation.3 | loop fusion | flops 294912 | bytes 2364544 | tf_op jit(solution)/shard_map/cos | solution.py:22
  33.1 3.2 concatenate.50
  36.3 1.6 fusion.28
  38.0 1.4 copy-done.1
  41.2 24.9 %shard_map.239 = f32[32,4,1728]{2,1,0:T(4,128)S(1)} custom-call(f32[32,4,1728]{2,1,0:T(4,128)S(1)} %reshape.207.values), custom_call_target="tpu_custom_call" | custom-call | bytes 7077888 | tf_op jit(solution)/shard_map/pallas_call | solution.py:260
  66.6 10.8 %add_convert_fusion.normed = bf16[512,1152]{1,0:T(8,128)(2,1)} fusion(f32[512,1152]{1,0:T(8,128)} %copy-done.1, f32[1152]{0:T(1024)S(1)} %get-tuple-element.61, f32[1152]{0:T(1024)S(1)} %get-tuple-element.62, f32[1152]{0:T(1024)S(1)} %get-tuple-element.63, f32[1152]{0:T(1024)S(1)} %get-tuple-element.64, f32[1152]{0:T(1024)S(1)} %get-tuple-element.65, ...), kind=kLoop, calls=%fused_computation | loop fusion | flops 11796480 | bytes 3581952 | tf_op jit(solution)/shard_map/convert_element_type | solution.py:1392
  77.5 9.9 %fusion.37 = bf16[1152,512]{0,1:T(8,128)(2,1)} fusion(f32[1152]{0:T(1024)S(1)} %get-tuple-element.61, f32[1152]{0:T(1024)S(1)} %get-tuple-element.62, f32[1152]{0:T(1024)S(1)} %get-tuple-element.63, f32[1152]{0:T(1024)S(1)} %get-tuple-element.64, f32[1152]{0:T(1024)S(1)} %get-tuple-element.65, pred[512]{0:T(512)(128)(4,1)} %get-tuple-element.89, ...), kind=kLoop, calls=%fused_computation.97 | loop fusion | flops 11796480 | bytes 3581952 | tf_op jit(solution)/shard_map/transpose | solution.py:1454
  89.0 0.7 reshape.225.up_bias
  89.7 0.9 copy.63.slots
  91.3 2.6 copy.67.normed_t
  94.5 0.8 pad_maximum_fusion.joined_shard
  95.4 0.9 maximum_select_fusion.1.down_shard
  96.3 161.5 %shard_map.240 = (bf16[4,4,2,144,1152]{4,3,2,1,0:T(8,128)(2,1)}, bf16[4,4,2,144,1152]{4,3,2,1,0:T(8,128)(2,1)}, bf16[4,4,2,144,1152]{4,3,2,1,0:T(8,128)(2,1)}, b...) custom-call(bf16[512,1152]{1,0:T(8,128)(2,1)} %add_convert_fusion.no, ...), custom_call_target="tpu_custom_call" | custom-call | flops 13589544960 | bytes 100000000 | tf_op jit(solution)/shard_map/pallas_call | solution.py:703
  257.8 2.5 copy.64
  260.3 1.6 copy.66
  261.9 191.9 %shard_map.241 = (bf16[32,144,1152]{2,1,0:T(8,128)(2,1)}, bf16[32,144,1152]{2,1,0:T(8,128)(2,1)}, bf16[4,512,1024]{2,1,0:T(8,128)(2,1)}, bf16[512,1152]{1,0:T(8,...) custom-call(bf16[4,512,1152]{2,1,0:T(8,128)(2,1)} %get-tuple-element, ...), custom_call_target="tpu_custom_call" | custom-call | flops 29896998912 | bytes 100000000 | tf_op jit(solution)/shard_map/pallas_call | solution.py:1162
  453.8 90.3 %shard_map.242 = (bf16[32,144,1152]{2,1,0:T(8,128)(2,1)}, f32[512,1152]{1,0:T(8,128)}, f32[2,8,1152]{2,1,0:T(8,128)}, f32[144,1152]{1,0:T(8,128)}) custom-call(bf16[4,1152,1152]{2,1,0:T(8,128)(2,1)} %bitcast.92, bf16[4,512,1024]{2,1,0:T(8,128)(2,1)} %get-tuple-element.47.blocks, bf16[4,512,512]{2,1,0:T(8,128)(2,1)} %get-tuple-element.48.windows, ...), custom_call_target="tpu_custom_call" | custom-call | flops 9512681472 | bytes 30000000 | tf_op jit(solution)/shard_map/pallas_call | solution.py:1306
  544.1 0.9 convert.25
  545.5 20.0 %shard_map.243 = bf16[32,16,432]{2,1,0:T(8,128)(2,1)S(1)} custom-call(bf16[32,16,432]{2,1,0:T(8,128)(2,1)S(1)} %bitcast.69), custom_call_target="tpu_custom_call" | custom-call | bytes 3538944 | tf_op jit(solution)/shard_map/pallas_call | solution.py:260
  566.8 0.8 slice.143
  568.0 9.1 %shard_map.244 = f32[32,8,128]{2,1,0:T(8,128)S(1)} custom-call(f32[32,8,128]{2,1,0:T(8,128)S(1)} %bitcast.71), custom_call_target="tpu_custom_call" | custom-call | bytes 1048576 | tf_op jit(solution)/shard_map/pallas_call | solution.py:260
  578.5 0.8 slice.146
  579.3 0.8 slice.149
  583.2 2.4 fusion.5
  585.6 0.9 fusion
  586.5 1.0 copy.95
  587.5 1.4 copy.96
  589.1 0.8 copy.97
  (128 shorter events, 15.2 us)
Async XLA Ops:
  0.6 39.9 %copy-start = (bf16[144,1728]{1,0:T(8,128)(2,1)S(1)}, bf16[144,1728]{1,0:T(8,128)(2,1)}, u32[]{:S(2)}) copy-start(bf16[144,1728]{1,0:T(8,128)(2,1)} %param.20) | copy-start | bytes 1492996
  0.7 24.7 %copy-start.18 = (s32[512]{0:T(512)S(1)}, s32[512]{0:T(512)}, u32[]{:S(2)}) copy-start(s32[512]{0:T(512)} %param.18) | copy-start | bytes 6148
  0.7 25.2 %copy-start.25 = (s32[4]{0:T(128)S(1)}, s32[4]{0:T(128)}, u32[]{:S(2)}) copy-start(s32[4]{0:T(128)} %param.19) | copy-start | bytes 52
  0.7 25.3 %copy-start.24 = (s32[512]{0:T(512)S(1)}, s32[512]{0:T(512)}, u32[]{:S(2)}) copy-start(s32[512]{0:T(512)} %param.17) | copy-start | bytes 6148
  2.5 92.9 %collective-permute-start = (bf16[144,576]{1,0:T(8,128)(2,1)}, bf16[144,576]{1,0:T(8,128)(2,1)S(1)}, u32[]{:S(2)}, u32[]{:S(2)}) collective-permute-start(bf16[144,576]{1,0:T(8,128)(2,1)} %get-tuple-element.77), channel_id=1, source_target_pairs={{0,1},{1,0},{2,3},{3,2},{4,5},{5,4},{6,7},{7,6},{8,9},{9,8},{10,11... | collective-permute-start | bytes 497672 | tf_op jit(solution)/shard_map/ppermute | solution.py:149
  37.9 1.4 copy-start.1
  37.9 1.8 copy-start.16
  40.5 25.6 %copy-start.9 = (bf16[128,1152]{1,0:T(8,128)(2,1)}, bf16[128,1152]{1,0:T(8,128)(2,1)S(1)}, u32[]{:S(2)}) copy-start(bf16[128,1152]{1,0:T(8,128)(2,1)S(1)} %reshape.206) | copy-start | bytes 884740
  40.9 25.5 %copy-start.13 = (f32[32,216]{1,0:T(8,128)S(1)}, f32[32,216]{1,0:T(8,128)}, u32[]{:S(2)}) copy-start(f32[32,216]{1,0:T(8,128)} %slice_convert_fusion.1) | copy-start | bytes 82948
  40.9 25.8 %copy-start.17 = (f32[512]{0:T(512)S(1)}, f32[512]{0:T(512)}, u32[]{:S(2)}) copy-start(f32[512]{0:T(512)} %copy-done.16) | copy-start | bytes 6148
  66.2 11.2 %copy-start.2 = (f32[512,1152]{1,0:T(8,128)S(1)}, f32[512,1152]{1,0:T(8,128)}, u32[]{:S(2)}) copy-start(f32[512,1152]{1,0:T(8,128)} %copy-done.1) | copy-start | bytes 7077892
  77.4 10.7 %copy-start.21 = (bf16[16,72]{1,0:T(8,128)(2,1)S(1)}, bf16[16,72]{1,0:T(8,128)(2,1)}, u32[]{:S(2)}) copy-start(bf16[16,72]{1,0:T(8,128)(2,1)} %get-tuple-element.74) | copy-start | bytes 6916
  77.4 10.8 %copy-start.20 = (bf16[16,72]{1,0:T(8,128)(2,1)S(1)}, bf16[16,72]{1,0:T(8,128)(2,1)}, u32[]{:S(2)}) copy-start(bf16[16,72]{1,0:T(8,128)(2,1)} %get-tuple-element.75) | copy-start | bytes 6916
  77.4 11.6 %copy-start.12 = (f32[32,144]{1,0:T(8,128)S(1)}, f32[32,144]{1,0:T(8,128)}, u32[]{:S(2)}) copy-start(f32[32,144]{1,0:T(8,128)} %slice_convert_fusion) | copy-start | bytes 55300
  77.5 12.3 %copy-start.19 = (s32[512]{0:T(512)S(1)}, s32[512]{0:T(512)}, u32[]{:S(2)}) copy-start(s32[512]{0:T(512)} %param.18) | copy-start | bytes 6148
  87.4 7.1 %copy-start.10 = (bf16[144,864]{1,0:T(8,128)(2,1)S(1)}, bf16[144,864]{1,0:T(8,128)(2,1)}, u32[]{:S(2)}) copy-start(bf16[144,864]{1,0:T(8,128)(2,1)} %param.22) | copy-start | bytes 746500
  87.4 7.1 %copy-start.14 = (bf16[144,288]{1,0:T(8,128)(2,1)S(1)}, bf16[144,288]{1,0:T(8,128)(2,1)}, u32[]{:S(2)}) copy-start(bf16[144,288]{1,0:T(8,128)(2,1)} %param.24) | copy-start | bytes 248836
  257.8 2.5 copy-start.5
  453.8 91.2 %copy-start.11 = (f32[4,8,1152]{2,1,0:T(8,128)S(1)}, f32[4,8,1152]{2,1,0:T(8,128)}, u32[]{:S(2)}) copy-start(f32[4,8,1152]{2,1,0:T(8,128)} %get-tuple-element.53) | copy-start | bytes 442372
  545.0 21.7 %copy-start.22 = (f32[8,1152]{1,0:T(8,128)S(1)}, f32[8,1152]{1,0:T(8,128)}, u32[]{:S(2)}) copy-start(f32[8,1152]{1,0:T(8,128)} %get-tuple-element.56) | copy-start | bytes 110596
  545.0 22.6 %copy-start.23 = (f32[1,3456]{1,0:T(1,128)S(1)}, f32[1,3456]{1,0:T(1,128)}, u32[]{:S(2)}) copy-start(f32[1,3456]{1,0:T(1,128)} %get-tuple-element.54) | copy-start | bytes 41476
  545.5 33.0 %copy-start.6 = (f32[144,1152]{1,0:T(8,128)S(1)}, f32[144,1152]{1,0:T(8,128)}, u32[]{:S(2)}) copy-start(f32[144,1152]{1,0:T(8,128)} %get-tuple-element.57) | copy-start | bytes 1990660
  566.2 13.9 %copy-start.8 = (f32[144,1152]{1,0:T(8,128)S(1)}, f32[144,1152]{1,0:T(8,128)}, u32[]{:S(2)}) copy-start(f32[144,1152]{1,0:T(8,128)} %get-tuple-element.59) | copy-start | bytes 1990660
  580.1 1.7 copy-start.15
  581.3 4.3 collective-permute-start.1
  581.5 5.0 copy-start.4
  583.2 4.4 copy-start.3
  587.5 1.5 copy-start.7
